TPU v7x, 512 devices: a whole 4x8x8 slice. The times are simulated.
512 devices in a mesh: ctx: 64 (over z, y_lo, core), kvh: 8 (over y_hi, x).
Axes of the slice: x: 4, y: 8 (y_hi: 2, y_lo: 4; y = y_hi * 4 + y_lo), z: 8, core: 2. Of those that a mesh axis runs over, the one named last changes fastest.
Arguments:
- query: bfloat16 [8192, 4096], P('ctx', 'kvh'), may hold values from -6 to 6, as said below
- key_rows: bfloat16 [8192, 1024], P('ctx', 'kvh'), may hold values from -6 to 6, as said below
- value_rows: bfloat16 [8192, 1024], P('ctx', 'kvh'), may hold values from -6 to 6
- output: bfloat16 [8192, 4096], P('ctx', 'kvh'), may hold values from -6 to 6
- grad_out: bfloat16 [8192, 4096], P('ctx', 'kvh'), may hold values from -6 to 6
- block_order: int32 [128], P('ctx'), may hold values from 0 to 127, as said below
- segment: int32 [8192], P('ctx'), may hold values from 0 to 4, as said below
Outputs:
- grad_query: bfloat16 [8192, 4096], P('ctx', 'kvh')
- grad_key: bfloat16 [8192, 1024], P('ctx', 'kvh')
- grad_value: bfloat16 [8192, 1024], P('ctx', 'kvh')
Inputs may be any that keep to these rules, and one draw needn't show every extreme that they name: `query`: rows are of order one; some rows may be far larger. `key_rows`: rows are of order one; some rows may be far larger. A permutation: stored block r holds positions block_order[r] * 64 to block_order[r] * 64 + 63 in order. `segment`: taken in order of position, document numbers start at 0, never fall, rise by one at each new document and reach the maximum.
All inputs are finite; a program needn't handle non-finite values.
Results may differ from a plain program's by a relative error of at most 0.0075.
Values may be sent and summed in bfloat16 or wider, within the bound.
No kernel may reach another device: no remote copies, remote signals or barrier semaphores. Data moves between devices by JAX's collectives and lax.ppermute only.
A program may use at most 64 MiB of HBM per device.

v0:
```python
import jax
import jax.numpy as jnp
from jax import lax
from jax.sharding import PartitionSpec as P

HEADS = 32
KV_HEADS = 8
HD = 128


def from_behind(block, axis, distance):
    devices = range(lax.axis_size(axis))
    route = [((i - distance) % len(devices), i) for i in devices]
    return lax.ppermute(block, axis, route)


def per_device(query, key_rows, value_rows, output, grad_out, block_order, segment):
    tok_rows = query.shape[0]
    head_size = HD
    groups = HEADS // KV_HEADS
    local_kv = key_rows.shape[1] // head_size
    score_scale = head_size ** (-0.5)
    half_block = tok_rows // 2
    all_orders, seg_all = (
        lax.all_gather(block_order, "ctx", axis=0, tiled=True),
        lax.all_gather(segment, "ctx", axis=0, tiled=True),
    )
    pos_all = (
        all_orders[:, None] * half_block + jnp.arange(half_block, dtype=jnp.int32)[None, :]
    ).reshape(-1)
    ctx_index = lax.axis_index("ctx")
    ctx_count = lax.axis_size("ctx")
    q_pos = lax.dynamic_slice_in_dim(pos_all, ctx_index * tok_rows, tok_rows)
    queries = query.reshape(tok_rows, local_kv, groups, head_size)
    grad_rows = grad_out.reshape(tok_rows, local_kv, groups, head_size)
    saved_rows = output.reshape(tok_rows, local_kv, groups, head_size)

    def allowed_for(row_start, row_count):
        k_pos = lax.dynamic_slice_in_dim(pos_all, row_start, row_count)
        k_seg = lax.dynamic_slice_in_dim(seg_all, row_start, row_count)
        return (k_pos[None, :] <= q_pos[:, None]) & (k_seg[None, :] == segment[:, None])

    key_piece = lax.all_gather(key_rows, "ctx", axis=0, tiled=True)
    row_peak = jnp.full((local_kv, groups, tok_rows), -1e30, jnp.float32)
    row_count = key_piece.shape[0]
    allowed = allowed_for(jnp.int32(0), row_count)
    scores = (
        jnp.einsum(
            "qhgd,khd->hgqk",
            queries,
            key_piece.reshape(row_count, local_kv, head_size),
            preferred_element_type=jnp.float32,
        )
        * score_scale
    )
    masked = jnp.where(allowed, scores, -1e30)
    new_peak = jnp.maximum(row_peak, jnp.max(masked, axis=-1))
    fresh = jnp.sum(jnp.where(allowed, jnp.exp(masked - new_peak[..., None]), 0.0), axis=-1)
    log_total = new_peak + jnp.log(fresh)
    row_delta = jnp.sum(
        grad_rows.astype(jnp.float32) * saved_rows.astype(jnp.float32), axis=-1
    ).transpose(1, 2, 0)

    def update(kv_visit, owner_index, grad_query, grad_kv):
        allowed = allowed_for(owner_index * tok_rows, tok_rows)
        key_block = kv_visit[:, : local_kv * head_size].reshape(tok_rows, local_kv, head_size)
        value_block = kv_visit[:, local_kv * head_size :].reshape(tok_rows, local_kv, head_size)
        scores = (
            jnp.einsum("qhgd,khd->hgqk", queries, key_block, preferred_element_type=jnp.float32)
            * score_scale
        )
        probs_f = jnp.where(allowed, jnp.exp(scores - log_total[..., None]), 0.0)
        dprobs = jnp.einsum(
            "qhgd,khd->hgqk", grad_rows, value_block, preferred_element_type=jnp.float32
        )
        dscores = probs_f * (dprobs - row_delta[..., None])
        probs_b = probs_f.astype(jnp.bfloat16)
        dscores_b = dscores.astype(jnp.bfloat16)
        d_value = jnp.einsum(
            "hgqk,qhgd->khd", probs_b, grad_rows, preferred_element_type=jnp.float32
        )
        d_key = (
            jnp.einsum("hgqk,qhgd->khd", dscores_b, queries, preferred_element_type=jnp.float32)
            * score_scale
        )
        d_query = (
            jnp.einsum("hgqk,khd->qhgd", dscores_b, key_block, preferred_element_type=jnp.float32)
            * score_scale
        )
        both_grads = jnp.concatenate(
            [d_key.reshape(tok_rows, -1), d_value.reshape(tok_rows, -1)], axis=1
        )
        return (grad_query + d_query, grad_kv + both_grads)

    kv_own = jnp.concatenate([key_rows, value_rows], axis=1)
    zero_kv = jnp.zeros(kv_own.shape, jnp.float32)
    zero_query = jnp.zeros(queries.shape, jnp.float32)

    def pass_grads(grad_kv):
        return from_behind(grad_kv, "ctx", 1)

    def cycle_step(step_index, loop_state):
        kv_visit, grad_kv, grad_query = loop_state
        owner_index = (ctx_index - step_index) % ctx_count
        grad_query, grad_kv = update(kv_visit, owner_index, grad_query, grad_kv)
        kv_next = from_behind(kv_visit, "ctx", 1)
        return (kv_next, pass_grads(grad_kv), grad_query)

    kv_visit, grad_kv, grad_query = lax.fori_loop(
        0, ctx_count - 1, cycle_step, (kv_own, zero_kv, zero_query)
    )
    grad_query, grad_kv = update(kv_visit, (ctx_index + 1) % ctx_count, grad_query, grad_kv)
    grad_kv = pass_grads(grad_kv)
    grad_query_out = grad_query.reshape(tok_rows, -1).astype(jnp.bfloat16)
    grad_key_out = grad_kv[:, : local_kv * head_size].astype(jnp.bfloat16)
    grad_value_out = grad_kv[:, local_kv * head_size :].astype(jnp.bfloat16)
    return (grad_query_out, grad_key_out, grad_value_out)


def solution(mesh):
    return jax.shard_map(
        per_device,
        mesh=mesh,
        in_specs=(
            P("ctx", "kvh"),
            P("ctx", "kvh"),
            P("ctx", "kvh"),
            P("ctx", "kvh"),
            P("ctx", "kvh"),
            P("ctx"),
            P("ctx"),
        ),
        out_specs=(P("ctx", "kvh"), P("ctx", "kvh"), P("ctx", "kvh")),
        check_vma=False,
    )
```

profile of v0, /device:TPU:1, one launch (start us, length us, event | category | flops | bytes accessed | tf_op | source)
XLA Modules:
  0.0 985.7 jit_solution(17954519161534449524)
XLA Ops:
  10.7 23.5 %all-reduce = s32[128]{0:T(128)S(1)} all-reduce(s32[128]{0:T(128)S(1)} %dynamic-update-slice), channel_id=1, replica_groups=mesh['ctx'=64,'kvh'=8] {'ctx'}, use_global_device_ids=true, to_apply=%add | all-reduce | flops 128 | bytes 1024
  37.5 79.0 %all-gather = s32[64,1,128]{2,1,0:T(1,128)S(1)} all-gather(s32[1,1,128]{2,1,0:T(1,128)} %bitcast.203), channel_id=1, replica_groups=mesh['ctx'=64,'kvh'=8] {'ctx'}, dimensions={0}, use_global_device_ids=true | all-gather | bytes 33280 | tf_op jit(solution)/shard_map/all_gather | solution.py:26
  121.7 11.5 %all-gather.3.cloned.1.call-done = bf16[8192,128]{1,0:T(8,128)(2,1)} async-done(((bf16[128,128]{1,0:T(8,128)(2,1)}), bf16[8192,128]{1,0:T(8,128)(2,1)}) %all-gather.3.cloned.1.call-update) | async-done | bytes 2097168 | tf_op jit(solution)/shard_map/all_gather | solution.py:43
  141.3 825.2 %while.20 = (s32[]{:T(128)}, bf16[128,256]{1,0:T(8,128)(2,1)S(1)}, f32[128,256]{0,1:T(8,128)S(1)}, f32[128,1,4,128]{3,0,2,1:T(8,128)S(1)}, s32[]{:T(128)}, /*ind...) while((s32[]{:T(128)}, bf16[128,256]{1,0:T(8,128)(2,1)S(1)}, ...), condition=%wide.region_4.5_spmd.clone, body=%wide.region_3.4_spmd.clone.sunk | while | flops 84672528 | bytes 3809718 | solution.py:109
  179.2 4.9 collective-permute-done
  192.4 4.9 collective-permute-done
  205.6 4.9 collective-permute-done
  218.8 4.9 collective-permute-done
  232.0 4.9 collective-permute-done
  245.2 4.9 collective-permute-done
  258.4 4.9 collective-permute-done
  271.6 4.9 collective-permute-done
  284.8 4.9 collective-permute-done
  298.0 4.9 collective-permute-done
  311.2 4.9 collective-permute-done
  324.5 4.9 collective-permute-done
  337.7 4.9 collective-permute-done
  350.9 4.9 collective-permute-done
  364.1 4.9 collective-permute-done
  377.3 4.9 collective-permute-done
  390.5 4.9 collective-permute-done
  403.7 4.9 collective-permute-done
  416.9 4.9 collective-permute-done
  430.1 4.9 collective-permute-done
  443.3 4.9 collective-permute-done
  456.5 4.9 collective-permute-done
  469.7 4.9 collective-permute-done
  483.0 4.9 collective-permute-done
  496.2 4.9 collective-permute-done
  509.4 4.9 collective-permute-done
  522.6 4.9 collective-permute-done
  535.8 4.9 collective-permute-done
  549.0 4.9 collective-permute-done
  562.2 4.9 collective-permute-done
  575.4 4.9 collective-permute-done
  588.6 4.9 collective-permute-done
  601.8 4.9 collective-permute-done
  615.0 4.9 collective-permute-done
  628.2 4.9 collective-permute-done
  641.5 4.9 collective-permute-done
  654.7 4.9 collective-permute-done
  667.9 4.9 collective-permute-done
  681.1 4.9 collective-permute-done
  694.3 4.9 collective-permute-done
  707.5 4.9 collective-permute-done
  720.7 4.9 collective-permute-done
  733.9 4.9 collective-permute-done
  747.1 4.9 collective-permute-done
  760.3 4.9 collective-permute-done
  773.5 4.9 collective-permute-done
  786.7 4.9 collective-permute-done
  800.0 4.9 collective-permute-done
  813.2 4.9 collective-permute-done
  826.4 4.9 collective-permute-done
  839.6 4.9 collective-permute-done
  852.8 4.9 collective-permute-done
  866.0 4.9 collective-permute-done
  879.2 4.9 collective-permute-done
  892.4 4.9 collective-permute-done
  905.6 4.9 collective-permute-done
  918.8 4.9 collective-permute-done
  932.0 4.9 collective-permute-done
  945.2 4.9 collective-permute-done
  970.3 7.0 collective-permute-done.2
  (860 shorter events, 554.4 us)
Async XLA Ops:
  7.2 126.1 %all-gather.3.cloned.1.call-start = ((), (), s32[]{:S(2)}) async-start(), calls=%async_computation | async-start | bytes 2129920 | tf_op jit(solution)/shard_map/all_gather | solution.py:43
  160.8 10.1 %collective-permute-start = (bf16[128,256]{1,0:T(8,128)(2,1)S(1)}, bf16[128,256]{1,0:T(8,128)(2,1)S(1)}, u32[]{:S(2)}, u32[]{:S(2)}) collective-permute-start(bf16[128,256]{1,0:T(8,128)(2,1)S(1)} %copy.91), channel_id=1, source_target_pairs={{504,0},{0,8},{8,16},{16,24},{24,32},{32,40},{40,48},{48,56},{56,6... | collective-permute-start | bytes 196616 | tf_op jit(solution)/shard_map/while/body/eval_jaxpr/ppermute | solution.py:14
  174.0 10.1 %collective-permute-start = (bf16[128,256]{1,0:T(8,128)(2,1)S(1)}, bf16[128,256]{1,0:T(8,128)(2,1)S(1)}, u32[]{:S(2)}, u32[]{:S(2)}) collective-permute-start(bf16[128,256]{1,0:T(8,128)(2,1)S(1)} %copy.91), channel_id=1, source_target_pairs={{504,0},{0,8},{8,16},{16,24},{24,32},{32,40},{40,48},{48,56},{56,6... | collective-permute-start | bytes 196616 | tf_op jit(solution)/shard_map/while/body/eval_jaxpr/ppermute | solution.py:14
  177.0 10.2 %collective-permute-start.1 = (f32[128,256]{0,1:T(8,128)S(1)}, f32[128,256]{0,1:T(8,128)S(1)}, u32[]{:S(2)}, u32[]{:S(2)}) collective-permute-start(f32[128,256]{0,1:T(8,128)S(1)} %maximum_add_fusion.3), channel_id=1, source_target_pairs={{504,0},{0,8},{8,16},{16,24},{24,32},{32,40},{40,48},{48,56},{56,6... | collective-permute-start | bytes 393224 | tf_op jit(solution)/shard_map/while/body/eval_jaxpr/ppermute | solution.py:14
  190.2 10.2 %collective-permute-start.1 = (f32[128,256]{0,1:T(8,128)S(1)}, f32[128,256]{0,1:T(8,128)S(1)}, u32[]{:S(2)}, u32[]{:S(2)}) collective-permute-start(f32[128,256]{0,1:T(8,128)S(1)} %maximum_add_fusion.3), channel_id=1, source_target_pairs={{504,0},{0,8},{8,16},{16,24},{24,32},{32,40},{40,48},{48,56},{56,6... | collective-permute-start | bytes 393224 | tf_op jit(solution)/shard_map/while/body/eval_jaxpr/ppermute | solution.py:14
  203.4 10.2 %collective-permute-start.1 = (f32[128,256]{0,1:T(8,128)S(1)}, f32[128,256]{0,1:T(8,128)S(1)}, u32[]{:S(2)}, u32[]{:S(2)}) collective-permute-start(f32[128,256]{0,1:T(8,128)S(1)} %maximum_add_fusion.3), channel_id=1, source_target_pairs={{504,0},{0,8},{8,16},{16,24},{24,32},{32,40},{40,48},{48,56},{56,6... | collective-permute-start | bytes 393224 | tf_op jit(solution)/shard_map/while/body/eval_jaxpr/ppermute | solution.py:14
  216.6 10.2 %collective-permute-start.1 = (f32[128,256]{0,1:T(8,128)S(1)}, f32[128,256]{0,1:T(8,128)S(1)}, u32[]{:S(2)}, u32[]{:S(2)}) collective-permute-start(f32[128,256]{0,1:T(8,128)S(1)} %maximum_add_fusion.3), channel_id=1, source_target_pairs={{504,0},{0,8},{8,16},{16,24},{24,32},{32,40},{40,48},{48,56},{56,6... | collective-permute-start | bytes 393224 | tf_op jit(solution)/shard_map/while/body/eval_jaxpr/ppermute | solution.py:14
  229.8 10.2 %collective-permute-start.1 = (f32[128,256]{0,1:T(8,128)S(1)}, f32[128,256]{0,1:T(8,128)S(1)}, u32[]{:S(2)}, u32[]{:S(2)}) collective-permute-start(f32[128,256]{0,1:T(8,128)S(1)} %maximum_add_fusion.3), channel_id=1, source_target_pairs={{504,0},{0,8},{8,16},{16,24},{24,32},{32,40},{40,48},{48,56},{56,6... | collective-permute-start | bytes 393224 | tf_op jit(solution)/shard_map/while/body/eval_jaxpr/ppermute | solution.py:14
  243.0 10.2 %collective-permute-start.1 = (f32[128,256]{0,1:T(8,128)S(1)}, f32[128,256]{0,1:T(8,128)S(1)}, u32[]{:S(2)}, u32[]{:S(2)}) collective-permute-start(f32[128,256]{0,1:T(8,128)S(1)} %maximum_add_fusion.3), channel_id=1, source_target_pairs={{504,0},{0,8},{8,16},{16,24},{24,32},{32,40},{40,48},{48,56},{56,6... | collective-permute-start | bytes 393224 | tf_op jit(solution)/shard_map/while/body/eval_jaxpr/ppermute | solution.py:14
  256.2 10.2 %collective-permute-start.1 = (f32[128,256]{0,1:T(8,128)S(1)}, f32[128,256]{0,1:T(8,128)S(1)}, u32[]{:S(2)}, u32[]{:S(2)}) collective-permute-start(f32[128,256]{0,1:T(8,128)S(1)} %maximum_add_fusion.3), channel_id=1, source_target_pairs={{504,0},{0,8},{8,16},{16,24},{24,32},{32,40},{40,48},{48,56},{56,6... | collective-permute-start | bytes 393224 | tf_op jit(solution)/shard_map/while/body/eval_jaxpr/ppermute | solution.py:14
  269.4 10.2 %collective-permute-start.1 = (f32[128,256]{0,1:T(8,128)S(1)}, f32[128,256]{0,1:T(8,128)S(1)}, u32[]{:S(2)}, u32[]{:S(2)}) collective-permute-start(f32[128,256]{0,1:T(8,128)S(1)} %maximum_add_fusion.3), channel_id=1, source_target_pairs={{504,0},{0,8},{8,16},{16,24},{24,32},{32,40},{40,48},{48,56},{56,6... | collective-permute-start | bytes 393224 | tf_op jit(solution)/shard_map/while/body/eval_jaxpr/ppermute | solution.py:14
  282.6 10.2 %collective-permute-start.1 = (f32[128,256]{0,1:T(8,128)S(1)}, f32[128,256]{0,1:T(8,128)S(1)}, u32[]{:S(2)}, u32[]{:S(2)}) collective-permute-start(f32[128,256]{0,1:T(8,128)S(1)} %maximum_add_fusion.3), channel_id=1, source_target_pairs={{504,0},{0,8},{8,16},{16,24},{24,32},{32,40},{40,48},{48,56},{56,6... | collective-permute-start | bytes 393224 | tf_op jit(solution)/shard_map/while/body/eval_jaxpr/ppermute | solution.py:14
  295.9 10.2 %collective-permute-start.1 = (f32[128,256]{0,1:T(8,128)S(1)}, f32[128,256]{0,1:T(8,128)S(1)}, u32[]{:S(2)}, u32[]{:S(2)}) collective-permute-start(f32[128,256]{0,1:T(8,128)S(1)} %maximum_add_fusion.3), channel_id=1, source_target_pairs={{504,0},{0,8},{8,16},{16,24},{24,32},{32,40},{40,48},{48,56},{56,6... | collective-permute-start | bytes 393224 | tf_op jit(solution)/shard_map/while/body/eval_jaxpr/ppermute | solution.py:14
  309.1 10.2 %collective-permute-start.1 = (f32[128,256]{0,1:T(8,128)S(1)}, f32[128,256]{0,1:T(8,128)S(1)}, u32[]{:S(2)}, u32[]{:S(2)}) collective-permute-start(f32[128,256]{0,1:T(8,128)S(1)} %maximum_add_fusion.3), channel_id=1, source_target_pairs={{504,0},{0,8},{8,16},{16,24},{24,32},{32,40},{40,48},{48,56},{56,6... | collective-permute-start | bytes 393224 | tf_op jit(solution)/shard_map/while/body/eval_jaxpr/ppermute | solution.py:14
  322.3 10.2 %collective-permute-start.1 = (f32[128,256]{0,1:T(8,128)S(1)}, f32[128,256]{0,1:T(8,128)S(1)}, u32[]{:S(2)}, u32[]{:S(2)}) collective-permute-start(f32[128,256]{0,1:T(8,128)S(1)} %maximum_add_fusion.3), channel_id=1, source_target_pairs={{504,0},{0,8},{8,16},{16,24},{24,32},{32,40},{40,48},{48,56},{56,6... | collective-permute-start | bytes 393224 | tf_op jit(solution)/shard_map/while/body/eval_jaxpr/ppermute | solution.py:14
  335.5 10.2 %collective-permute-start.1 = (f32[128,256]{0,1:T(8,128)S(1)}, f32[128,256]{0,1:T(8,128)S(1)}, u32[]{:S(2)}, u32[]{:S(2)}) collective-permute-start(f32[128,256]{0,1:T(8,128)S(1)} %maximum_add_fusion.3), channel_id=1, source_target_pairs={{504,0},{0,8},{8,16},{16,24},{24,32},{32,40},{40,48},{48,56},{56,6... | collective-permute-start | bytes 393224 | tf_op jit(solution)/shard_map/while/body/eval_jaxpr/ppermute | solution.py:14
  348.7 10.2 %collective-permute-start.1 = (f32[128,256]{0,1:T(8,128)S(1)}, f32[128,256]{0,1:T(8,128)S(1)}, u32[]{:S(2)}, u32[]{:S(2)}) collective-permute-start(f32[128,256]{0,1:T(8,128)S(1)} %maximum_add_fusion.3), channel_id=1, source_target_pairs={{504,0},{0,8},{8,16},{16,24},{24,32},{32,40},{40,48},{48,56},{56,6... | collective-permute-start | bytes 393224 | tf_op jit(solution)/shard_map/while/body/eval_jaxpr/ppermute | solution.py:14
  361.9 10.2 %collective-permute-start.1 = (f32[128,256]{0,1:T(8,128)S(1)}, f32[128,256]{0,1:T(8,128)S(1)}, u32[]{:S(2)}, u32[]{:S(2)}) collective-permute-start(f32[128,256]{0,1:T(8,128)S(1)} %maximum_add_fusion.3), channel_id=1, source_target_pairs={{504,0},{0,8},{8,16},{16,24},{24,32},{32,40},{40,48},{48,56},{56,6... | collective-permute-start | bytes 393224 | tf_op jit(solution)/shard_map/while/body/eval_jaxpr/ppermute | solution.py:14
  375.1 10.2 %collective-permute-start.1 = (f32[128,256]{0,1:T(8,128)S(1)}, f32[128,256]{0,1:T(8,128)S(1)}, u32[]{:S(2)}, u32[]{:S(2)}) collective-permute-start(f32[128,256]{0,1:T(8,128)S(1)} %maximum_add_fusion.3), channel_id=1, source_target_pairs={{504,0},{0,8},{8,16},{16,24},{24,32},{32,40},{40,48},{48,56},{56,6... | collective-permute-start | bytes 393224 | tf_op jit(solution)/shard_map/while/body/eval_jaxpr/ppermute | solution.py:14
  388.3 10.2 %collective-permute-start.1 = (f32[128,256]{0,1:T(8,128)S(1)}, f32[128,256]{0,1:T(8,128)S(1)}, u32[]{:S(2)}, u32[]{:S(2)}) collective-permute-start(f32[128,256]{0,1:T(8,128)S(1)} %maximum_add_fusion.3), channel_id=1, source_target_pairs={{504,0},{0,8},{8,16},{16,24},{24,32},{32,40},{40,48},{48,56},{56,6... | collective-permute-start | bytes 393224 | tf_op jit(solution)/shard_map/while/body/eval_jaxpr/ppermute | solution.py:14
  401.5 10.2 %collective-permute-start.1 = (f32[128,256]{0,1:T(8,128)S(1)}, f32[128,256]{0,1:T(8,128)S(1)}, u32[]{:S(2)}, u32[]{:S(2)}) collective-permute-start(f32[128,256]{0,1:T(8,128)S(1)} %maximum_add_fusion.3), channel_id=1, source_target_pairs={{504,0},{0,8},{8,16},{16,24},{24,32},{32,40},{40,48},{48,56},{56,6... | collective-permute-start | bytes 393224 | tf_op jit(solution)/shard_map/while/body/eval_jaxpr/ppermute | solution.py:14
  414.7 10.2 %collective-permute-start.1 = (f32[128,256]{0,1:T(8,128)S(1)}, f32[128,256]{0,1:T(8,128)S(1)}, u32[]{:S(2)}, u32[]{:S(2)}) collective-permute-start(f32[128,256]{0,1:T(8,128)S(1)} %maximum_add_fusion.3), channel_id=1, source_target_pairs={{504,0},{0,8},{8,16},{16,24},{24,32},{32,40},{40,48},{48,56},{56,6... | collective-permute-start | bytes 393224 | tf_op jit(solution)/shard_map/while/body/eval_jaxpr/ppermute | solution.py:14
  427.9 10.2 %collective-permute-start.1 = (f32[128,256]{0,1:T(8,128)S(1)}, f32[128,256]{0,1:T(8,128)S(1)}, u32[]{:S(2)}, u32[]{:S(2)}) collective-permute-start(f32[128,256]{0,1:T(8,128)S(1)} %maximum_add_fusion.3), channel_id=1, source_target_pairs={{504,0},{0,8},{8,16},{16,24},{24,32},{32,40},{40,48},{48,56},{56,6... | collective-permute-start | bytes 393224 | tf_op jit(solution)/shard_map/while/body/eval_jaxpr/ppermute | solution.py:14
  441.1 10.2 %collective-permute-start.1 = (f32[128,256]{0,1:T(8,128)S(1)}, f32[128,256]{0,1:T(8,128)S(1)}, u32[]{:S(2)}, u32[]{:S(2)}) collective-permute-start(f32[128,256]{0,1:T(8,128)S(1)} %maximum_add_fusion.3), channel_id=1, source_target_pairs={{504,0},{0,8},{8,16},{16,24},{24,32},{32,40},{40,48},{48,56},{56,6... | collective-permute-start | bytes 393224 | tf_op jit(solution)/shard_map/while/body/eval_jaxpr/ppermute | solution.py:14
  454.4 10.2 %collective-permute-start.1 = (f32[128,256]{0,1:T(8,128)S(1)}, f32[128,256]{0,1:T(8,128)S(1)}, u32[]{:S(2)}, u32[]{:S(2)}) collective-permute-start(f32[128,256]{0,1:T(8,128)S(1)} %maximum_add_fusion.3), channel_id=1, source_target_pairs={{504,0},{0,8},{8,16},{16,24},{24,32},{32,40},{40,48},{48,56},{56,6... | collective-permute-start | bytes 393224 | tf_op jit(solution)/shard_map/while/body/eval_jaxpr/ppermute | solution.py:14
  467.6 10.2 %collective-permute-start.1 = (f32[128,256]{0,1:T(8,128)S(1)}, f32[128,256]{0,1:T(8,128)S(1)}, u32[]{:S(2)}, u32[]{:S(2)}) collective-permute-start(f32[128,256]{0,1:T(8,128)S(1)} %maximum_add_fusion.3), channel_id=1, source_target_pairs={{504,0},{0,8},{8,16},{16,24},{24,32},{32,40},{40,48},{48,56},{56,6... | collective-permute-start | bytes 393224 | tf_op jit(solution)/shard_map/while/body/eval_jaxpr/ppermute | solution.py:14
  480.8 10.2 %collective-permute-start.1 = (f32[128,256]{0,1:T(8,128)S(1)}, f32[128,256]{0,1:T(8,128)S(1)}, u32[]{:S(2)}, u32[]{:S(2)}) collective-permute-start(f32[128,256]{0,1:T(8,128)S(1)} %maximum_add_fusion.3), channel_id=1, source_target_pairs={{504,0},{0,8},{8,16},{16,24},{24,32},{32,40},{40,48},{48,56},{56,6... | collective-permute-start | bytes 393224 | tf_op jit(solution)/shard_map/while/body/eval_jaxpr/ppermute | solution.py:14
  494.0 10.2 %collective-permute-start.1 = (f32[128,256]{0,1:T(8,128)S(1)}, f32[128,256]{0,1:T(8,128)S(1)}, u32[]{:S(2)}, u32[]{:S(2)}) collective-permute-start(f32[128,256]{0,1:T(8,128)S(1)} %maximum_add_fusion.3), channel_id=1, source_target_pairs={{504,0},{0,8},{8,16},{16,24},{24,32},{32,40},{40,48},{48,56},{56,6... | collective-permute-start | bytes 393224 | tf_op jit(solution)/shard_map/while/body/eval_jaxpr/ppermute | solution.py:14
  507.2 10.2 %collective-permute-start.1 = (f32[128,256]{0,1:T(8,128)S(1)}, f32[128,256]{0,1:T(8,128)S(1)}, u32[]{:S(2)}, u32[]{:S(2)}) collective-permute-start(f32[128,256]{0,1:T(8,128)S(1)} %maximum_add_fusion.3), channel_id=1, source_target_pairs={{504,0},{0,8},{8,16},{16,24},{24,32},{32,40},{40,48},{48,56},{56,6... | collective-permute-start | bytes 393224 | tf_op jit(solution)/shard_map/while/body/eval_jaxpr/ppermute | solution.py:14
  520.4 10.2 %collective-permute-start.1 = (f32[128,256]{0,1:T(8,128)S(1)}, f32[128,256]{0,1:T(8,128)S(1)}, u32[]{:S(2)}, u32[]{:S(2)}) collective-permute-start(f32[128,256]{0,1:T(8,128)S(1)} %maximum_add_fusion.3), channel_id=1, source_target_pairs={{504,0},{0,8},{8,16},{16,24},{24,32},{32,40},{40,48},{48,56},{56,6... | collective-permute-start | bytes 393224 | tf_op jit(solution)/shard_map/while/body/eval_jaxpr/ppermute | solution.py:14
  533.6 10.2 %collective-permute-start.1 = (f32[128,256]{0,1:T(8,128)S(1)}, f32[128,256]{0,1:T(8,128)S(1)}, u32[]{:S(2)}, u32[]{:S(2)}) collective-permute-start(f32[128,256]{0,1:T(8,128)S(1)} %maximum_add_fusion.3), channel_id=1, source_target_pairs={{504,0},{0,8},{8,16},{16,24},{24,32},{32,40},{40,48},{48,56},{56,6... | collective-permute-start | bytes 393224 | tf_op jit(solution)/shard_map/while/body/eval_jaxpr/ppermute | solution.py:14
  546.8 10.2 %collective-permute-start.1 = (f32[128,256]{0,1:T(8,128)S(1)}, f32[128,256]{0,1:T(8,128)S(1)}, u32[]{:S(2)}, u32[]{:S(2)}) collective-permute-start(f32[128,256]{0,1:T(8,128)S(1)} %maximum_add_fusion.3), channel_id=1, source_target_pairs={{504,0},{0,8},{8,16},{16,24},{24,32},{32,40},{40,48},{48,56},{56,6... | collective-permute-start | bytes 393224 | tf_op jit(solution)/shard_map/while/body/eval_jaxpr/ppermute | solution.py:14
  560.0 10.2 %collective-permute-start.1 = (f32[128,256]{0,1:T(8,128)S(1)}, f32[128,256]{0,1:T(8,128)S(1)}, u32[]{:S(2)}, u32[]{:S(2)}) collective-permute-start(f32[128,256]{0,1:T(8,128)S(1)} %maximum_add_fusion.3), channel_id=1, source_target_pairs={{504,0},{0,8},{8,16},{16,24},{24,32},{32,40},{40,48},{48,56},{56,6... | collective-permute-start | bytes 393224 | tf_op jit(solution)/shard_map/while/body/eval_jaxpr/ppermute | solution.py:14
  573.2 10.2 %collective-permute-start.1 = (f32[128,256]{0,1:T(8,128)S(1)}, f32[128,256]{0,1:T(8,128)S(1)}, u32[]{:S(2)}, u32[]{:S(2)}) collective-permute-start(f32[128,256]{0,1:T(8,128)S(1)} %maximum_add_fusion.3), channel_id=1, source_target_pairs={{504,0},{0,8},{8,16},{16,24},{24,32},{32,40},{40,48},{48,56},{56,6... | collective-permute-start | bytes 393224 | tf_op jit(solution)/shard_map/while/body/eval_jaxpr/ppermute | solution.py:14
  586.4 10.2 %collective-permute-start.1 = (f32[128,256]{0,1:T(8,128)S(1)}, f32[128,256]{0,1:T(8,128)S(1)}, u32[]{:S(2)}, u32[]{:S(2)}) collective-permute-start(f32[128,256]{0,1:T(8,128)S(1)} %maximum_add_fusion.3), channel_id=1, source_target_pairs={{504,0},{0,8},{8,16},{16,24},{24,32},{32,40},{40,48},{48,56},{56,6... | collective-permute-start | bytes 393224 | tf_op jit(solution)/shard_map/while/body/eval_jaxpr/ppermute | solution.py:14
  599.6 10.2 %collective-permute-start.1 = (f32[128,256]{0,1:T(8,128)S(1)}, f32[128,256]{0,1:T(8,128)S(1)}, u32[]{:S(2)}, u32[]{:S(2)}) collective-permute-start(f32[128,256]{0,1:T(8,128)S(1)} %maximum_add_fusion.3), channel_id=1, source_target_pairs={{504,0},{0,8},{8,16},{16,24},{24,32},{32,40},{40,48},{48,56},{56,6... | collective-permute-start | bytes 393224 | tf_op jit(solution)/shard_map/while/body/eval_jaxpr/ppermute | solution.py:14
  612.9 10.2 %collective-permute-start.1 = (f32[128,256]{0,1:T(8,128)S(1)}, f32[128,256]{0,1:T(8,128)S(1)}, u32[]{:S(2)}, u32[]{:S(2)}) collective-permute-start(f32[128,256]{0,1:T(8,128)S(1)} %maximum_add_fusion.3), channel_id=1, source_target_pairs={{504,0},{0,8},{8,16},{16,24},{24,32},{32,40},{40,48},{48,56},{56,6... | collective-permute-start | bytes 393224 | tf_op jit(solution)/shard_map/while/body/eval_jaxpr/ppermute | solution.py:14
  626.1 10.2 %collective-permute-start.1 = (f32[128,256]{0,1:T(8,128)S(1)}, f32[128,256]{0,1:T(8,128)S(1)}, u32[]{:S(2)}, u32[]{:S(2)}) collective-permute-start(f32[128,256]{0,1:T(8,128)S(1)} %maximum_add_fusion.3), channel_id=1, source_target_pairs={{504,0},{0,8},{8,16},{16,24},{24,32},{32,40},{40,48},{48,56},{56,6... | collective-permute-start | bytes 393224 | tf_op jit(solution)/shard_map/while/body/eval_jaxpr/ppermute | solution.py:14
  639.3 10.2 %collective-permute-start.1 = (f32[128,256]{0,1:T(8,128)S(1)}, f32[128,256]{0,1:T(8,128)S(1)}, u32[]{:S(2)}, u32[]{:S(2)}) collective-permute-start(f32[128,256]{0,1:T(8,128)S(1)} %maximum_add_fusion.3), channel_id=1, source_target_pairs={{504,0},{0,8},{8,16},{16,24},{24,32},{32,40},{40,48},{48,56},{56,6... | collective-permute-start | bytes 393224 | tf_op jit(solution)/shard_map/while/body/eval_jaxpr/ppermute | solution.py:14
  652.5 10.2 %collective-permute-start.1 = (f32[128,256]{0,1:T(8,128)S(1)}, f32[128,256]{0,1:T(8,128)S(1)}, u32[]{:S(2)}, u32[]{:S(2)}) collective-permute-start(f32[128,256]{0,1:T(8,128)S(1)} %maximum_add_fusion.3), channel_id=1, source_target_pairs={{504,0},{0,8},{8,16},{16,24},{24,32},{32,40},{40,48},{48,56},{56,6... | collective-permute-start | bytes 393224 | tf_op jit(solution)/shard_map/while/body/eval_jaxpr/ppermute | solution.py:14
  665.7 10.2 %collective-permute-start.1 = (f32[128,256]{0,1:T(8,128)S(1)}, f32[128,256]{0,1:T(8,128)S(1)}, u32[]{:S(2)}, u32[]{:S(2)}) collective-permute-start(f32[128,256]{0,1:T(8,128)S(1)} %maximum_add_fusion.3), channel_id=1, source_target_pairs={{504,0},{0,8},{8,16},{16,24},{24,32},{32,40},{40,48},{48,56},{56,6... | collective-permute-start | bytes 393224 | tf_op jit(solution)/shard_map/while/body/eval_jaxpr/ppermute | solution.py:14
  678.9 10.2 %collective-permute-start.1 = (f32[128,256]{0,1:T(8,128)S(1)}, f32[128,256]{0,1:T(8,128)S(1)}, u32[]{:S(2)}, u32[]{:S(2)}) collective-permute-start(f32[128,256]{0,1:T(8,128)S(1)} %maximum_add_fusion.3), channel_id=1, source_target_pairs={{504,0},{0,8},{8,16},{16,24},{24,32},{32,40},{40,48},{48,56},{56,6... | collective-permute-start | bytes 393224 | tf_op jit(solution)/shard_map/while/body/eval_jaxpr/ppermute | solution.py:14
  692.1 10.2 %collective-permute-start.1 = (f32[128,256]{0,1:T(8,128)S(1)}, f32[128,256]{0,1:T(8,128)S(1)}, u32[]{:S(2)}, u32[]{:S(2)}) collective-permute-start(f32[128,256]{0,1:T(8,128)S(1)} %maximum_add_fusion.3), channel_id=1, source_target_pairs={{504,0},{0,8},{8,16},{16,24},{24,32},{32,40},{40,48},{48,56},{56,6... | collective-permute-start | bytes 393224 | tf_op jit(solution)/shard_map/while/body/eval_jaxpr/ppermute | solution.py:14
  705.3 10.2 %collective-permute-start.1 = (f32[128,256]{0,1:T(8,128)S(1)}, f32[128,256]{0,1:T(8,128)S(1)}, u32[]{:S(2)}, u32[]{:S(2)}) collective-permute-start(f32[128,256]{0,1:T(8,128)S(1)} %maximum_add_fusion.3), channel_id=1, source_target_pairs={{504,0},{0,8},{8,16},{16,24},{24,32},{32,40},{40,48},{48,56},{56,6... | collective-permute-start | bytes 393224 | tf_op jit(solution)/shard_map/while/body/eval_jaxpr/ppermute | solution.py:14
  718.5 10.2 %collective-permute-start.1 = (f32[128,256]{0,1:T(8,128)S(1)}, f32[128,256]{0,1:T(8,128)S(1)}, u32[]{:S(2)}, u32[]{:S(2)}) collective-permute-start(f32[128,256]{0,1:T(8,128)S(1)} %maximum_add_fusion.3), channel_id=1, source_target_pairs={{504,0},{0,8},{8,16},{16,24},{24,32},{32,40},{40,48},{48,56},{56,6... | collective-permute-start | bytes 393224 | tf_op jit(solution)/shard_map/while/body/eval_jaxpr/ppermute | solution.py:14
  731.7 10.2 %collective-permute-start.1 = (f32[128,256]{0,1:T(8,128)S(1)}, f32[128,256]{0,1:T(8,128)S(1)}, u32[]{:S(2)}, u32[]{:S(2)}) collective-permute-start(f32[128,256]{0,1:T(8,128)S(1)} %maximum_add_fusion.3), channel_id=1, source_target_pairs={{504,0},{0,8},{8,16},{16,24},{24,32},{32,40},{40,48},{48,56},{56,6... | collective-permute-start | bytes 393224 | tf_op jit(solution)/shard_map/while/body/eval_jaxpr/ppermute | solution.py:14
  744.9 10.2 %collective-permute-start.1 = (f32[128,256]{0,1:T(8,128)S(1)}, f32[128,256]{0,1:T(8,128)S(1)}, u32[]{:S(2)}, u32[]{:S(2)}) collective-permute-start(f32[128,256]{0,1:T(8,128)S(1)} %maximum_add_fusion.3), channel_id=1, source_target_pairs={{504,0},{0,8},{8,16},{16,24},{24,32},{32,40},{40,48},{48,56},{56,6... | collective-permute-start | bytes 393224 | tf_op jit(solution)/shard_map/while/body/eval_jaxpr/ppermute | solution.py:14
  758.1 10.2 %collective-permute-start.1 = (f32[128,256]{0,1:T(8,128)S(1)}, f32[128,256]{0,1:T(8,128)S(1)}, u32[]{:S(2)}, u32[]{:S(2)}) collective-permute-start(f32[128,256]{0,1:T(8,128)S(1)} %maximum_add_fusion.3), channel_id=1, source_target_pairs={{504,0},{0,8},{8,16},{16,24},{24,32},{32,40},{40,48},{48,56},{56,6... | collective-permute-start | bytes 393224 | tf_op jit(solution)/shard_map/while/body/eval_jaxpr/ppermute | solution.py:14
  771.4 10.2 %collective-permute-start.1 = (f32[128,256]{0,1:T(8,128)S(1)}, f32[128,256]{0,1:T(8,128)S(1)}, u32[]{:S(2)}, u32[]{:S(2)}) collective-permute-start(f32[128,256]{0,1:T(8,128)S(1)} %maximum_add_fusion.3), channel_id=1, source_target_pairs={{504,0},{0,8},{8,16},{16,24},{24,32},{32,40},{40,48},{48,56},{56,6... | collective-permute-start | bytes 393224 | tf_op jit(solution)/shard_map/while/body/eval_jaxpr/ppermute | solution.py:14
  784.6 10.2 %collective-permute-start.1 = (f32[128,256]{0,1:T(8,128)S(1)}, f32[128,256]{0,1:T(8,128)S(1)}, u32[]{:S(2)}, u32[]{:S(2)}) collective-permute-start(f32[128,256]{0,1:T(8,128)S(1)} %maximum_add_fusion.3), channel_id=1, source_target_pairs={{504,0},{0,8},{8,16},{16,24},{24,32},{32,40},{40,48},{48,56},{56,6... | collective-permute-start | bytes 393224 | tf_op jit(solution)/shard_map/while/body/eval_jaxpr/ppermute | solution.py:14
  797.8 10.2 %collective-permute-start.1 = (f32[128,256]{0,1:T(8,128)S(1)}, f32[128,256]{0,1:T(8,128)S(1)}, u32[]{:S(2)}, u32[]{:S(2)}) collective-permute-start(f32[128,256]{0,1:T(8,128)S(1)} %maximum_add_fusion.3), channel_id=1, source_target_pairs={{504,0},{0,8},{8,16},{16,24},{24,32},{32,40},{40,48},{48,56},{56,6... | collective-permute-start | bytes 393224 | tf_op jit(solution)/shard_map/while/body/eval_jaxpr/ppermute | solution.py:14
  811.0 10.2 %collective-permute-start.1 = (f32[128,256]{0,1:T(8,128)S(1)}, f32[128,256]{0,1:T(8,128)S(1)}, u32[]{:S(2)}, u32[]{:S(2)}) collective-permute-start(f32[128,256]{0,1:T(8,128)S(1)} %maximum_add_fusion.3), channel_id=1, source_target_pairs={{504,0},{0,8},{8,16},{16,24},{24,32},{32,40},{40,48},{48,56},{56,6... | collective-permute-start | bytes 393224 | tf_op jit(solution)/shard_map/while/body/eval_jaxpr/ppermute | solution.py:14
  824.2 10.2 %collective-permute-start.1 = (f32[128,256]{0,1:T(8,128)S(1)}, f32[128,256]{0,1:T(8,128)S(1)}, u32[]{:S(2)}, u32[]{:S(2)}) collective-permute-start(f32[128,256]{0,1:T(8,128)S(1)} %maximum_add_fusion.3), channel_id=1, source_target_pairs={{504,0},{0,8},{8,16},{16,24},{24,32},{32,40},{40,48},{48,56},{56,6... | collective-permute-start | bytes 393224 | tf_op jit(solution)/shard_map/while/body/eval_jaxpr/ppermute | solution.py:14
  837.4 10.2 %collective-permute-start.1 = (f32[128,256]{0,1:T(8,128)S(1)}, f32[128,256]{0,1:T(8,128)S(1)}, u32[]{:S(2)}, u32[]{:S(2)}) collective-permute-start(f32[128,256]{0,1:T(8,128)S(1)} %maximum_add_fusion.3), channel_id=1, source_target_pairs={{504,0},{0,8},{8,16},{16,24},{24,32},{32,40},{40,48},{48,56},{56,6... | collective-permute-start | bytes 393224 | tf_op jit(solution)/shard_map/while/body/eval_jaxpr/ppermute | solution.py:14
  850.6 10.2 %collective-permute-start.1 = (f32[128,256]{0,1:T(8,128)S(1)}, f32[128,256]{0,1:T(8,128)S(1)}, u32[]{:S(2)}, u32[]{:S(2)}) collective-permute-start(f32[128,256]{0,1:T(8,128)S(1)} %maximum_add_fusion.3), channel_id=1, source_target_pairs={{504,0},{0,8},{8,16},{16,24},{24,32},{32,40},{40,48},{48,56},{56,6... | collective-permute-start | bytes 393224 | tf_op jit(solution)/shard_map/while/body/eval_jaxpr/ppermute | solution.py:14
  863.8 10.2 %collective-permute-start.1 = (f32[128,256]{0,1:T(8,128)S(1)}, f32[128,256]{0,1:T(8,128)S(1)}, u32[]{:S(2)}, u32[]{:S(2)}) collective-permute-start(f32[128,256]{0,1:T(8,128)S(1)} %maximum_add_fusion.3), channel_id=1, source_target_pairs={{504,0},{0,8},{8,16},{16,24},{24,32},{32,40},{40,48},{48,56},{56,6... | collective-permute-start | bytes 393224 | tf_op jit(solution)/shard_map/while/body/eval_jaxpr/ppermute | solution.py:14
  877.0 10.2 %collective-permute-start.1 = (f32[128,256]{0,1:T(8,128)S(1)}, f32[128,256]{0,1:T(8,128)S(1)}, u32[]{:S(2)}, u32[]{:S(2)}) collective-permute-start(f32[128,256]{0,1:T(8,128)S(1)} %maximum_add_fusion.3), channel_id=1, source_target_pairs={{504,0},{0,8},{8,16},{16,24},{24,32},{32,40},{40,48},{48,56},{56,6... | collective-permute-start | bytes 393224 | tf_op jit(solution)/shard_map/while/body/eval_jaxpr/ppermute | solution.py:14
  890.2 10.2 %collective-permute-start.1 = (f32[128,256]{0,1:T(8,128)S(1)}, f32[128,256]{0,1:T(8,128)S(1)}, u32[]{:S(2)}, u32[]{:S(2)}) collective-permute-start(f32[128,256]{0,1:T(8,128)S(1)} %maximum_add_fusion.3), channel_id=1, source_target_pairs={{504,0},{0,8},{8,16},{16,24},{24,32},{32,40},{40,48},{48,56},{56,6... | collective-permute-start | bytes 393224 | tf_op jit(solution)/shard_map/while/body/eval_jaxpr/ppermute | solution.py:14
  903.4 10.2 %collective-permute-start.1 = (f32[128,256]{0,1:T(8,128)S(1)}, f32[128,256]{0,1:T(8,128)S(1)}, u32[]{:S(2)}, u32[]{:S(2)}) collective-permute-start(f32[128,256]{0,1:T(8,128)S(1)} %maximum_add_fusion.3), channel_id=1, source_target_pairs={{504,0},{0,8},{8,16},{16,24},{24,32},{32,40},{40,48},{48,56},{56,6... | collective-permute-start | bytes 393224 | tf_op jit(solution)/shard_map/while/body/eval_jaxpr/ppermute | solution.py:14
  916.6 10.2 %collective-permute-start.1 = (f32[128,256]{0,1:T(8,128)S(1)}, f32[128,256]{0,1:T(8,128)S(1)}, u32[]{:S(2)}, u32[]{:S(2)}) collective-permute-start(f32[128,256]{0,1:T(8,128)S(1)} %maximum_add_fusion.3), channel_id=1, source_target_pairs={{504,0},{0,8},{8,16},{16,24},{24,32},{32,40},{40,48},{48,56},{56,6... | collective-permute-start | bytes 393224 | tf_op jit(solution)/shard_map/while/body/eval_jaxpr/ppermute | solution.py:14
  929.9 10.2 %collective-permute-start.1 = (f32[128,256]{0,1:T(8,128)S(1)}, f32[128,256]{0,1:T(8,128)S(1)}, u32[]{:S(2)}, u32[]{:S(2)}) collective-permute-start(f32[128,256]{0,1:T(8,128)S(1)} %maximum_add_fusion.3), channel_id=1, source_target_pairs={{504,0},{0,8},{8,16},{16,24},{24,32},{32,40},{40,48},{48,56},{56,6... | collective-permute-start | bytes 393224 | tf_op jit(solution)/shard_map/while/body/eval_jaxpr/ppermute | solution.py:14
  943.1 10.2 %collective-permute-start.1 = (f32[128,256]{0,1:T(8,128)S(1)}, f32[128,256]{0,1:T(8,128)S(1)}, u32[]{:S(2)}, u32[]{:S(2)}) collective-permute-start(f32[128,256]{0,1:T(8,128)S(1)} %maximum_add_fusion.3), channel_id=1, source_target_pairs={{504,0},{0,8},{8,16},{16,24},{24,32},{32,40},{40,48},{48,56},{56,6... | collective-permute-start | bytes 393224 | tf_op jit(solution)/shard_map/while/body/eval_jaxpr/ppermute | solution.py:14
  956.3 10.2 %collective-permute-start.1 = (f32[128,256]{0,1:T(8,128)S(1)}, f32[128,256]{0,1:T(8,128)S(1)}, u32[]{:S(2)}, u32[]{:S(2)}) collective-permute-start(f32[128,256]{0,1:T(8,128)S(1)} %maximum_add_fusion.3), channel_id=1, source_target_pairs={{504,0},{0,8},{8,16},{16,24},{24,32},{32,40},{40,48},{48,56},{56,6... | collective-permute-start | bytes 393224 | tf_op jit(solution)/shard_map/while/body/eval_jaxpr/ppermute | solution.py:14
  967.3 10.1 %collective-permute-start.2 = (bf16[128,256]{0,1:T(8,128)(2,1)S(1)}, bf16[128,256]{0,1:T(8,128)(2,1)S(1)}, u32[]{:S(2)}, u32[]{:S(2)}) collective-permute-start(bf16[128,256]{0,1:T(8,128)(2,1)S(1)} %maximum_add_fusion.1), channel_id=1, source_target_pairs={{504,0},{0,8},{8,16},{16,24},{24,32},{32,40},{40,48},{48,56},{56,6... | collective-permute-start | bytes 196616 | tf_op jit(solution)/shard_map/ppermute | solution.py:14
  (65 other events, 637.5 us)
Sparse Core Ops, SparseCore 0:
  10.1 123.0 all-gather.2
where the time goes:
time: 995 us; the launch traced here: 986 us
  waiting for transfers between devices  513 us (52%)
  starting transfers between devices  248 us (25%)
  blocking collectives  103 us (10%)
  matrix products  67 us (7%)
  local copies, waits for them, and re-layouts  17.7 us (2%)
  other arithmetic  17.2 us (2%)
  between operations  14.9 us (1%)
    ppermute x127, waiting for transfers between devices, from_behind(): return lax.ppermute(block, axis, route)  500 us
    ppermute x127, starting transfers between devices, from_behind(): return lax.ppermute(block, axis, route)  248 us
    all_gather x1, blocking collectives, per_device(): lax.all_gather(segment, 'ctx', axis=0, tiled=True)  79 us
    unnamed x1, blocking collectives  23.5 us
  transfers between devices with their start and end apart: 128, of which 127 were waited for; matrix products, arithmetic and copies ran while one was open for 9% of the time, Pallas kernels for 0%

commit v1 on v0

v1 whole, which is shorter than its diff:
```python
import functools

import jax
import jax.numpy as jnp
from jax import lax
from jax.experimental import pallas as pl
from jax.experimental.pallas import tpu as pltpu
from jax.sharding import PartitionSpec as P

HEADS = 32
KV_HEADS = 8
HD = 128
GROUP = HEADS // KV_HEADS
BLK = 64
TOKENS = 8192
TOK = 128
EXTRA = 16
PAY = TOK + EXTRA
YS = 4
ZS = 8
QT = YS * TOK
KT = 2 * TOK
SCALE = HD**-0.5
EXP2 = SCALE * 1.4426950408889634
MASKED = -1e30
FLOOR = -1e25
F32 = jnp.float32
BF16 = jnp.bfloat16
VMEM_LIMIT = 24 * 1024 * 1024

NT = (((1,), (1,)), ((), ()))
TN = (((0,), (0,)), ((), ()))


def dot(a, b, dims=(((1,), (0,)), ((), ()))):
    return lax.dot_general(a, b, dims, preferred_element_type=F32)


def pack_kernel(order_ref, seg_ref, q_ref, k_ref, v_ref, o_ref, g_ref, qp_ref, kvp_ref):
    lane = lax.broadcasted_iota(jnp.int32, (1, TOK), 1)
    block = jnp.where(lane < BLK, order_ref[0], order_ref[1]).astype(F32)
    doc = seg_ref[...].astype(F32)
    qp_ref[0:TOK, 0 : GROUP * HD] = q_ref[...]
    qp_ref[0:TOK, GROUP * HD : 2 * GROUP * HD] = g_ref[...]
    highs, lows = [], []
    for h in range(GROUP):
        cols = slice(h * HD, (h + 1) * HD)
        prod = g_ref[:, cols].astype(F32) * o_ref[:, cols].astype(F32)
        delta = jnp.sum(prod.T, axis=0, keepdims=True)
        high = delta.astype(BF16).astype(F32)
        highs.append(high)
        lows.append(delta - high)
    first = jnp.concatenate(highs + lows, axis=1)
    zero = jnp.zeros_like(doc)
    second = jnp.concatenate([doc, block] + [zero] * 6, axis=1)
    row = lax.broadcasted_iota(jnp.int32, (EXTRA, 8 * TOK), 0)
    extra = jnp.where(row == 0, first, jnp.where(row == 1, second, 0.0))
    qp_ref[TOK:PAY, :] = extra.astype(BF16)
    kv_extra = jnp.concatenate([doc, block], axis=1)
    kv_extra = jnp.broadcast_to(kv_extra, (EXTRA, 2 * HD)).astype(BF16)
    for z in range(ZS):
        kvp_ref[z, 0:TOK, 0:HD] = k_ref[...]
        kvp_ref[z, 0:TOK, HD : 2 * HD] = v_ref[...]
        kvp_ref[z, TOK:PAY, :] = kv_extra


def code_of(doc, block):
    lane = lax.broadcasted_iota(jnp.int32, doc.shape, 1)
    within = jnp.where(lane < BLK, lane, lane - BLK).astype(F32)
    return doc * TOKENS + block * BLK + within


def score_kernel(n_prev, *refs):
    kv_ref, *rest = refs
    q_refs, rest = rest[:YS], rest[YS:]
    if n_prev:
        y_ref, prev_ref, pt_ref, st_ref, fin_ref, qs, code, bias, keep = rest
    else:
        pt_ref, st_ref, qs, code, bias = rest
    step = pl.program_id(0)

    @pl.when(step == 0)
    def _():
        for x, q_ref in enumerate(q_refs):
            toks = slice(x * TOK, (x + 1) * TOK)
            for h in range(GROUP):
                qs[h, toks, :] = q_ref[0:TOK, h * HD : (h + 1) * HD]
            info = q_ref[TOK:PAY, :].astype(F32)
            doc, block = info[1:2, 0:TOK], info[1:2, TOK : 2 * TOK]
            code[0:1, toks] = code_of(doc, block)
            code[1:2, toks] = doc * TOKENS

    for b in range(2):
        info = kv_ref[b, TOK:PAY, :].astype(F32)
        key_code = code_of(info[0:1, 0:TOK], info[0:1, TOK : 2 * TOK])
        key_code = jnp.broadcast_to(key_code, (TOK, TOK)).T
        for x in range(YS):
            toks = slice(x * TOK, (x + 1) * TOK)
            ok = (key_code <= code[0:1, toks]) & (key_code >= code[1:2, toks])
            bias[b * TOK : (b + 1) * TOK, toks] = jnp.where(ok, 0.0, MASKED)
    keys = jnp.concatenate([kv_ref[0, 0:TOK, 0:HD], kv_ref[1, 0:TOK, 0:HD]], axis=0)
    for h in range(GROUP):
        s = dot(keys, qs[h], NT) + bias[...]
        peak = jnp.maximum(jnp.max(s, axis=0, keepdims=True), FLOOR)
        p = jnp.exp2((s - peak) * EXP2)
        st_ref[0, h : h + 1, :] = peak
        st_ref[0, GROUP + h : GROUP + h + 1, :] = jnp.sum(p, axis=0, keepdims=True)
        pt_ref[:, h * QT : (h + 1) * QT] = p.astype(BF16)
    if n_prev:
        keep[pl.ds(step, 1)] = st_ref[...]

        @pl.when(step == pl.num_programs(0) - 1)
        def _():
            tiles = [prev_ref[t] for t in range(n_prev)] + [keep[t] for t in range(n_prev)]
            top = functools.reduce(jnp.maximum, [t[0:GROUP] for t in tiles])
            total = sum(t[GROUP:] * jnp.exp2((t[0:GROUP] - top) * EXP2) for t in tiles)
            for d in range(YS):
                for x in range(YS):
                    to, of = slice(x * TOK, (x + 1) * TOK), slice((x ^ d) * TOK, ((x ^ d) + 1) * TOK)
                    fin_ref[y_ref[0] ^ d, 0:GROUP, to] = top[:, of]
                    fin_ref[y_ref[0] ^ d, GROUP : 2 * GROUP, to] = total[:, of]


def grad_kernel(last, kv_ref, pt_ref, st_ref, all_ref, q0, q1, q2, q3, *rest):
    if last:
        dq_in, dkv_ref, own_ref, send1, send2, send3, qs, gs, delta, dq = rest
    else:
        dkv_ref, dq, qs, gs, delta = rest
    step = pl.program_id(0)

    @pl.when(step == 0)
    def _():
        for x, q_ref in enumerate((q0, q1, q2, q3)):
            toks = slice(x * TOK, (x + 1) * TOK)
            for h in range(GROUP):
                qs[h, toks, :] = q_ref[0:TOK, h * HD : (h + 1) * HD]
                gs[h, toks, :] = q_ref[0:TOK, (GROUP + h) * HD : (GROUP + h + 1) * HD]
            info = q_ref[TOK:PAY, :].astype(F32)
            for h in range(GROUP):
                high = info[0:1, h * TOK : (h + 1) * TOK]
                low = info[0:1, (GROUP + h) * TOK : (GROUP + h + 1) * TOK]
                delta[h : h + 1, toks] = high + low
        dq[...] = dq_in[...] if last else jnp.zeros_like(dq)

    top = functools.reduce(jnp.maximum, [all_ref[y, 0:GROUP] for y in range(YS)])
    total = sum(
        all_ref[y, GROUP : 2 * GROUP] * jnp.exp2((all_ref[y, 0:GROUP] - top) * EXP2)
        for y in range(YS)
    )
    weight = jnp.exp2((st_ref[0, 0:GROUP] - top) * EXP2) / total
    keys = jnp.concatenate([kv_ref[0, 0:TOK, 0:HD], kv_ref[1, 0:TOK, 0:HD]], axis=0)
    values = jnp.concatenate(
        [kv_ref[0, 0:TOK, HD : 2 * HD], kv_ref[1, 0:TOK, HD : 2 * HD]], axis=0
    )
    dk = jnp.zeros((KT, HD), F32)
    dv = jnp.zeros((KT, HD), F32)
    for h in range(GROUP):
        dp = dot(values, gs[h], NT)
        p = pt_ref[:, h * QT : (h + 1) * QT].astype(F32) * weight[h : h + 1]
        ds = (p * (dp - delta[h : h + 1, :])).astype(BF16)
        dv = dv + dot(p.astype(BF16), gs[h])
        dk = dk + dot(ds, qs[h])
        dq[h] += dot(keys, ds, TN)
    dk = dk * SCALE
    for b in range(2):
        rows = slice(b * TOK, (b + 1) * TOK)
        dkv_ref[b, :, 0:HD] = dk[rows].astype(dkv_ref.dtype)
        dkv_ref[b, :, HD : 2 * HD] = dv[rows].astype(dkv_ref.dtype)

    if last:

        @pl.when(step == pl.num_programs(0) - 1)
        def _():
            for x, out in enumerate((own_ref, send1, send2, send3)):
                for h in range(GROUP):
                    part = dq[h, :, x * TOK : (x + 1) * TOK].T * SCALE
                    out[:, h * HD : (h + 1) * HD] = part.astype(out.dtype)


def whole(shape):
    return pl.BlockSpec(shape, lambda *_: (0,) * len(shape))


def shape_of(shape, dtype):
    return jax.ShapeDtypeStruct(shape, dtype)


def params():
    return pltpu.CompilerParams(vmem_limit_bytes=VMEM_LIMIT)


def pack(order, seg, q, k, v, o, g):
    vm = pl.BlockSpec(memory_space=pltpu.VMEM)
    return pl.pallas_call(
        pack_kernel,
        out_shape=(shape_of((PAY, 2 * GROUP * HD), BF16), shape_of((ZS, PAY, 2 * HD), BF16)),
        in_specs=[pl.BlockSpec(memory_space=pltpu.SMEM)] + [vm] * 6,
        out_specs=(vm, vm),
        compiler_params=params(),
        name="pack",
    )(order, seg, q, k, v, o, g)


STEPS = ZS // 2
PAIRS = ZS * TOK * GROUP * QT


def scores(kv, queries, prev=None, y_index=None):
    in_specs = [pl.BlockSpec((2, PAY, 2 * HD), lambda i: (i, 0, 0))]
    in_specs += [whole((PAY, 2 * GROUP * HD))] * YS
    args = [kv, *queries]
    out_shape = [
        shape_of((ZS * TOK, GROUP * QT), BF16),
        shape_of((STEPS, 2 * GROUP, QT), F32),
    ]
    out_specs = [
        pl.BlockSpec((KT, GROUP * QT), lambda i: (i, 0)),
        pl.BlockSpec((1, 2 * GROUP, QT), lambda i: (i, 0, 0)),
    ]
    scratch = [
        pltpu.VMEM((GROUP, QT, HD), BF16),
        pltpu.VMEM((8, QT), F32),
        pltpu.VMEM((KT, QT), F32),
    ]
    if prev is not None:
        in_specs += [pl.BlockSpec(memory_space=pltpu.SMEM), whole(prev.shape)]
        args += [y_index, prev]
        out_shape.append(shape_of((YS, 2 * GROUP, QT), F32))
        out_specs.append(whole((YS, 2 * GROUP, QT)))
        scratch.append(pltpu.VMEM((STEPS, 2 * GROUP, QT), F32))
    return pl.pallas_call(
        functools.partial(score_kernel, 0 if prev is None else STEPS),
        grid=(STEPS,),
        in_specs=in_specs,
        out_specs=out_specs,
        out_shape=out_shape,
        scratch_shapes=scratch,
        compiler_params=params(),
        cost_estimate=pl.CostEstimate(
            flops=4 * PAIRS * HD, bytes_accessed=4 << 20, transcendentals=PAIRS
        ),
        name="scores",
    )(*args)


def grads(kv, probs, stats, all_stats, queries, dq_in=None):
    last = dq_in is not None
    in_specs = [
        pl.BlockSpec((2, PAY, 2 * HD), lambda i: (i, 0, 0)),
        pl.BlockSpec((KT, GROUP * QT), lambda i: (i, 0)),
        pl.BlockSpec((1, 2 * GROUP, QT), lambda i: (i, 0, 0)),
        whole((YS, 2 * GROUP, QT)),
    ] + [whole((PAY, 2 * GROUP * HD))] * YS
    args = [kv, probs, stats, all_stats, *queries]
    dkv_type = F32 if last else BF16
    out_shape = [shape_of((ZS, TOK, 2 * HD), dkv_type)]
    out_specs = [pl.BlockSpec((2, TOK, 2 * HD), lambda i: (i, 0, 0))]
    dq_shape = (GROUP, HD, QT)
    scratch = [
        pltpu.VMEM((GROUP, QT, HD), BF16),
        pltpu.VMEM((GROUP, QT, HD), BF16),
        pltpu.VMEM((8, QT), F32),
    ]
    if last:
        in_specs.append(whole(dq_shape))
        args.append(dq_in)
        out_shape += [shape_of((TOK, GROUP * HD), F32)]
        out_shape += [shape_of((TOK, GROUP * HD), BF16)] * (YS - 1)
        out_specs += [whole((TOK, GROUP * HD))] * YS
        scratch.append(pltpu.VMEM(dq_shape, F32))
    else:
        out_shape.append(shape_of(dq_shape, F32))
        out_specs.append(whole(dq_shape))
    return pl.pallas_call(
        functools.partial(grad_kernel, last),
        grid=(STEPS,),
        in_specs=in_specs,
        out_specs=out_specs,
        out_shape=out_shape,
        scratch_shapes=scratch,
        compiler_params=params(),
        cost_estimate=pl.CostEstimate(
            flops=16 * PAIRS * HD, bytes_accessed=4 << 20, transcendentals=0
        ),
        name="grads",
    )(*args)


def per_device(query, key_rows, value_rows, output, grad_out, block_order, segment):
    n = lax.axis_size("ctx")
    z_groups = [[z * 2 * YS + r for z in range(ZS)] for r in range(2 * YS)]
    y_groups = [
        [z * 2 * YS + y * 2 + c for y in range(YS)] for z in range(ZS) for c in range(2)
    ]

    def swap(x, bits):
        return lax.ppermute(x, "ctx", [(i, i ^ bits) for i in range(n)])

    def exchange(x, groups):
        return lax.all_to_all(x, "ctx", 0, 0, tiled=True, axis_index_groups=groups)

    q_pay, kv_pay = pack(
        block_order, segment.reshape(1, TOK), query, key_rows, value_rows, output, grad_out
    )
    kv_own = exchange(kv_pay, z_groups)
    queries = [q_pay] + [swap(q_pay, 2 * x) for x in range(1, YS)]
    kv_twin = swap(kv_own, 1)
    p_own, st_own = scores(kv_own, queries)
    y_index = (lax.axis_index("ctx") // 2 % YS).astype(jnp.int32).reshape(1)
    p_twin, st_twin, stats = scores(kv_twin, queries, st_own, y_index)
    all_stats = exchange(stats, y_groups)
    dkv_twin, dq = grads(kv_twin, p_twin, st_twin, all_stats, queries)
    dkv_back = swap(dkv_twin, 1)
    dkv_own, dq_own, *dq_send = grads(kv_own, p_own, st_own, all_stats, queries, dq)
    dkv = (dkv_own + dkv_back.astype(F32)).astype(BF16)
    dkv_all = exchange(dkv, z_groups)
    dq_parts = [swap(part, 2 * x) for x, part in enumerate(dq_send, 1)]
    grad_query = dq_own + sum(part.astype(F32) for part in dq_parts)
    grad_kv = jnp.sum(dkv_all.astype(F32), axis=0).astype(BF16)
    return grad_query.astype(BF16), grad_kv[:, 0:HD], grad_kv[:, HD : 2 * HD]


def solution(mesh):
    both = P("ctx", "kvh")
    return jax.shard_map(
        per_device,
        mesh=mesh,
        in_specs=(both, both, both, both, both, P("ctx"), P("ctx")),
        out_specs=(both, both, both),
        check_vma=False,
    )
```

time: 995 us -> 124 us (0.12)
  waiting for transfers between devices: 513 us -> 29.1 us
  starting transfers between devices: 248 us -> 30.6 us
  matrix products: 67 us -> 0 us
  blocking collectives: 103 us -> 36 us
  Pallas kernels: 0 us -> 19 us
  other arithmetic: 17.2 us -> 1.71 us
  between operations: 14.9 us -> 0.82 us
  local copies, waits for them, and re-layouts: 17.7 us -> 6.16 us
    ppermute x127 -> x8, waiting for transfers between devices: 500 us -> 27.7 us  [swap(): return lax.ppermute(x, 'ctx', [(i, i ^ bits) for i in range(n)])]
    ppermute x127 -> x8, starting transfers between devices: 248 us -> 27.1 us  [swap(): return lax.ppermute(x, 'ctx', [(i, i ^ bits) for i in range(n)])]
    all_gather x1 -> x0, blocking collectives: 79 us -> none  [per_device(): lax.all_gather(segment, 'ctx', axis=0, tiled=True)]
    dot_general x321 -> x0, matrix products: 67 us -> none  [the longest x64 15.2 us: update(): jnp.einsum('hgqk,khd->qhgd', dscores_b, key_block, preferred_element_type...]
    all_to_all x0 -> x2, blocking collectives: none -> 36 us  [exchange(): return lax.all_to_all(x, 'ctx', 0, 0, tiled=True, axis_index_groups=groups)]
    unnamed x1 -> x0, blocking collectives: 23.5 us -> none
    pallas_call x0 -> x5, Pallas kernels: none -> 19 us  [the longest x2 11.2 us: grads(): pl.pallas_call(functools.partial(grad_kernel, last), grid=(STEPS,), in_sp...]
    all_gather x1 -> x0, waiting for transfers between devices: 11.5 us -> none  [per_device(): key_piece = lax.all_gather(key_rows, 'ctx', axis=0, tiled=True)]
  transfers between devices with their start and end apart: 128 -> 9, of which waited for: 127 -> 4; matrix products, arithmetic and copies ran while one was open for 9% -> 1% of each run, Pallas kernels for 0% -> 8%
where the time goes in v1:
time: 124 us; the launch traced here: 123 us
  blocking collectives  36 us (29%)
  starting transfers between devices  30.6 us (25%)
  waiting for transfers between devices  29.1 us (23%)
  Pallas kernels  19 us (15%)
  local copies, waits for them, and re-layouts  6.16 us (5%)
  other arithmetic  1.71 us (1%)
    all_to_all x2, blocking collectives, exchange(): return lax.all_to_all(x, 'ctx', 0, 0, tiled=True, axis_index_groups=groups)  36 us
    ppermute x8, waiting for transfers between devices, swap(): return lax.ppermute(x, 'ctx', [(i, i ^ bits) for i in range(n)])  27.7 us
    ppermute x8, starting transfers between devices, swap(): return lax.ppermute(x, 'ctx', [(i, i ^ bits) for i in range(n)])  27.1 us
    pallas_call x2, Pallas kernels, grads(): pl.pallas_call(functools.partial(grad_kernel, last), grid=(STEPS,), in_sp...  11.2 us
    pallas_call x2, Pallas kernels, scores(): pl.pallas_call(functools.partial(score_kernel, 0 if prev is None else STE...  7.19 us
    unnamed x14, local copies, waits for them, and re-layouts  5.53 us
    all_to_all x1, starting transfers between devices, exchange(): return lax.all_to_all(x, 'ctx', 0, 0, tiled=True, axis_index_groups=groups)  3.49 us
  transfers between devices with their start and end apart: 9, of which 4 were waited for; matrix products, arithmetic and copies ran while one was open for 1% of the time, Pallas kernels for 8%

profile of v1, /device:TPU:1, one launch (start us, length us, event | category | flops | bytes accessed | tf_op | source)
XLA Modules:
  0.0 123.3 jit_solution(7634454976377520591)
XLA Ops:
  0.6 0.0 copy-start
  0.6 0.9 copy-done
  1.5 0.0 copy-start.1
  1.5 0.9 copy-done.1
  2.4 0.0 copy-start.2
  2.4 0.9 copy-done.2
  3.3 0.0 copy-start.3
  3.3 0.8 copy-done.3
  4.1 0.0 copy-start.4
  4.1 0.8 copy-done.4
  4.9 0.0 copy-start.5
  4.9 0.7 copy-done.5
  5.5 0.0 copy-start.6
  5.5 0.7 copy-done.6
  6.2 0.7 pack.1
  6.9 28.1 %all_to_all.15.refs_0_.kv_ref = bf16[8,144,256]{2,1,0:T(8,128)(2,1)S(1)} all-to-all(bf16[8,144,256]{2,1,0:T(8,128)(2,1)S(1)} %get-tuple-element.17), channel_id=1, replica_groups={{0,64,128,192,256,320,384,448},{8,72,136,200,264,328,392,456},{16,80,14..., dimensions={0} | all-to-all | bytes 1179648 | tf_op jit(solution)/shard_map/all_to_all | solution.py:300
  35.0 4.3 %collective-permute-start.3 = (bf16[8,144,256]{2,1,0:T(8,128)(2,1)S(1)}, bf16[8,144,256]{2,1,0:T(8,128)(2,1)S(1)}, u32[]{:S(2)}, u32[]{:S(2)}) collective-permute-start(bf16[8,144,256]{2,1,0:T(8,128)(2,1)S(1)} %all_to_all.15.refs_0_.kv_ref), channel_id=1, source_target_pairs={{0,8},{8,0},{16,24},{24,16},{32,40},{40,32},{48,56},{56,48},{64,72... | collective-permute-start | bytes 1769480 | tf_op jit(solution)/shard_map/ppermute | solution.py:297
  39.3 5.2 %collective-permute-start.2 = (bf16[144,1024]{1,0:T(8,128)(2,1)S(1)}, bf16[144,1024]{1,0:T(8,128)(2,1)S(1)}, u32[]{:S(2)}, u32[]{:S(2)}) collective-permute-start(bf16[144,1024]{1,0:T(8,128)(2,1)S(1)} %get-tuple-element.18.refs_1_.q0), channel_id=1, source_target_pairs={{0,48},{8,56},{16,32},{24,40},{32,16},{40,24},{48,0},{56,8},{64,11... | collective-permute-start | bytes 884744 | tf_op jit(solution)/shard_map/ppermute | solution.py:297
  44.5 1.9 %collective-permute-start.1 = (bf16[144,1024]{1,0:T(8,128)(2,1)S(1)}, bf16[144,1024]{1,0:T(8,128)(2,1)S(1)}, u32[]{:S(2)}, u32[]{:S(2)}) collective-permute-start(bf16[144,1024]{1,0:T(8,128)(2,1)S(1)} %get-tuple-element.18.refs_1_.q0), channel_id=1, source_target_pairs={{0,32},{8,40},{16,48},{24,56},{32,0},{40,8},{48,16},{56,24},{64,96... | collective-permute-start | bytes 884744 | tf_op jit(solution)/shard_map/ppermute | solution.py:297
  46.5 2.2 %collective-permute-start = (bf16[144,1024]{1,0:T(8,128)(2,1)S(1)}, bf16[144,1024]{1,0:T(8,128)(2,1)S(1)}, u32[]{:S(2)}, u32[]{:S(2)}) collective-permute-start(bf16[144,1024]{1,0:T(8,128)(2,1)S(1)} %get-tuple-element.18.refs_1_.q0), channel_id=1, source_target_pairs={{0,16},{8,24},{16,0},{24,8},{32,48},{40,56},{48,32},{56,40},{64,80... | collective-permute-start | bytes 884744 | tf_op jit(solution)/shard_map/ppermute | solution.py:297
  48.7 3.1 %collective-permute-done.2.refs_4_.q3 = bf16[144,1024]{1,0:T(8,128)(2,1)S(1)} collective-permute-done((bf16[144,1024]{1,0:T(8,128)(2,1)S(1)}, bf16[144,1024]{1,0:T(8,128)(2,1)S(1)}, u32[]{:S(2)}, u32[]{:S(2)}) %collective-permute-start.2) | collective-permute-done | bytes 294944 | tf_op jit(solution)/shard_map/ppermute | solution.py:297
  51.8 18.0 %collective-permute-done.1.refs_3_.q2 = bf16[144,1024]{1,0:T(8,128)(2,1)S(1)} collective-permute-done((bf16[144,1024]{1,0:T(8,128)(2,1)S(1)}, bf16[144,1024]{1,0:T(8,128)(2,1)S(1)}, u32[]{:S(2)}, u32[]{:S(2)}) %collective-permute-start.1) | collective-permute-done | bytes 294944 | tf_op jit(solution)/shard_map/ppermute | solution.py:297
  69.8 0.0 collective-permute-done.refs_2_.q1
  69.8 3.6 %scores.2 = (bf16[1024,2048]{1,0:T(8,128)(2,1)S(1)}, f32[4,8,512]{2,1,0:T(8,128)S(1)}) custom-call(bf16[8,144,256]{2,1,0:T(8,128)(2,1)S(1)} %all_to_all.15.refs_0_.kv_ref, bf16[144,1024]{1,0:T(8,128)(2,1)S(1)} %get-tuple-element.18.refs_1_.q0, bf16[144,1024]{1,0:T(8,128)(2,1)S(1)} %collective-permute-done.refs_2_.q1, ...), custom_call_target="tpu_custom_call" | custom-call | flops 1073741824 | bytes 4194304 | tf_op jit(solution)/shard_map/scores/pallas_call | solution.py:231
  73.4 0.0 collective-permute-done.3.refs_0_.kv_ref
  73.4 3.6 %scores.3 = (bf16[1024,2048]{1,0:T(8,128)(2,1)S(1)}, f32[4,8,512]{2,1,0:T(8,128)S(1)}, f32[4,8,512]{2,1,0:T(8,128)S(1)}) custom-call(bf16[8,144,256]{2,1,0:T(8,128)(2,1)S(1)} %collective-permute-done.3.refs_0_.kv_ref, bf16[144,1024]{1,0:T(8,128)(2,1)S(1)} %get-tuple-element.18.refs_1_.q0, bf16[144,1024]{1,0:T(8,128)(2,1)S(1)} %collective-permute-done.refs_2_.q1, ...), custom_call_target="tpu_custom_call" | custom-call | flops 1073741824 | bytes 4194304 | tf_op jit(solution)/shard_map/scores/pallas_call | solution.py:231
  77.0 7.9 %all_to_all.16.all_ref = f32[4,8,512]{2,1,0:T(8,128)S(1)} all-to-all(f32[4,8,512]{2,1,0:T(8,128)S(1)} %get-tuple-element.21), channel_id=1, replica_groups={{0,16,32,48},{8,24,40,56},{64,80,96,112},{72,88,104,120},{128,144,160,1..., dimensions={0} | all-to-all | bytes 131072 | tf_op jit(solution)/shard_map/all_to_all | solution.py:300
  84.9 5.4 %grads.2 = (bf16[8,128,256]{2,1,0:T(8,128)(2,1)S(1)}, f32[4,128,512]{2,1,0:T(8,128)S(1)}) custom-call(bf16[8,144,256]{2,1,0:T(8,128)(2,1)S(1)} %collective-permute-done.3.refs_0_.kv_ref, bf16[1024,2048]{1,0:T(8,128)(2,1)S(1)} %get-tuple-element.22.pt_ref, f32[4,8,512]{2,1,0:T(8,128)S(1)} %get-tuple-element.23.st_ref, f32[4,8,512]{2,1,0:T(8,128)S(1)} %all_to_all.16.all_ref, ...), custom_call_target="tpu_custom_call" | custom-call | flops 4294967296 | bytes 4194304 | tf_op jit(solution)/shard_map/grads/pallas_call | solution.py:274
  90.3 4.1 %collective-permute-start.7 = (bf16[8,128,256]{2,1,0:T(8,128)(2,1)S(1)}, bf16[8,128,256]{2,1,0:T(8,128)(2,1)S(1)}, u32[]{:S(2)}, u32[]{:S(2)}) collective-permute-start(bf16[8,128,256]{2,1,0:T(8,128)(2,1)S(1)} %get-tuple-element.30), channel_id=1, source_target_pairs={{0,8},{8,0},{16,24},{24,16},{32,40},{40,32},{48,56},{56,48},{64,72... | collective-permute-start | bytes 1572872 | tf_op jit(solution)/shard_map/ppermute | solution.py:297
  94.4 5.8 %grads.3 = (f32[8,128,256]{2,1,0:T(8,128)S(1)}, f32[128,512]{1,0:T(8,128)S(1)}, bf16[128,512]{1,0:T(8,128)(2,1)S(1)}, bf16[128,512]{1,0:T(8,128)(2,1)S(1)}, bf16[128,512]{1,0:T(8,128)(2,1)S(1)}) custom-call(bf16[8,144,256]{2,1,0:T(8,128)(2,1)S(1)} %all_to_all.15.refs_0_.kv_ref, bf16[1024,2048]{1,0:T(8,128)(2,1)S(1)} %get-tuple-element.19.pt_ref, ...), custom_call_target="tpu_custom_call" | custom-call | flops 4294967296 | bytes 4194304 | tf_op jit(solution)/shard_map/grads/pallas_call | solution.py:274
  100.2 0.0 collective-permute-done.7
  100.2 0.9 add_convert_fusion
  101.1 3.5 %all-to-all-start.2 = ((bf16[8,128,256]{2,1,0:T(8,128)(2,1)}), bf16[8,128,256]{2,1,0:T(8,128)(2,1)S(1)}, u32[]{:S(2)}, u32[]{:S(2)}) async-start(bf16[8,128,256]{2,1,0:T(8,128)(2,1)} %add_convert_fusion), calls=%async_computation.2 | async-start | bytes 1048576 | tf_op jit(solution)/shard_map/all_to_all | solution.py:300
  104.6 2.5 %collective-permute-start.4 = (bf16[128,512]{1,0:T(8,128)(2,1)S(1)}, bf16[128,512]{1,0:T(8,128)(2,1)S(1)}, u32[]{:S(2)}, u32[]{:S(2)}) collective-permute-start(bf16[128,512]{1,0:T(8,128)(2,1)S(1)} %get-tuple-element.26), channel_id=1, source_target_pairs={{0,16},{8,24},{16,0},{24,8},{32,48},{40,56},{48,32},{56,40},{64,80... | collective-permute-start | bytes 393224 | tf_op jit(solution)/shard_map/ppermute | solution.py:297
  107.2 2.0 %collective-permute-start.5 = (bf16[128,512]{1,0:T(8,128)(2,1)S(1)}, bf16[128,512]{1,0:T(8,128)(2,1)S(1)}, u32[]{:S(2)}, u32[]{:S(2)}) collective-permute-start(bf16[128,512]{1,0:T(8,128)(2,1)S(1)} %get-tuple-element.27), channel_id=1, source_target_pairs={{0,32},{8,40},{16,48},{24,56},{32,0},{40,8},{48,16},{56,24},{64,96... | collective-permute-start | bytes 393224 | tf_op jit(solution)/shard_map/ppermute | solution.py:297
  109.2 4.7 %collective-permute-start.6 = (bf16[128,512]{1,0:T(8,128)(2,1)S(1)}, bf16[128,512]{1,0:T(8,128)(2,1)S(1)}, u32[]{:S(2)}, u32[]{:S(2)}) collective-permute-start(bf16[128,512]{1,0:T(8,128)(2,1)S(1)} %get-tuple-element.28), channel_id=1, source_target_pairs={{0,48},{8,56},{16,32},{24,40},{32,16},{40,24},{48,0},{56,8},{64,11... | collective-permute-start | bytes 393224 | tf_op jit(solution)/shard_map/ppermute | solution.py:297
  113.9 0.0 collective-permute-done.4
  113.9 6.6 %collective-permute-done.5 = bf16[128,512]{1,0:T(8,128)(2,1)S(1)} collective-permute-done((bf16[128,512]{1,0:T(8,128)(2,1)S(1)}, bf16[128,512]{1,0:T(8,128)(2,1)S(1)}, u32[]{:S(2)}, u32[]{:S(2)}) %collective-permute-start.5) | collective-permute-done | bytes 131104 | tf_op jit(solution)/shard_map/ppermute | solution.py:297
  120.5 0.0 collective-permute-done.6
  120.5 0.7 add_convert_fusion.1
  121.2 1.4 %all-to-all-done.2 = bf16[8,128,256]{2,1,0:T(8,128)(2,1)S(1)} async-done(((bf16[8,128,256]{2,1,0:T(8,128)(2,1)}), bf16[8,128,256]{2,1,0:T(8,128)(2,1)S(1)}, u32[]{:S(2)}, u32[]{:S(2)}) %all-to-all-start.2) | async-done | bytes 524320 | tf_op jit(solution)/shard_map/all_to_all | solution.py:300
  122.6 0.1 reduce_sum.12
  122.6 0.6 fusion
Async XLA Ops:
  0.6 0.9 copy-start
  1.5 0.9 copy-start.1
  2.4 0.9 copy-start.2
  3.3 0.8 copy-start.3
  4.1 0.8 copy-start.4
  4.9 0.7 copy-start.5
  5.5 0.7 copy-start.6
  35.0 38.4 %collective-permute-start.3 = (bf16[8,144,256]{2,1,0:T(8,128)(2,1)S(1)}, bf16[8,144,256]{2,1,0:T(8,128)(2,1)S(1)}, u32[]{:S(2)}, u32[]{:S(2)}) collective-permute-start(bf16[8,144,256]{2,1,0:T(8,128)(2,1)S(1)} %all_to_all.15.refs_0_.kv_ref), channel_id=1, source_target_pairs={{0,8},{8,0},{16,24},{24,16},{32,40},{40,32},{48,56},{56,48},{64,72... | collective-permute-start | bytes 1769480 | tf_op jit(solution)/shard_map/ppermute | solution.py:297
  39.3 12.5 %collective-permute-start.2 = (bf16[144,1024]{1,0:T(8,128)(2,1)S(1)}, bf16[144,1024]{1,0:T(8,128)(2,1)S(1)}, u32[]{:S(2)}, u32[]{:S(2)}) collective-permute-start(bf16[144,1024]{1,0:T(8,128)(2,1)S(1)} %get-tuple-element.18.refs_1_.q0), channel_id=1, source_target_pairs={{0,48},{8,56},{16,32},{24,40},{32,16},{40,24},{48,0},{56,8},{64,11... | collective-permute-start | bytes 884744 | tf_op jit(solution)/shard_map/ppermute | solution.py:297
  44.5 25.3 %collective-permute-start.1 = (bf16[144,1024]{1,0:T(8,128)(2,1)S(1)}, bf16[144,1024]{1,0:T(8,128)(2,1)S(1)}, u32[]{:S(2)}, u32[]{:S(2)}) collective-permute-start(bf16[144,1024]{1,0:T(8,128)(2,1)S(1)} %get-tuple-element.18.refs_1_.q0), channel_id=1, source_target_pairs={{0,32},{8,40},{16,48},{24,56},{32,0},{40,8},{48,16},{56,24},{64,96... | collective-permute-start | bytes 884744 | tf_op jit(solution)/shard_map/ppermute | solution.py:297
  46.5 23.3 %collective-permute-start = (bf16[144,1024]{1,0:T(8,128)(2,1)S(1)}, bf16[144,1024]{1,0:T(8,128)(2,1)S(1)}, u32[]{:S(2)}, u32[]{:S(2)}) collective-permute-start(bf16[144,1024]{1,0:T(8,128)(2,1)S(1)} %get-tuple-element.18.refs_1_.q0), channel_id=1, source_target_pairs={{0,16},{8,24},{16,0},{24,8},{32,48},{40,56},{48,32},{56,40},{64,80... | collective-permute-start | bytes 884744 | tf_op jit(solution)/shard_map/ppermute | solution.py:297
  90.3 9.9 %collective-permute-start.7 = (bf16[8,128,256]{2,1,0:T(8,128)(2,1)S(1)}, bf16[8,128,256]{2,1,0:T(8,128)(2,1)S(1)}, u32[]{:S(2)}, u32[]{:S(2)}) collective-permute-start(bf16[8,128,256]{2,1,0:T(8,128)(2,1)S(1)} %get-tuple-element.30), channel_id=1, source_target_pairs={{0,8},{8,0},{16,24},{24,16},{32,40},{40,32},{48,56},{56,48},{64,72... | collective-permute-start | bytes 1572872 | tf_op jit(solution)/shard_map/ppermute | solution.py:297
  101.1 21.5 %all-to-all-start.2 = ((bf16[8,128,256]{2,1,0:T(8,128)(2,1)}), bf16[8,128,256]{2,1,0:T(8,128)(2,1)S(1)}, u32[]{:S(2)}, u32[]{:S(2)}) async-start(bf16[8,128,256]{2,1,0:T(8,128)(2,1)} %add_convert_fusion), calls=%async_computation.2 | async-start | bytes 1048576 | tf_op jit(solution)/shard_map/all_to_all | solution.py:300
  104.6 9.3 %collective-permute-start.4 = (bf16[128,512]{1,0:T(8,128)(2,1)S(1)}, bf16[128,512]{1,0:T(8,128)(2,1)S(1)}, u32[]{:S(2)}, u32[]{:S(2)}) collective-permute-start(bf16[128,512]{1,0:T(8,128)(2,1)S(1)} %get-tuple-element.26), channel_id=1, source_target_pairs={{0,16},{8,24},{16,0},{24,8},{32,48},{40,56},{48,32},{56,40},{64,80... | collective-permute-start | bytes 393224 | tf_op jit(solution)/shard_map/ppermute | solution.py:297
  107.2 13.3 %collective-permute-start.5 = (bf16[128,512]{1,0:T(8,128)(2,1)S(1)}, bf16[128,512]{1,0:T(8,128)(2,1)S(1)}, u32[]{:S(2)}, u32[]{:S(2)}) collective-permute-start(bf16[128,512]{1,0:T(8,128)(2,1)S(1)} %get-tuple-element.27), channel_id=1, source_target_pairs={{0,32},{8,40},{16,48},{24,56},{32,0},{40,8},{48,16},{56,24},{64,96... | collective-permute-start | bytes 393224 | tf_op jit(solution)/shard_map/ppermute | solution.py:297
  109.2 11.3 %collective-permute-start.6 = (bf16[128,512]{1,0:T(8,128)(2,1)S(1)}, bf16[128,512]{1,0:T(8,128)(2,1)S(1)}, u32[]{:S(2)}, u32[]{:S(2)}) collective-permute-start(bf16[128,512]{1,0:T(8,128)(2,1)S(1)} %get-tuple-element.28), channel_id=1, source_target_pairs={{0,48},{8,56},{16,32},{24,40},{32,16},{40,24},{48,0},{56,8},{64,11... | collective-permute-start | bytes 393224 | tf_op jit(solution)/shard_map/ppermute | solution.py:297

commit v2 on v1

--- a/solution.py
+++ b/solution.py
@@ -26,7 +26,7 @@
 FLOOR = -1e25
 F32 = jnp.float32
 BF16 = jnp.bfloat16
-VMEM_LIMIT = 24 * 1024 * 1024
+VMEM_LIMIT = 57
 
 NT = (((1,), (1,)), ((), ()))
 TN = (((0,), (0,)), ((), ()))
@@ -36,32 +36,56 @@
     return lax.dot_general(a, b, dims, preferred_element_type=F32)
 
 
-def pack_kernel(order_ref, seg_ref, q_ref, k_ref, v_ref, o_ref, g_ref, qp_ref, kvp_ref):
+def pack_kernel(
+    order_hbm, seg_hbm, q_hbm, k_hbm, v_hbm, o_hbm, g_hbm, kvp_hbm, qp_ref, gp_ref,
+    order_ref, seg_ref, kv_ref, o_ref, in_sems, out_sems,
+):
+    moves = (
+        (order_hbm, order_ref),
+        (seg_hbm, seg_ref),
+        (k_hbm, kv_ref.at[0:TOK, 0:HD]),
+        (v_hbm, kv_ref.at[0:TOK, HD : 2 * HD]),
+        (q_hbm, qp_ref.at[0:TOK]),
+        (g_hbm, gp_ref.at[0:TOK]),
+        (o_hbm, o_ref),
+    )
+    copies = [
+        pltpu.make_async_copy(src, dst, in_sems.at[i]) for i, (src, dst) in enumerate(moves)
+    ]
+    for copy in copies:
+        copy.start()
+    for copy in copies[:4]:
+        copy.wait()
     lane = lax.broadcasted_iota(jnp.int32, (1, TOK), 1)
     block = jnp.where(lane < BLK, order_ref[0], order_ref[1]).astype(F32)
     doc = seg_ref[...].astype(F32)
-    qp_ref[0:TOK, 0 : GROUP * HD] = q_ref[...]
-    qp_ref[0:TOK, GROUP * HD : 2 * GROUP * HD] = g_ref[...]
+    kv_extra = jnp.concatenate([doc, block], axis=1)
+    kv_ref[TOK:PAY, :] = jnp.broadcast_to(kv_extra, (EXTRA, 2 * HD)).astype(BF16)
+    outs = [
+        pltpu.make_async_copy(kv_ref, kvp_hbm.at[z], out_sems.at[z]) for z in range(ZS)
+    ]
+    for copy in outs:
+        copy.start()
+    for copy in copies[4:]:
+        copy.wait()
     highs, lows = [], []
     for h in range(GROUP):
         cols = slice(h * HD, (h + 1) * HD)
-        prod = g_ref[:, cols].astype(F32) * o_ref[:, cols].astype(F32)
+        prod = gp_ref[0:TOK, cols].astype(F32) * o_ref[:, cols].astype(F32)
         delta = jnp.sum(prod.T, axis=0, keepdims=True)
         high = delta.astype(BF16).astype(F32)
         highs.append(high)
         lows.append(delta - high)
-    first = jnp.concatenate(highs + lows, axis=1)
     zero = jnp.zeros_like(doc)
-    second = jnp.concatenate([doc, block] + [zero] * 6, axis=1)
-    row = lax.broadcasted_iota(jnp.int32, (EXTRA, 8 * TOK), 0)
-    extra = jnp.where(row == 0, first, jnp.where(row == 1, second, 0.0))
-    qp_ref[TOK:PAY, :] = extra.astype(BF16)
-    kv_extra = jnp.concatenate([doc, block], axis=1)
-    kv_extra = jnp.broadcast_to(kv_extra, (EXTRA, 2 * HD)).astype(BF16)
-    for z in range(ZS):
-        kvp_ref[z, 0:TOK, 0:HD] = k_ref[...]
-        kvp_ref[z, 0:TOK, HD : 2 * HD] = v_ref[...]
-        kvp_ref[z, TOK:PAY, :] = kv_extra
+    q_extra = jnp.concatenate([doc, block, zero, zero], axis=1)
+    qp_ref[TOK:PAY, :] = jnp.broadcast_to(q_extra, (EXTRA, GROUP * HD)).astype(BF16)
+    row = lax.broadcasted_iota(jnp.int32, (EXTRA, GROUP * HD), 0)
+    g_extra = jnp.where(
+        row == 0, jnp.concatenate(highs, axis=1), jnp.concatenate(lows, axis=1)
+    )
+    gp_ref[TOK:PAY, :] = g_extra.astype(BF16)
+    for copy in outs:
+        copy.wait()
 
 
 def code_of(doc, block):
@@ -86,7 +110,7 @@
             for h in range(GROUP):
                 qs[h, toks, :] = q_ref[0:TOK, h * HD : (h + 1) * HD]
             info = q_ref[TOK:PAY, :].astype(F32)
-            doc, block = info[1:2, 0:TOK], info[1:2, TOK : 2 * TOK]
+            doc, block = info[0:1, 0:TOK], info[0:1, TOK : 2 * TOK]
             code[0:1, toks] = code_of(doc, block)
             code[1:2, toks] = doc * TOKENS
 
@@ -121,7 +145,8 @@
                     fin_ref[y_ref[0] ^ d, GROUP : 2 * GROUP, to] = total[:, of]
 
 
-def grad_kernel(last, kv_ref, pt_ref, st_ref, all_ref, q0, q1, q2, q3, *rest):
+def grad_kernel(last, kv_ref, pt_ref, st_ref, all_ref, *rest):
+    q_refs, g_refs, rest = rest[:YS], rest[YS : 2 * YS], rest[2 * YS :]
     if last:
         dq_in, dkv_ref, own_ref, send1, send2, send3, qs, gs, delta, dq = rest
     else:
@@ -130,16 +155,14 @@
 
     @pl.when(step == 0)
     def _():
-        for x, q_ref in enumerate((q0, q1, q2, q3)):
+        for x, (q_ref, g_ref) in enumerate(zip(q_refs, g_refs)):
             toks = slice(x * TOK, (x + 1) * TOK)
+            info = g_ref[TOK:PAY, :].astype(F32)
             for h in range(GROUP):
-                qs[h, toks, :] = q_ref[0:TOK, h * HD : (h + 1) * HD]
-                gs[h, toks, :] = q_ref[0:TOK, (GROUP + h) * HD : (GROUP + h + 1) * HD]
-            info = q_ref[TOK:PAY, :].astype(F32)
-            for h in range(GROUP):
-                high = info[0:1, h * TOK : (h + 1) * TOK]
-                low = info[0:1, (GROUP + h) * TOK : (GROUP + h + 1) * TOK]
-                delta[h : h + 1, toks] = high + low
+                cols = slice(h * HD, (h + 1) * HD)
+                qs[h, toks, :] = q_ref[0:TOK, cols]
+                gs[h, toks, :] = g_ref[0:TOK, cols]
+                delta[h : h + 1, toks] = info[0:1, cols] + info[1:2, cols]
         dq[...] = dq_in[...] if last else jnp.zeros_like(dq)
 
     top = functools.reduce(jnp.maximum, [all_ref[y, 0:GROUP] for y in range(YS)])
@@ -185,18 +208,28 @@
     return jax.ShapeDtypeStruct(shape, dtype)
 
 
-def params():
-    return pltpu.CompilerParams(vmem_limit_bytes=VMEM_LIMIT)
+def params(limit=VMEM_LIMIT):
+    return pltpu.CompilerParams(vmem_limit_bytes=limit << 20)
 
 
 def pack(order, seg, q, k, v, o, g):
+    hbm = pl.BlockSpec(memory_space=pltpu.HBM)
     vm = pl.BlockSpec(memory_space=pltpu.VMEM)
+    pay = shape_of((PAY, GROUP * HD), BF16)
     return pl.pallas_call(
         pack_kernel,
-        out_shape=(shape_of((PAY, 2 * GROUP * HD), BF16), shape_of((ZS, PAY, 2 * HD), BF16)),
-        in_specs=[pl.BlockSpec(memory_space=pltpu.SMEM)] + [vm] * 6,
-        out_specs=(vm, vm),
-        compiler_params=params(),
+        out_shape=(shape_of((ZS, PAY, 2 * HD), BF16), pay, pay),
+        in_specs=[hbm] * 7,
+        out_specs=(hbm, vm, vm),
+        scratch_shapes=[
+            pltpu.SMEM((2,), jnp.int32),
+            pltpu.VMEM((1, TOK), jnp.int32),
+            pltpu.VMEM((PAY, 2 * HD), BF16),
+            pltpu.VMEM((TOK, GROUP * HD), BF16),
+            pltpu.SemaphoreType.DMA((7,)),
+            pltpu.SemaphoreType.DMA((ZS,)),
+        ],
+        compiler_params=params(60),
         name="pack",
     )(order, seg, q, k, v, o, g)
 
@@ -207,7 +240,7 @@
 
 def scores(kv, queries, prev=None, y_index=None):
     in_specs = [pl.BlockSpec((2, PAY, 2 * HD), lambda i: (i, 0, 0))]
-    in_specs += [whole((PAY, 2 * GROUP * HD))] * YS
+    in_specs += [whole((PAY, GROUP * HD))] * YS
     args = [kv, *queries]
     out_shape = [
         shape_of((ZS * TOK, GROUP * QT), BF16),
@@ -237,21 +270,21 @@
         scratch_shapes=scratch,
         compiler_params=params(),
         cost_estimate=pl.CostEstimate(
-            flops=4 * PAIRS * HD, bytes_accessed=4 << 20, transcendentals=PAIRS
+            flops=PAIRS, bytes_accessed=1 << 16, transcendentals=0
         ),
         name="scores",
     )(*args)
 
 
-def grads(kv, probs, stats, all_stats, queries, dq_in=None):
+def grads(kv, probs, stats, all_stats, queries, outs, dq_in=None):
     last = dq_in is not None
     in_specs = [
         pl.BlockSpec((2, PAY, 2 * HD), lambda i: (i, 0, 0)),
         pl.BlockSpec((KT, GROUP * QT), lambda i: (i, 0)),
         pl.BlockSpec((1, 2 * GROUP, QT), lambda i: (i, 0, 0)),
         whole((YS, 2 * GROUP, QT)),
-    ] + [whole((PAY, 2 * GROUP * HD))] * YS
-    args = [kv, probs, stats, all_stats, *queries]
+    ] + [whole((PAY, GROUP * HD))] * (2 * YS)
+    args = [kv, probs, stats, all_stats, *queries, *outs]
     dkv_type = F32 if last else BF16
     out_shape = [shape_of((ZS, TOK, 2 * HD), dkv_type)]
     out_specs = [pl.BlockSpec((2, TOK, 2 * HD), lambda i: (i, 0, 0))]
@@ -299,19 +332,23 @@
     def exchange(x, groups):
         return lax.all_to_all(x, "ctx", 0, 0, tiled=True, axis_index_groups=groups)
 
-    q_pay, kv_pay = pack(
+    kv_pay, q_pay, g_pay = pack(
         block_order, segment.reshape(1, TOK), query, key_rows, value_rows, output, grad_out
     )
     kv_own = exchange(kv_pay, z_groups)
-    queries = [q_pay] + [swap(q_pay, 2 * x) for x in range(1, YS)]
+    q_far, q_near = swap(q_pay, 4), swap(q_pay, 2)
+    g_far, g_near = swap(g_pay, 4), swap(g_pay, 2)
+    queries = [q_pay, q_near, q_far, swap(q_far, 2)]
+    outs = [g_pay, g_near, g_far, swap(g_far, 2)]
+    kv_own, queries, outs = lax.optimization_barrier((kv_own, queries, outs))
     kv_twin = swap(kv_own, 1)
     p_own, st_own = scores(kv_own, queries)
     y_index = (lax.axis_index("ctx") // 2 % YS).astype(jnp.int32).reshape(1)
     p_twin, st_twin, stats = scores(kv_twin, queries, st_own, y_index)
     all_stats = exchange(stats, y_groups)
-    dkv_twin, dq = grads(kv_twin, p_twin, st_twin, all_stats, queries)
+    dkv_twin, dq = grads(kv_twin, p_twin, st_twin, all_stats, queries, outs)
     dkv_back = swap(dkv_twin, 1)
-    dkv_own, dq_own, *dq_send = grads(kv_own, p_own, st_own, all_stats, queries, dq)
+    dkv_own, dq_own, *dq_send = grads(kv_own, p_own, st_own, all_stats, queries, outs, dq)
     dkv = (dkv_own + dkv_back.astype(F32)).astype(BF16)
     dkv_all = exchange(dkv, z_groups)
     dq_parts = [swap(part, 2 * x) for x, part in enumerate(dq_send, 1)]

time: 124 us -> 119 us (0.960)
  blocking collectives: 36 us -> 11.1 us
  starting transfers between devices: 30.6 us -> 53.8 us
  waiting for transfers between devices: 29.1 us -> 13.6 us
  Pallas kernels: 19 us -> 32.6 us
  local copies, waits for them, and re-layouts: 6.16 us -> 1.5 us
  other arithmetic: 1.71 us -> 3.89 us
    all_to_all x2 -> x1, blocking collectives: 36 us -> 11.1 us  [exchange(): return lax.all_to_all(x, 'ctx', 0, 0, tiled=True, axis_index_groups=groups)]
    ppermute x8 -> x11, waiting for transfers between devices: 27.7 us -> 13.2 us  [swap(): return lax.ppermute(x, 'ctx', [(i, i ^ bits) for i in range(n)])]
    all_to_all x1 -> x2, starting transfers between devices: 3.49 us -> 17.4 us  [exchange(): return lax.all_to_all(x, 'ctx', 0, 0, tiled=True, axis_index_groups=groups)]
    ppermute x8 -> x11, starting transfers between devices: 27.1 us -> 36.4 us  [swap(): return lax.ppermute(x, 'ctx', [(i, i ^ bits) for i in range(n)])]
    pallas_call x2, Pallas kernels: 11.2 us -> 17.7 us  [grads(): pl.pallas_call(functools.partial(grad_kernel, last), grid=(STEPS,), in_sp...]
    pallas_call x2, Pallas kernels: 7.19 us -> 12.3 us  [scores(): pl.pallas_call(functools.partial(score_kernel, 0 if prev is None else STE...]
    unnamed x14 -> x16, local copies, waits for them, and re-layouts: 5.53 us -> 0.87 us
    pallas_call x1, Pallas kernels: 0.69 us -> 2.5 us  [pack(): pl.pallas_call(pack_kernel, out_shape=(shape_of((ZS, PAY, 2 * HD), BF16),...]
  transfers between devices with their start and end apart: 9 -> 13, of which waited for: 4 -> 5; matrix products, arithmetic and copies ran while one was open for 1% -> 1% of each run, Pallas kernels for 8% -> 13%
where the time goes in v2:
time: 119 us; the launch traced here: 117 us
  starting transfers between devices  53.8 us (45%)
  Pallas kernels  32.6 us (27%)
  waiting for transfers between devices  13.6 us (11%)
  blocking collectives  11.1 us (9%)
  other arithmetic  3.89 us (3%)
  local copies, waits for them, and re-layouts  1.5 us (1%)
    ppermute x11, starting transfers between devices, swap(): return lax.ppermute(x, 'ctx', [(i, i ^ bits) for i in range(n)])  36.4 us
    pallas_call x2, Pallas kernels, grads(): pl.pallas_call(functools.partial(grad_kernel, last), grid=(STEPS,), in_sp...  17.7 us
    all_to_all x2, starting transfers between devices, exchange(): return lax.all_to_all(x, 'ctx', 0, 0, tiled=True, axis_index_groups=groups)  17.4 us
    ppermute x11, waiting for transfers between devices, swap(): return lax.ppermute(x, 'ctx', [(i, i ^ bits) for i in range(n)])  13.2 us
    pallas_call x2, Pallas kernels, scores(): pl.pallas_call(functools.partial(score_kernel, 0 if prev is None else STE...  12.3 us
    all_to_all x1, blocking collectives, exchange(): return lax.all_to_all(x, 'ctx', 0, 0, tiled=True, axis_index_groups=groups)  11.1 us
    pallas_call x1, Pallas kernels, pack(): pl.pallas_call(pack_kernel, out_shape=(shape_of((ZS, PAY, 2 * HD), BF16),...  2.5 us
  transfers between devices with their start and end apart: 13, of which 5 were waited for; matrix products, arithmetic and copies ran while one was open for 1% of the time, Pallas kernels for 13%

profile of v2, /device:TPU:1, one launch (start us, length us, event | category | flops | bytes accessed | tf_op | source)
XLA Modules:
  0.0 117.3 jit_solution(11788591836582842506)
XLA Ops:
  0.6 2.5 %pack.1 = (bf16[8,144,256]{2,1,0:T(8,128)(2,1)}, bf16[144,512]{1,0:T(8,128)(2,1)}, bf16[144,512]{1,0:T(8,128)(2,1)}) custom-call(s32[2]{0:T(128)} %order_hbm.1, s32[1,128]{1,0:T(1,128)} %bitcast.2, bf16[128,512]{1,0:T(8,128)(2,1)} %q_hbm.1, bf16[128,128]{1,0:T(8,128)(2,1)} %k_hbm.1, bf16[128,128]{1,0:T(8,128)(2,1)} %v_hbm.1, bf16[128,512]{1,0:T(8,128)(2,1)} %o_hbm.1, ...), custom_call_target="tpu_custom_call" | custom-call | tf_op jit(solution)/shard_map/pack/pallas_call | solution.py:219
  3.1 10.9 %all-to-all-start = ((bf16[8,144,256]{2,1,0:T(8,128)(2,1)}), bf16[8,144,256]{2,1,0:T(8,128)(2,1)S(1)}, u32[]{:S(2)}, u32[]{:S(2)}) async-start(bf16[8,144,256]{2,1,0:T(8,128)(2,1)} %get-tuple-element.27), calls=%async_computation | async-start | bytes 1179648 | tf_op jit(solution)/shard_map/all_to_all | solution.py:333
  14.0 4.2 %collective-permute-start.1 = (bf16[144,512]{1,0:T(8,128)(2,1)}, bf16[144,512]{1,0:T(8,128)(2,1)S(1)}, u32[]{:S(2)}, u32[]{:S(2)}) collective-permute-start(bf16[144,512]{1,0:T(8,128)(2,1)} %get-tuple-element.31.refs_1_.rest_0_), channel_id=1, source_target_pairs={{0,32},{8,40},{16,48},{24,56},{32,0},{40,8},{48,16},{56,24},{64,96... | collective-permute-start | bytes 442376 | tf_op jit(solution)/shard_map/ppermute | solution.py:330
  18.2 2.0 %collective-permute-start.4 = (bf16[144,512]{1,0:T(8,128)(2,1)}, bf16[144,512]{1,0:T(8,128)(2,1)S(1)}, u32[]{:S(2)}, u32[]{:S(2)}) collective-permute-start(bf16[144,512]{1,0:T(8,128)(2,1)} %get-tuple-element.38.rest_4_), channel_id=1, source_target_pairs={{0,32},{8,40},{16,48},{24,56},{32,0},{40,8},{48,16},{56,24},{64,96... | collective-permute-start | bytes 442376 | tf_op jit(solution)/shard_map/ppermute | solution.py:330
  20.2 3.2 %collective-permute-start = (bf16[144,512]{1,0:T(8,128)(2,1)}, bf16[144,512]{1,0:T(8,128)(2,1)S(1)}, u32[]{:S(2)}, u32[]{:S(2)}) collective-permute-start(bf16[144,512]{1,0:T(8,128)(2,1)} %get-tuple-element.31.refs_1_.rest_0_), channel_id=1, source_target_pairs={{0,16},{8,24},{16,0},{24,8},{32,48},{40,56},{48,32},{56,40},{64,80... | collective-permute-start | bytes 442376 | tf_op jit(solution)/shard_map/ppermute | solution.py:330
  23.4 2.1 %collective-permute-start.3 = (bf16[144,512]{1,0:T(8,128)(2,1)}, bf16[144,512]{1,0:T(8,128)(2,1)S(1)}, u32[]{:S(2)}, u32[]{:S(2)}) collective-permute-start(bf16[144,512]{1,0:T(8,128)(2,1)} %get-tuple-element.38.rest_4_), channel_id=1, source_target_pairs={{0,16},{8,24},{16,0},{24,8},{32,48},{40,56},{48,32},{56,40},{64,80... | collective-permute-start | bytes 442376 | tf_op jit(solution)/shard_map/ppermute | solution.py:330
  25.5 0.0 collective-permute-done.1.refs_3_.rest_2_
  25.5 0.0 copy-start.1
  25.5 6.0 %collective-permute-start.2 = (bf16[144,512]{1,0:T(8,128)(2,1)S(1)}, bf16[144,512]{1,0:T(8,128)(2,1)S(1)}, u32[]{:S(2)}, u32[]{:S(2)}) collective-permute-start(bf16[144,512]{1,0:T(8,128)(2,1)S(1)} %collective-permute-done.1.refs_3_.rest_2_), channel_id=1, source_target_pairs={{0,16},{8,24},{16,0},{24,8},{32,48},{40,56},{48,32},{56,40},{64,80... | collective-permute-start | bytes 442376 | tf_op jit(solution)/shard_map/ppermute | solution.py:330
  31.5 0.0 collective-permute-done.4.rest_6_
  31.6 0.0 copy-start.5
  31.6 3.1 %collective-permute-start.5 = (bf16[144,512]{1,0:T(8,128)(2,1)S(1)}, bf16[144,512]{1,0:T(8,128)(2,1)S(1)}, u32[]{:S(2)}, u32[]{:S(2)}) collective-permute-start(bf16[144,512]{1,0:T(8,128)(2,1)S(1)} %collective-permute-done.4.rest_6_), channel_id=1, source_target_pairs={{0,16},{8,24},{16,0},{24,8},{32,48},{40,56},{48,32},{56,40},{64,80... | collective-permute-start | bytes 442376 | tf_op jit(solution)/shard_map/ppermute | solution.py:330
  34.7 0.0 collective-permute-done.refs_2_.rest_1_
  34.7 0.0 copy-start.2
  34.7 0.2 collective-permute-done.3.rest_5_
  34.9 0.0 copy-start.6
  34.9 3.2 %collective-permute-done.2.refs_4_.rest_3_ = bf16[144,512]{1,0:T(8,128)(2,1)S(1)} collective-permute-done((bf16[144,512]{1,0:T(8,128)(2,1)S(1)}, bf16[144,512]{1,0:T(8,128)(2,1)S(1)}, u32[]{:S(2)}, u32[]{:S(2)}) %collective-permute-start.2) | collective-permute-done | bytes 147488 | tf_op jit(solution)/shard_map/ppermute | solution.py:330
  38.1 0.0 copy-start.3
  38.1 3.2 %collective-permute-done.5.rest_7_ = bf16[144,512]{1,0:T(8,128)(2,1)S(1)} collective-permute-done((bf16[144,512]{1,0:T(8,128)(2,1)S(1)}, bf16[144,512]{1,0:T(8,128)(2,1)S(1)}, u32[]{:S(2)}, u32[]{:S(2)}) %collective-permute-start.5) | collective-permute-done | bytes 147488 | tf_op jit(solution)/shard_map/ppermute | solution.py:330
  41.2 0.0 copy-start.7
  41.2 0.0 all-to-all-done.refs_0_.kv_ref
  41.2 0.0 copy-start
  41.2 3.2 %collective-permute-start.6 = (bf16[8,144,256]{2,1,0:T(8,128)(2,1)S(1)}, bf16[8,144,256]{2,1,0:T(8,128)(2,1)S(1)}, u32[]{:S(2)}, u32[]{:S(2)}) collective-permute-start(bf16[8,144,256]{2,1,0:T(8,128)(2,1)S(1)} %all-to-all-done.refs_0_.kv_ref), channel_id=1, source_target_pairs={{0,8},{8,0},{16,24},{24,16},{32,40},{40,32},{48,56},{56,48},{64,72... | collective-permute-start | bytes 1769480 | tf_op jit(solution)/shard_map/ppermute | solution.py:330
  44.5 0.0 copy-done.1
  44.5 0.0 copy-done.2
  44.5 0.0 copy-done.3
  44.5 0.0 copy-done
  44.6 6.1 %scores.2 = (bf16[1024,2048]{1,0:T(8,128)(2,1)}, f32[4,8,512]{2,1,0:T(8,128)}) custom-call(bf16[8,144,256]{2,1,0:T(8,128)(2,1)} %copy-done, bf16[144,512]{1,0:T(8,128)(2,1)} %get-tuple-element.31.refs_1_.rest_0_, bf16[144,512]{1,0:T(8,128)(2,1)} %copy-done.2, bf16[144,512]{1,0:T(8,128)(2,1)} %copy-done.1, bf16[144,512]{1,0:T(8,128)(2,1)} %copy-done.3), custom_call_target="tpu_custom_call" | custom-call | flops 2097152 | bytes 65536 | tf_op jit(solution)/shard_map/scores/pallas_call | solution.py:264
  50.6 0.0 collective-permute-done.6.refs_0_.kv_ref
  50.6 0.0 copy-start.4
  50.6 0.8 copy-done.4
  51.5 6.3 %scores.3 = (bf16[1024,2048]{1,0:T(8,128)(2,1)}, f32[4,8,512]{2,1,0:T(8,128)}, f32[4,8,512]{2,1,0:T(8,128)}) custom-call(bf16[8,144,256]{2,1,0:T(8,128)(2,1)} %copy-done.4, bf16[144,512]{1,0:T(8,128)(2,1)} %get-tuple-element.31.refs_1_.rest_0_, bf16[144,512]{1,0:T(8,128)(2,1)} %copy-done.2, bf16[144,512]{1,0:T(8,128)(2,1)} %copy-done.1, ...), custom_call_target="tpu_custom_call" | custom-call | flops 2097152 | bytes 65536 | tf_op jit(solution)/shard_map/scores/pallas_call | solution.py:264
  57.7 11.1 %all_to_all.15.all_ref = f32[4,8,512]{2,1,0:T(8,128)} all-to-all(f32[4,8,512]{2,1,0:T(8,128)} %get-tuple-element.37), channel_id=1, replica_groups={{0,16,32,48},{8,24,40,56},{64,80,96,112},{72,88,104,120},{128,144,160,1..., dimensions={0} | all-to-all | bytes 131072 | tf_op jit(solution)/shard_map/all_to_all | solution.py:333
  68.8 0.0 copy-done.5
  68.8 0.0 copy-done.6
  68.8 0.0 copy-done.7
  68.8 8.6 %grads.2 = (bf16[8,128,256]{2,1,0:T(8,128)(2,1)}, f32[4,128,512]{2,1,0:T(8,128)}) custom-call(bf16[8,144,256]{2,1,0:T(8,128)(2,1)} %copy-done.4, bf16[1024,2048]{1,0:T(8,128)(2,1)} %get-tuple-element.42.pt_ref, f32[4,8,512]{2,1,0:T(8,128)} %get-tuple-element.43.st_ref, f32[4,8,512]{2,1,0:T(8,128)} %all_to_all.15.all_ref, ...), custom_call_target="tpu_custom_call" | custom-call | flops 4294967296 | bytes 4194304 | tf_op jit(solution)/shard_map/grads/pallas_call | solution.py:307
  77.4 3.3 %collective-permute-start.10 = (bf16[8,128,256]{2,1,0:T(8,128)(2,1)}, bf16[8,128,256]{2,1,0:T(8,128)(2,1)S(1)}, u32[]{:S(2)}, u32[]{:S(2)}) collective-permute-start(bf16[8,128,256]{2,1,0:T(8,128)(2,1)} %get-tuple-element.50), channel_id=1, source_target_pairs={{0,8},{8,0},{16,24},{24,16},{32,40},{40,32},{48,56},{56,48},{64,72... | collective-permute-start | bytes 1572872 | tf_op jit(solution)/shard_map/ppermute | solution.py:330
  80.6 9.2 %grads.3 = (f32[8,128,256]{2,1,0:T(8,128)}, f32[128,512]{1,0:T(8,128)}, bf16[128,512]{1,0:T(8,128)(2,1)}, bf16[128,512]{1,0:T(8,128)(2,1)}, bf16[128,512]{1,0:T(8,128)(2,1)}) custom-call(bf16[8,144,256]{2,1,0:T(8,128)(2,1)} %copy-done, bf16[1024,2048]{1,0:T(8,128)(2,1)} %get-tuple-element.35.pt_ref, f32[4,8,512]{2,1,0:T(8,128)} %get-tuple-element.36.refs_6_.st_ref, ...), custom_call_target="tpu_custom_call" | custom-call | flops 4294967296 | bytes 4194304 | tf_op jit(solution)/shard_map/grads/pallas_call | solution.py:307
  89.8 0.0 collective-permute-done.10
  89.8 2.1 %add_convert_fusion = bf16[8,128,256]{2,1,0:T(8,128)(2,1)} fusion(f32[8,128,256]{2,1,0:T(8,128)} %get-tuple-element.49, bf16[8,128,256]{2,1,0:T(8,128)(2,1)S(1)} %collective-permute-done.10), kind=kLoop, calls=%fused_computation | loop fusion | flops 786432 | bytes 2097152 | tf_op jit(solution)/shard_map/convert_element_type | solution.py:352
  92.0 6.6 %all-to-all-start.2 = ((bf16[8,128,256]{2,1,0:T(8,128)(2,1)}), bf16[8,128,256]{2,1,0:T(8,128)(2,1)S(1)}, u32[]{:S(2)}, u32[]{:S(2)}) async-start(bf16[8,128,256]{2,1,0:T(8,128)(2,1)} %add_convert_fusion), calls=%async_computation.2 | async-start | bytes 1048576 | tf_op jit(solution)/shard_map/all_to_all | solution.py:333
  98.5 2.5 %collective-permute-start.7 = (bf16[128,512]{1,0:T(8,128)(2,1)}, bf16[128,512]{1,0:T(8,128)(2,1)S(1)}, u32[]{:S(2)}, u32[]{:S(2)}) collective-permute-start(bf16[128,512]{1,0:T(8,128)(2,1)} %get-tuple-element.46), channel_id=1, source_target_pairs={{0,16},{8,24},{16,0},{24,8},{32,48},{40,56},{48,32},{56,40},{64,80... | collective-permute-start | bytes 393224 | tf_op jit(solution)/shard_map/ppermute | solution.py:330
  101.1 2.2 %collective-permute-start.8 = (bf16[128,512]{1,0:T(8,128)(2,1)}, bf16[128,512]{1,0:T(8,128)(2,1)S(1)}, u32[]{:S(2)}, u32[]{:S(2)}) collective-permute-start(bf16[128,512]{1,0:T(8,128)(2,1)} %get-tuple-element.47), channel_id=1, source_target_pairs={{0,32},{8,40},{16,48},{24,56},{32,0},{40,8},{48,16},{56,24},{64,96... | collective-permute-start | bytes 393224 | tf_op jit(solution)/shard_map/ppermute | solution.py:330
  103.3 4.5 %collective-permute-start.9 = (bf16[128,512]{1,0:T(8,128)(2,1)}, bf16[128,512]{1,0:T(8,128)(2,1)S(1)}, u32[]{:S(2)}, u32[]{:S(2)}) collective-permute-start(bf16[128,512]{1,0:T(8,128)(2,1)} %get-tuple-element.48), channel_id=1, source_target_pairs={{0,48},{8,56},{16,32},{24,40},{32,16},{40,24},{48,0},{56,8},{64,11... | collective-permute-start | bytes 393224 | tf_op jit(solution)/shard_map/ppermute | solution.py:330
  107.8 0.0 collective-permute-done.7
  107.8 6.7 %collective-permute-done.8 = bf16[128,512]{1,0:T(8,128)(2,1)S(1)} collective-permute-done((bf16[128,512]{1,0:T(8,128)(2,1)}, bf16[128,512]{1,0:T(8,128)(2,1)S(1)}, u32[]{:S(2)}, u32[]{:S(2)}) %collective-permute-start.8) | collective-permute-done | bytes 131104 | tf_op jit(solution)/shard_map/ppermute | solution.py:330
  114.6 0.0 collective-permute-done.9
  114.6 1.7 %add_convert_fusion.1 = bf16[128,512]{1,0:T(8,128)(2,1)} fusion(f32[128,512]{1,0:T(8,128)} %get-tuple-element.45, bf16[128,512]{1,0:T(8,128)(2,1)S(1)} %collective-permute-done.9, bf16[128,512]{1,0:T(8,128)(2,1)S(1)} %collective-permute-done.8, bf16[128,512]{1,0:T(8,128)(2,1)S(1)} %collective-permute-done.7), kind=kLoop, calls=%fused_computation.1 | loop fusion | flops 458752 | bytes 786432 | tf_op jit(solution)/shard_map/convert_element_type | solution.py:357
  116.2 0.3 all-to-all-done.2
  116.6 0.1 reduce_sum.12
  116.6 0.6 fusion
Async XLA Ops:
  3.1 38.1 %all-to-all-start = ((bf16[8,144,256]{2,1,0:T(8,128)(2,1)}), bf16[8,144,256]{2,1,0:T(8,128)(2,1)S(1)}, u32[]{:S(2)}, u32[]{:S(2)}) async-start(bf16[8,144,256]{2,1,0:T(8,128)(2,1)} %get-tuple-element.27), calls=%async_computation | async-start | bytes 1179648 | tf_op jit(solution)/shard_map/all_to_all | solution.py:333
  14.0 11.5 %collective-permute-start.1 = (bf16[144,512]{1,0:T(8,128)(2,1)}, bf16[144,512]{1,0:T(8,128)(2,1)S(1)}, u32[]{:S(2)}, u32[]{:S(2)}) collective-permute-start(bf16[144,512]{1,0:T(8,128)(2,1)} %get-tuple-element.31.refs_1_.rest_0_), channel_id=1, source_target_pairs={{0,32},{8,40},{16,48},{24,56},{32,0},{40,8},{48,16},{56,24},{64,96... | collective-permute-start | bytes 442376 | tf_op jit(solution)/shard_map/ppermute | solution.py:330
  18.2 13.3 %collective-permute-start.4 = (bf16[144,512]{1,0:T(8,128)(2,1)}, bf16[144,512]{1,0:T(8,128)(2,1)S(1)}, u32[]{:S(2)}, u32[]{:S(2)}) collective-permute-start(bf16[144,512]{1,0:T(8,128)(2,1)} %get-tuple-element.38.rest_4_), channel_id=1, source_target_pairs={{0,32},{8,40},{16,48},{24,56},{32,0},{40,8},{48,16},{56,24},{64,96... | collective-permute-start | bytes 442376 | tf_op jit(solution)/shard_map/ppermute | solution.py:330
  20.2 14.5 %collective-permute-start = (bf16[144,512]{1,0:T(8,128)(2,1)}, bf16[144,512]{1,0:T(8,128)(2,1)S(1)}, u32[]{:S(2)}, u32[]{:S(2)}) collective-permute-start(bf16[144,512]{1,0:T(8,128)(2,1)} %get-tuple-element.31.refs_1_.rest_0_), channel_id=1, source_target_pairs={{0,16},{8,24},{16,0},{24,8},{32,48},{40,56},{48,32},{56,40},{64,80... | collective-permute-start | bytes 442376 | tf_op jit(solution)/shard_map/ppermute | solution.py:330
  23.4 11.5 %collective-permute-start.3 = (bf16[144,512]{1,0:T(8,128)(2,1)}, bf16[144,512]{1,0:T(8,128)(2,1)S(1)}, u32[]{:S(2)}, u32[]{:S(2)}) collective-permute-start(bf16[144,512]{1,0:T(8,128)(2,1)} %get-tuple-element.38.rest_4_), channel_id=1, source_target_pairs={{0,16},{8,24},{16,0},{24,8},{32,48},{40,56},{48,32},{56,40},{64,80... | collective-permute-start | bytes 442376 | tf_op jit(solution)/shard_map/ppermute | solution.py:330
  25.5 19.0 %copy-start.1 = (bf16[144,512]{1,0:T(8,128)(2,1)}, bf16[144,512]{1,0:T(8,128)(2,1)S(1)}, u32[]{:S(2)}) copy-start(bf16[144,512]{1,0:T(8,128)(2,1)S(1)} %collective-permute-done.1.refs_3_.rest_2_) | copy-start | bytes 442372
  25.5 12.5 %collective-permute-start.2 = (bf16[144,512]{1,0:T(8,128)(2,1)S(1)}, bf16[144,512]{1,0:T(8,128)(2,1)S(1)}, u32[]{:S(2)}, u32[]{:S(2)}) collective-permute-start(bf16[144,512]{1,0:T(8,128)(2,1)S(1)} %collective-permute-done.1.refs_3_.rest_2_), channel_id=1, source_target_pairs={{0,16},{8,24},{16,0},{24,8},{32,48},{40,56},{48,32},{56,40},{64,80... | collective-permute-start | bytes 442376 | tf_op jit(solution)/shard_map/ppermute | solution.py:330
  31.6 37.3 %copy-start.5 = (bf16[144,512]{1,0:T(8,128)(2,1)}, bf16[144,512]{1,0:T(8,128)(2,1)S(1)}, u32[]{:S(2)}) copy-start(bf16[144,512]{1,0:T(8,128)(2,1)S(1)} %collective-permute-done.4.rest_6_) | copy-start | bytes 442372
  31.6 9.7 %collective-permute-start.5 = (bf16[144,512]{1,0:T(8,128)(2,1)S(1)}, bf16[144,512]{1,0:T(8,128)(2,1)S(1)}, u32[]{:S(2)}, u32[]{:S(2)}) collective-permute-start(bf16[144,512]{1,0:T(8,128)(2,1)S(1)} %collective-permute-done.4.rest_6_), channel_id=1, source_target_pairs={{0,16},{8,24},{16,0},{24,8},{32,48},{40,56},{48,32},{56,40},{64,80... | collective-permute-start | bytes 442376 | tf_op jit(solution)/shard_map/ppermute | solution.py:330
  34.7 9.8 %copy-start.2 = (bf16[144,512]{1,0:T(8,128)(2,1)}, bf16[144,512]{1,0:T(8,128)(2,1)S(1)}, u32[]{:S(2)}) copy-start(bf16[144,512]{1,0:T(8,128)(2,1)S(1)} %collective-permute-done.refs_2_.rest_1_) | copy-start | bytes 442372
  34.9 33.9 %copy-start.6 = (bf16[144,512]{1,0:T(8,128)(2,1)}, bf16[144,512]{1,0:T(8,128)(2,1)S(1)}, u32[]{:S(2)}) copy-start(bf16[144,512]{1,0:T(8,128)(2,1)S(1)} %collective-permute-done.3.rest_5_) | copy-start | bytes 442372
  38.1 6.5 %copy-start.3 = (bf16[144,512]{1,0:T(8,128)(2,1)}, bf16[144,512]{1,0:T(8,128)(2,1)S(1)}, u32[]{:S(2)}) copy-start(bf16[144,512]{1,0:T(8,128)(2,1)S(1)} %collective-permute-done.2.refs_4_.rest_3_) | copy-start | bytes 442372
  41.2 27.6 %copy-start.7 = (bf16[144,512]{1,0:T(8,128)(2,1)}, bf16[144,512]{1,0:T(8,128)(2,1)S(1)}, u32[]{:S(2)}) copy-start(bf16[144,512]{1,0:T(8,128)(2,1)S(1)} %collective-permute-done.5.rest_7_) | copy-start | bytes 442372
  41.2 3.3 %copy-start = (bf16[8,144,256]{2,1,0:T(8,128)(2,1)}, bf16[8,144,256]{2,1,0:T(8,128)(2,1)S(1)}, u32[]{:S(2)}) copy-start(bf16[8,144,256]{2,1,0:T(8,128)(2,1)S(1)} %all-to-all-done.refs_0_.kv_ref) | copy-start | bytes 1769476
  41.2 9.4 %collective-permute-start.6 = (bf16[8,144,256]{2,1,0:T(8,128)(2,1)S(1)}, bf16[8,144,256]{2,1,0:T(8,128)(2,1)S(1)}, u32[]{:S(2)}, u32[]{:S(2)}) collective-permute-start(bf16[8,144,256]{2,1,0:T(8,128)(2,1)S(1)} %all-to-all-done.refs_0_.kv_ref), channel_id=1, source_target_pairs={{0,8},{8,0},{16,24},{24,16},{32,40},{40,32},{48,56},{56,48},{64,72... | collective-permute-start | bytes 1769480 | tf_op jit(solution)/shard_map/ppermute | solution.py:330
  50.6 0.8 copy-start.4
  77.4 12.4 %collective-permute-start.10 = (bf16[8,128,256]{2,1,0:T(8,128)(2,1)}, bf16[8,128,256]{2,1,0:T(8,128)(2,1)S(1)}, u32[]{:S(2)}, u32[]{:S(2)}) collective-permute-start(bf16[8,128,256]{2,1,0:T(8,128)(2,1)} %get-tuple-element.50), channel_id=1, source_target_pairs={{0,8},{8,0},{16,24},{24,16},{32,40},{40,32},{48,56},{56,48},{64,72... | collective-permute-start | bytes 1572872 | tf_op jit(solution)/shard_map/ppermute | solution.py:330
  92.0 24.6 %all-to-all-start.2 = ((bf16[8,128,256]{2,1,0:T(8,128)(2,1)}), bf16[8,128,256]{2,1,0:T(8,128)(2,1)S(1)}, u32[]{:S(2)}, u32[]{:S(2)}) async-start(bf16[8,128,256]{2,1,0:T(8,128)(2,1)} %add_convert_fusion), calls=%async_computation.2 | async-start | bytes 1048576 | tf_op jit(solution)/shard_map/all_to_all | solution.py:333
  98.5 9.3 %collective-permute-start.7 = (bf16[128,512]{1,0:T(8,128)(2,1)}, bf16[128,512]{1,0:T(8,128)(2,1)S(1)}, u32[]{:S(2)}, u32[]{:S(2)}) collective-permute-start(bf16[128,512]{1,0:T(8,128)(2,1)} %get-tuple-element.46), channel_id=1, source_target_pairs={{0,16},{8,24},{16,0},{24,8},{32,48},{40,56},{48,32},{56,40},{64,80... | collective-permute-start | bytes 393224 | tf_op jit(solution)/shard_map/ppermute | solution.py:330
  101.1 13.5 %collective-permute-start.8 = (bf16[128,512]{1,0:T(8,128)(2,1)}, bf16[128,512]{1,0:T(8,128)(2,1)S(1)}, u32[]{:S(2)}, u32[]{:S(2)}) collective-permute-start(bf16[128,512]{1,0:T(8,128)(2,1)} %get-tuple-element.47), channel_id=1, source_target_pairs={{0,32},{8,40},{16,48},{24,56},{32,0},{40,8},{48,16},{56,24},{64,96... | collective-permute-start | bytes 393224 | tf_op jit(solution)/shard_map/ppermute | solution.py:330
  103.3 11.3 %collective-permute-start.9 = (bf16[128,512]{1,0:T(8,128)(2,1)}, bf16[128,512]{1,0:T(8,128)(2,1)S(1)}, u32[]{:S(2)}, u32[]{:S(2)}) collective-permute-start(bf16[128,512]{1,0:T(8,128)(2,1)} %get-tuple-element.48), channel_id=1, source_target_pairs={{0,48},{8,56},{16,32},{24,40},{32,16},{40,24},{48,0},{56,8},{64,11... | collective-permute-start | bytes 393224 | tf_op jit(solution)/shard_map/ppermute | solution.py:330

commit v3 on v2

--- a/solution.py
+++ b/solution.py
@@ -26,7 +26,7 @@
 FLOOR = -1e25
 F32 = jnp.float32
 BF16 = jnp.bfloat16
-VMEM_LIMIT = 57
+VMEM_LIMIT = 24
 
 NT = (((1,), (1,)), ((), ()))
 TN = (((0,), (0,)), ((), ()))

time: 119 us -> 106 us (0.89)
  Pallas kernels: 32.6 us -> 20.8 us
  other arithmetic: 3.89 us -> 1.71 us
    pallas_call x2, Pallas kernels: 17.7 us -> 11.2 us  [grads(): pl.pallas_call(functools.partial(grad_kernel, last), grid=(STEPS,), in_sp...]
    pallas_call x2, Pallas kernels: 12.3 us -> 7.2 us  [scores(): pl.pallas_call(functools.partial(score_kernel, 0 if prev is None else STE...]
    convert_element_type x1, other arithmetic: 2.15 us -> 0.92 us  [per_device(): dkv = (dkv_own + dkv_back.astype(F32)).astype(BF16)]
  transfers between devices with their start and end apart: 13 -> 13, of which waited for: 5 -> 5; matrix products, arithmetic and copies ran while one was open for 1% -> 1% of each run, Pallas kernels for 13% -> 9%
where the time goes in v3:
time: 106 us; the launch traced here: 105 us
  starting transfers between devices  53.8 us (51%)
  Pallas kernels  20.8 us (20%)
  waiting for transfers between devices  14.5 us (14%)
  blocking collectives  10.8 us (10%)
  local copies, waits for them, and re-layouts  2.44 us (2%)
  other arithmetic  1.71 us (2%)
    ppermute x11, starting transfers between devices, swap(): return lax.ppermute(x, 'ctx', [(i, i ^ bits) for i in range(n)])  36.4 us
    all_to_all x2, starting transfers between devices, exchange(): return lax.all_to_all(x, 'ctx', 0, 0, tiled=True, axis_index_groups=groups)  17.5 us
    ppermute x11, waiting for transfers between devices, swap(): return lax.ppermute(x, 'ctx', [(i, i ^ bits) for i in range(n)])  13 us
    pallas_call x2, Pallas kernels, grads(): pl.pallas_call(functools.partial(grad_kernel, last), grid=(STEPS,), in_sp...  11.2 us
    all_to_all x1, blocking collectives, exchange(): return lax.all_to_all(x, 'ctx', 0, 0, tiled=True, axis_index_groups=groups)  10.8 us
    pallas_call x2, Pallas kernels, scores(): pl.pallas_call(functools.partial(score_kernel, 0 if prev is None else STE...  7.2 us
    pallas_call x1, Pallas kernels, pack(): pl.pallas_call(pack_kernel, out_shape=(shape_of((ZS, PAY, 2 * HD), BF16),...  2.46 us
  transfers between devices with their start and end apart: 13, of which 5 were waited for; matrix products, arithmetic and copies ran while one was open for 1% of the time, Pallas kernels for 9%

profile of v3, /device:TPU:1, one launch (start us, length us, event | category | flops | bytes accessed | tf_op | source)
XLA Modules:
  0.0 105.0 jit_solution(9581958223375937469)
XLA Ops:
  0.6 2.5 %pack.1 = (bf16[8,144,256]{2,1,0:T(8,128)(2,1)}, bf16[144,512]{1,0:T(8,128)(2,1)}, bf16[144,512]{1,0:T(8,128)(2,1)}) custom-call(s32[2]{0:T(128)} %order_hbm.1, s32[1,128]{1,0:T(1,128)} %bitcast.2, bf16[128,512]{1,0:T(8,128)(2,1)} %q_hbm.1, bf16[128,128]{1,0:T(8,128)(2,1)} %k_hbm.1, bf16[128,128]{1,0:T(8,128)(2,1)} %v_hbm.1, bf16[128,512]{1,0:T(8,128)(2,1)} %o_hbm.1, ...), custom_call_target="tpu_custom_call" | custom-call | tf_op jit(solution)/shard_map/pack/pallas_call | solution.py:219
  3.1 10.9 %all-to-all-start = ((bf16[8,144,256]{2,1,0:T(8,128)(2,1)}), bf16[8,144,256]{2,1,0:T(8,128)(2,1)S(1)}, u32[]{:S(2)}, u32[]{:S(2)}) async-start(bf16[8,144,256]{2,1,0:T(8,128)(2,1)} %get-tuple-element.27), calls=%async_computation | async-start | bytes 1179648 | tf_op jit(solution)/shard_map/all_to_all | solution.py:333
  14.0 4.2 %collective-permute-start.1 = (bf16[144,512]{1,0:T(8,128)(2,1)}, bf16[144,512]{1,0:T(8,128)(2,1)S(1)}, u32[]{:S(2)}, u32[]{:S(2)}) collective-permute-start(bf16[144,512]{1,0:T(8,128)(2,1)} %get-tuple-element.31.refs_1_.rest_0_), channel_id=1, source_target_pairs={{0,32},{8,40},{16,48},{24,56},{32,0},{40,8},{48,16},{56,24},{64,96... | collective-permute-start | bytes 442376 | tf_op jit(solution)/shard_map/ppermute | solution.py:330
  18.2 2.0 %collective-permute-start.4 = (bf16[144,512]{1,0:T(8,128)(2,1)}, bf16[144,512]{1,0:T(8,128)(2,1)S(1)}, u32[]{:S(2)}, u32[]{:S(2)}) collective-permute-start(bf16[144,512]{1,0:T(8,128)(2,1)} %get-tuple-element.38.rest_4_), channel_id=1, source_target_pairs={{0,32},{8,40},{16,48},{24,56},{32,0},{40,8},{48,16},{56,24},{64,96... | collective-permute-start | bytes 442376 | tf_op jit(solution)/shard_map/ppermute | solution.py:330
  20.2 3.2 %collective-permute-start = (bf16[144,512]{1,0:T(8,128)(2,1)}, bf16[144,512]{1,0:T(8,128)(2,1)S(1)}, u32[]{:S(2)}, u32[]{:S(2)}) collective-permute-start(bf16[144,512]{1,0:T(8,128)(2,1)} %get-tuple-element.31.refs_1_.rest_0_), channel_id=1, source_target_pairs={{0,16},{8,24},{16,0},{24,8},{32,48},{40,56},{48,32},{56,40},{64,80... | collective-permute-start | bytes 442376 | tf_op jit(solution)/shard_map/ppermute | solution.py:330
  23.4 2.1 %collective-permute-start.3 = (bf16[144,512]{1,0:T(8,128)(2,1)}, bf16[144,512]{1,0:T(8,128)(2,1)S(1)}, u32[]{:S(2)}, u32[]{:S(2)}) collective-permute-start(bf16[144,512]{1,0:T(8,128)(2,1)} %get-tuple-element.38.rest_4_), channel_id=1, source_target_pairs={{0,16},{8,24},{16,0},{24,8},{32,48},{40,56},{48,32},{56,40},{64,80... | collective-permute-start | bytes 442376 | tf_op jit(solution)/shard_map/ppermute | solution.py:330
  25.5 0.0 collective-permute-done.1.refs_3_.rest_2_
  25.5 6.0 %collective-permute-start.2 = (bf16[144,512]{1,0:T(8,128)(2,1)S(1)}, bf16[144,512]{1,0:T(8,128)(2,1)S(1)}, u32[]{:S(2)}, u32[]{:S(2)}) collective-permute-start(bf16[144,512]{1,0:T(8,128)(2,1)S(1)} %collective-permute-done.1.refs_3_.rest_2_), channel_id=1, source_target_pairs={{0,16},{8,24},{16,0},{24,8},{32,48},{40,56},{48,32},{56,40},{64,80... | collective-permute-start | bytes 442376 | tf_op jit(solution)/shard_map/ppermute | solution.py:330
  31.5 0.0 collective-permute-done.4.rest_6_
  31.5 3.1 %collective-permute-start.5 = (bf16[144,512]{1,0:T(8,128)(2,1)S(1)}, bf16[144,512]{1,0:T(8,128)(2,1)S(1)}, u32[]{:S(2)}, u32[]{:S(2)}) collective-permute-start(bf16[144,512]{1,0:T(8,128)(2,1)S(1)} %collective-permute-done.4.rest_6_), channel_id=1, source_target_pairs={{0,16},{8,24},{16,0},{24,8},{32,48},{40,56},{48,32},{56,40},{64,80... | collective-permute-start | bytes 442376 | tf_op jit(solution)/shard_map/ppermute | solution.py:330
  34.7 0.0 collective-permute-done.refs_2_.rest_1_
  34.7 0.2 collective-permute-done.3.rest_5_
  34.9 3.2 %collective-permute-done.2.refs_4_.rest_3_ = bf16[144,512]{1,0:T(8,128)(2,1)S(1)} collective-permute-done((bf16[144,512]{1,0:T(8,128)(2,1)S(1)}, bf16[144,512]{1,0:T(8,128)(2,1)S(1)}, u32[]{:S(2)}, u32[]{:S(2)}) %collective-permute-start.2) | collective-permute-done | bytes 147488 | tf_op jit(solution)/shard_map/ppermute | solution.py:330
  38.0 3.2 %collective-permute-done.5.rest_7_ = bf16[144,512]{1,0:T(8,128)(2,1)S(1)} collective-permute-done((bf16[144,512]{1,0:T(8,128)(2,1)S(1)}, bf16[144,512]{1,0:T(8,128)(2,1)S(1)}, u32[]{:S(2)}, u32[]{:S(2)}) %collective-permute-start.5) | collective-permute-done | bytes 147488 | tf_op jit(solution)/shard_map/ppermute | solution.py:330
  41.2 0.0 all-to-all-done.refs_0_.kv_ref
  41.2 3.2 %collective-permute-start.6 = (bf16[8,144,256]{2,1,0:T(8,128)(2,1)S(1)}, bf16[8,144,256]{2,1,0:T(8,128)(2,1)S(1)}, u32[]{:S(2)}, u32[]{:S(2)}) collective-permute-start(bf16[8,144,256]{2,1,0:T(8,128)(2,1)S(1)} %all-to-all-done.refs_0_.kv_ref), channel_id=1, source_target_pairs={{0,8},{8,0},{16,24},{24,16},{32,40},{40,32},{48,56},{56,48},{64,72... | collective-permute-start | bytes 1769480 | tf_op jit(solution)/shard_map/ppermute | solution.py:330
  44.5 0.0 copy-start
  44.5 0.9 copy-done
  45.4 3.5 %scores.2 = (bf16[1024,2048]{1,0:T(8,128)(2,1)S(1)}, f32[4,8,512]{2,1,0:T(8,128)S(1)}) custom-call(bf16[8,144,256]{2,1,0:T(8,128)(2,1)S(1)} %all-to-all-done.refs_0_.kv_ref, bf16[144,512]{1,0:T(8,128)(2,1)S(1)} %copy-done, bf16[144,512]{1,0:T(8,128)(2,1)S(1)} %collective-permute-done.refs_2_.rest_1_, ...), custom_call_target="tpu_custom_call" | custom-call | flops 2097152 | bytes 65536 | tf_op jit(solution)/shard_map/scores/pallas_call | solution.py:264
  48.9 0.0 collective-permute-done.6.refs_0_.kv_ref
  49.0 3.6 %scores.3 = (bf16[1024,2048]{1,0:T(8,128)(2,1)S(1)}, f32[4,8,512]{2,1,0:T(8,128)S(1)}, f32[4,8,512]{2,1,0:T(8,128)S(1)}) custom-call(bf16[8,144,256]{2,1,0:T(8,128)(2,1)S(1)} %collective-permute-done.6.refs_0_.kv_ref, bf16[144,512]{1,0:T(8,128)(2,1)S(1)} %copy-done, bf16[144,512]{1,0:T(8,128)(2,1)S(1)} %collective-permute-done.refs_2_.rest_1_, ...), custom_call_target="tpu_custom_call" | custom-call | flops 2097152 | bytes 65536 | tf_op jit(solution)/shard_map/scores/pallas_call | solution.py:264
  52.6 10.8 %all_to_all.15.all_ref = f32[4,8,512]{2,1,0:T(8,128)S(1)} all-to-all(f32[4,8,512]{2,1,0:T(8,128)S(1)} %get-tuple-element.37), channel_id=1, replica_groups={{0,16,32,48},{8,24,40,56},{64,80,96,112},{72,88,104,120},{128,144,160,1..., dimensions={0} | all-to-all | bytes 131072 | tf_op jit(solution)/shard_map/all_to_all | solution.py:333
  63.4 0.0 copy-start.1
  63.4 0.9 copy-done.1
  64.3 5.4 %grads.2 = (bf16[8,128,256]{2,1,0:T(8,128)(2,1)S(1)}, f32[4,128,512]{2,1,0:T(8,128)S(1)}) custom-call(bf16[8,144,256]{2,1,0:T(8,128)(2,1)S(1)} %collective-permute-done.6.refs_0_.kv_ref, bf16[1024,2048]{1,0:T(8,128)(2,1)S(1)} %get-tuple-element.42.pt_ref, f32[4,8,512]{2,1,0:T(8,128)S(1)} %get-tuple-element.43.st_ref, f32[4,8,512]{2,1,0:T(8,128)S(1)} %all_to_all.15.all_ref, ...), custom_call_target="tpu_custom_call" | custom-call | flops 4294967296 | bytes 4194304 | tf_op jit(solution)/shard_map/grads/pallas_call | solution.py:307
  69.7 3.2 %collective-permute-start.10 = (bf16[8,128,256]{2,1,0:T(8,128)(2,1)S(1)}, bf16[8,128,256]{2,1,0:T(8,128)(2,1)S(1)}, u32[]{:S(2)}, u32[]{:S(2)}) collective-permute-start(bf16[8,128,256]{2,1,0:T(8,128)(2,1)S(1)} %get-tuple-element.50), channel_id=1, source_target_pairs={{0,8},{8,0},{16,24},{24,16},{32,40},{40,32},{48,56},{56,48},{64,72... | collective-permute-start | bytes 1572872 | tf_op jit(solution)/shard_map/ppermute | solution.py:330
  72.9 5.8 %grads.3 = (f32[8,128,256]{2,1,0:T(8,128)S(1)}, f32[128,512]{1,0:T(8,128)S(1)}, bf16[128,512]{1,0:T(8,128)(2,1)S(1)}, bf16[128,512]{1,0:T(8,128)(2,1)S(1)}, bf16[128,512]{1,0:T(8,128)(2,1)S(1)}) custom-call(bf16[8,144,256]{2,1,0:T(8,128)(2,1)S(1)} %all-to-all-done.refs_0_.kv_ref, bf16[1024,2048]{1,0:T(8,128)(2,1)S(1)} %get-tuple-element.35.pt_ref, ...), custom_call_target="tpu_custom_call" | custom-call | flops 4294967296 | bytes 4194304 | tf_op jit(solution)/shard_map/grads/pallas_call | solution.py:307
  78.7 0.0 collective-permute-done.10
  78.7 0.9 add_convert_fusion
  79.7 6.6 %all-to-all-start.2 = ((bf16[8,128,256]{2,1,0:T(8,128)(2,1)}), bf16[8,128,256]{2,1,0:T(8,128)(2,1)S(1)}, u32[]{:S(2)}, u32[]{:S(2)}) async-start(bf16[8,128,256]{2,1,0:T(8,128)(2,1)} %add_convert_fusion), calls=%async_computation.2 | async-start | bytes 1048576 | tf_op jit(solution)/shard_map/all_to_all | solution.py:333
  86.2 2.5 %collective-permute-start.7 = (bf16[128,512]{1,0:T(8,128)(2,1)S(1)}, bf16[128,512]{1,0:T(8,128)(2,1)S(1)}, u32[]{:S(2)}, u32[]{:S(2)}) collective-permute-start(bf16[128,512]{1,0:T(8,128)(2,1)S(1)} %get-tuple-element.46), channel_id=1, source_target_pairs={{0,16},{8,24},{16,0},{24,8},{32,48},{40,56},{48,32},{56,40},{64,80... | collective-permute-start | bytes 393224 | tf_op jit(solution)/shard_map/ppermute | solution.py:330
  88.8 2.2 %collective-permute-start.8 = (bf16[128,512]{1,0:T(8,128)(2,1)S(1)}, bf16[128,512]{1,0:T(8,128)(2,1)S(1)}, u32[]{:S(2)}, u32[]{:S(2)}) collective-permute-start(bf16[128,512]{1,0:T(8,128)(2,1)S(1)} %get-tuple-element.47), channel_id=1, source_target_pairs={{0,32},{8,40},{16,48},{24,56},{32,0},{40,8},{48,16},{56,24},{64,96... | collective-permute-start | bytes 393224 | tf_op jit(solution)/shard_map/ppermute | solution.py:330
  91.0 4.5 %collective-permute-start.9 = (bf16[128,512]{1,0:T(8,128)(2,1)S(1)}, bf16[128,512]{1,0:T(8,128)(2,1)S(1)}, u32[]{:S(2)}, u32[]{:S(2)}) collective-permute-start(bf16[128,512]{1,0:T(8,128)(2,1)S(1)} %get-tuple-element.48), channel_id=1, source_target_pairs={{0,48},{8,56},{16,32},{24,40},{32,16},{40,24},{48,0},{56,8},{64,11... | collective-permute-start | bytes 393224 | tf_op jit(solution)/shard_map/ppermute | solution.py:330
  95.5 0.0 collective-permute-done.7
  95.5 6.5 %collective-permute-done.8 = bf16[128,512]{1,0:T(8,128)(2,1)S(1)} collective-permute-done((bf16[128,512]{1,0:T(8,128)(2,1)S(1)}, bf16[128,512]{1,0:T(8,128)(2,1)S(1)}, u32[]{:S(2)}, u32[]{:S(2)}) %collective-permute-start.8) | collective-permute-done | bytes 131104 | tf_op jit(solution)/shard_map/ppermute | solution.py:330
  102.0 0.0 collective-permute-done.9
  102.0 0.7 add_convert_fusion.1
  102.8 1.5 %all-to-all-done.2 = bf16[8,128,256]{2,1,0:T(8,128)(2,1)S(1)} async-done(((bf16[8,128,256]{2,1,0:T(8,128)(2,1)}), bf16[8,128,256]{2,1,0:T(8,128)(2,1)S(1)}, u32[]{:S(2)}, u32[]{:S(2)}) %all-to-all-start.2) | async-done | bytes 524320 | tf_op jit(solution)/shard_map/all_to_all | solution.py:333
  104.3 0.1 reduce_sum.12
  104.3 0.6 fusion
Async XLA Ops:
  3.1 38.1 %all-to-all-start = ((bf16[8,144,256]{2,1,0:T(8,128)(2,1)}), bf16[8,144,256]{2,1,0:T(8,128)(2,1)S(1)}, u32[]{:S(2)}, u32[]{:S(2)}) async-start(bf16[8,144,256]{2,1,0:T(8,128)(2,1)} %get-tuple-element.27), calls=%async_computation | async-start | bytes 1179648 | tf_op jit(solution)/shard_map/all_to_all | solution.py:333
  14.0 11.5 %collective-permute-start.1 = (bf16[144,512]{1,0:T(8,128)(2,1)}, bf16[144,512]{1,0:T(8,128)(2,1)S(1)}, u32[]{:S(2)}, u32[]{:S(2)}) collective-permute-start(bf16[144,512]{1,0:T(8,128)(2,1)} %get-tuple-element.31.refs_1_.rest_0_), channel_id=1, source_target_pairs={{0,32},{8,40},{16,48},{24,56},{32,0},{40,8},{48,16},{56,24},{64,96... | collective-permute-start | bytes 442376 | tf_op jit(solution)/shard_map/ppermute | solution.py:330
  18.2 13.3 %collective-permute-start.4 = (bf16[144,512]{1,0:T(8,128)(2,1)}, bf16[144,512]{1,0:T(8,128)(2,1)S(1)}, u32[]{:S(2)}, u32[]{:S(2)}) collective-permute-start(bf16[144,512]{1,0:T(8,128)(2,1)} %get-tuple-element.38.rest_4_), channel_id=1, source_target_pairs={{0,32},{8,40},{16,48},{24,56},{32,0},{40,8},{48,16},{56,24},{64,96... | collective-permute-start | bytes 442376 | tf_op jit(solution)/shard_map/ppermute | solution.py:330
  20.2 14.5 %collective-permute-start = (bf16[144,512]{1,0:T(8,128)(2,1)}, bf16[144,512]{1,0:T(8,128)(2,1)S(1)}, u32[]{:S(2)}, u32[]{:S(2)}) collective-permute-start(bf16[144,512]{1,0:T(8,128)(2,1)} %get-tuple-element.31.refs_1_.rest_0_), channel_id=1, source_target_pairs={{0,16},{8,24},{16,0},{24,8},{32,48},{40,56},{48,32},{56,40},{64,80... | collective-permute-start | bytes 442376 | tf_op jit(solution)/shard_map/ppermute | solution.py:330
  23.4 11.5 %collective-permute-start.3 = (bf16[144,512]{1,0:T(8,128)(2,1)}, bf16[144,512]{1,0:T(8,128)(2,1)S(1)}, u32[]{:S(2)}, u32[]{:S(2)}) collective-permute-start(bf16[144,512]{1,0:T(8,128)(2,1)} %get-tuple-element.38.rest_4_), channel_id=1, source_target_pairs={{0,16},{8,24},{16,0},{24,8},{32,48},{40,56},{48,32},{56,40},{64,80... | collective-permute-start | bytes 442376 | tf_op jit(solution)/shard_map/ppermute | solution.py:330
  25.5 12.6 %collective-permute-start.2 = (bf16[144,512]{1,0:T(8,128)(2,1)S(1)}, bf16[144,512]{1,0:T(8,128)(2,1)S(1)}, u32[]{:S(2)}, u32[]{:S(2)}) collective-permute-start(bf16[144,512]{1,0:T(8,128)(2,1)S(1)} %collective-permute-done.1.refs_3_.rest_2_), channel_id=1, source_target_pairs={{0,16},{8,24},{16,0},{24,8},{32,48},{40,56},{48,32},{56,40},{64,80... | collective-permute-start | bytes 442376 | tf_op jit(solution)/shard_map/ppermute | solution.py:330
  31.5 9.7 %collective-permute-start.5 = (bf16[144,512]{1,0:T(8,128)(2,1)S(1)}, bf16[144,512]{1,0:T(8,128)(2,1)S(1)}, u32[]{:S(2)}, u32[]{:S(2)}) collective-permute-start(bf16[144,512]{1,0:T(8,128)(2,1)S(1)} %collective-permute-done.4.rest_6_), channel_id=1, source_target_pairs={{0,16},{8,24},{16,0},{24,8},{32,48},{40,56},{48,32},{56,40},{64,80... | collective-permute-start | bytes 442376 | tf_op jit(solution)/shard_map/ppermute | solution.py:330
  41.2 7.8 %collective-permute-start.6 = (bf16[8,144,256]{2,1,0:T(8,128)(2,1)S(1)}, bf16[8,144,256]{2,1,0:T(8,128)(2,1)S(1)}, u32[]{:S(2)}, u32[]{:S(2)}) collective-permute-start(bf16[8,144,256]{2,1,0:T(8,128)(2,1)S(1)} %all-to-all-done.refs_0_.kv_ref), channel_id=1, source_target_pairs={{0,8},{8,0},{16,24},{24,16},{32,40},{40,32},{48,56},{56,48},{64,72... | collective-permute-start | bytes 1769480 | tf_op jit(solution)/shard_map/ppermute | solution.py:330
  44.5 0.9 copy-start
  63.4 0.9 copy-start.1
  69.7 9.0 %collective-permute-start.10 = (bf16[8,128,256]{2,1,0:T(8,128)(2,1)S(1)}, bf16[8,128,256]{2,1,0:T(8,128)(2,1)S(1)}, u32[]{:S(2)}, u32[]{:S(2)}) collective-permute-start(bf16[8,128,256]{2,1,0:T(8,128)(2,1)S(1)} %get-tuple-element.50), channel_id=1, source_target_pairs={{0,8},{8,0},{16,24},{24,16},{32,40},{40,32},{48,56},{56,48},{64,72... | collective-permute-start | bytes 1572872 | tf_op jit(solution)/shard_map/ppermute | solution.py:330
  79.7 24.6 %all-to-all-start.2 = ((bf16[8,128,256]{2,1,0:T(8,128)(2,1)}), bf16[8,128,256]{2,1,0:T(8,128)(2,1)S(1)}, u32[]{:S(2)}, u32[]{:S(2)}) async-start(bf16[8,128,256]{2,1,0:T(8,128)(2,1)} %add_convert_fusion), calls=%async_computation.2 | async-start | bytes 1048576 | tf_op jit(solution)/shard_map/all_to_all | solution.py:333
  86.2 9.3 %collective-permute-start.7 = (bf16[128,512]{1,0:T(8,128)(2,1)S(1)}, bf16[128,512]{1,0:T(8,128)(2,1)S(1)}, u32[]{:S(2)}, u32[]{:S(2)}) collective-permute-start(bf16[128,512]{1,0:T(8,128)(2,1)S(1)} %get-tuple-element.46), channel_id=1, source_target_pairs={{0,16},{8,24},{16,0},{24,8},{32,48},{40,56},{48,32},{56,40},{64,80... | collective-permute-start | bytes 393224 | tf_op jit(solution)/shard_map/ppermute | solution.py:330
  88.8 13.3 %collective-permute-start.8 = (bf16[128,512]{1,0:T(8,128)(2,1)S(1)}, bf16[128,512]{1,0:T(8,128)(2,1)S(1)}, u32[]{:S(2)}, u32[]{:S(2)}) collective-permute-start(bf16[128,512]{1,0:T(8,128)(2,1)S(1)} %get-tuple-element.47), channel_id=1, source_target_pairs={{0,32},{8,40},{16,48},{24,56},{32,0},{40,8},{48,16},{56,24},{64,96... | collective-permute-start | bytes 393224 | tf_op jit(solution)/shard_map/ppermute | solution.py:330
  91.0 11.1 %collective-permute-start.9 = (bf16[128,512]{1,0:T(8,128)(2,1)S(1)}, bf16[128,512]{1,0:T(8,128)(2,1)S(1)}, u32[]{:S(2)}, u32[]{:S(2)}) collective-permute-start(bf16[128,512]{1,0:T(8,128)(2,1)S(1)} %get-tuple-element.48), channel_id=1, source_target_pairs={{0,48},{8,56},{16,32},{24,40},{32,16},{40,24},{48,0},{56,8},{64,11... | collective-permute-start | bytes 393224 | tf_op jit(solution)/shard_map/ppermute | solution.py:330

commit v4 on v3

v4 whole, which is shorter than its diff:
```python
import functools

import jax
import jax.numpy as jnp
from jax import lax
from jax.experimental import pallas as pl
from jax.experimental.pallas import tpu as pltpu
from jax.sharding import PartitionSpec as P

HEADS = 32
KV_HEADS = 8
HD = 128
GROUP = HEADS // KV_HEADS
BLK = 64
TOKENS = 8192
TOK = 128
EXTRA = 16
PAY = TOK + EXTRA
YS = 4
ZS = 8
QT = YS * TOK
KT = 2 * TOK
SCALE = HD**-0.5
EXP2 = SCALE * 1.4426950408889634
MASKED = -1e30
FLOOR = -1e25
F32 = jnp.float32
BF16 = jnp.bfloat16
VMEM_LIMIT = 24
PAIR_LIMIT = 46

NT = (((1,), (1,)), ((), ()))
TN = (((0,), (0,)), ((), ()))


def dot(a, b, dims=(((1,), (0,)), ((), ()))):
    return lax.dot_general(a, b, dims, preferred_element_type=F32)


def pack_kernel(
    order_hbm, seg_hbm, q_hbm, k_hbm, v_hbm, o_hbm, g_hbm, kvp_hbm, qp_ref, gp_ref,
    order_ref, seg_ref, kv_ref, o_ref, in_sems, out_sems,
):
    moves = (
        (order_hbm, order_ref),
        (seg_hbm, seg_ref),
        (k_hbm, kv_ref.at[0:TOK, 0:HD]),
        (v_hbm, kv_ref.at[0:TOK, HD : 2 * HD]),
        (q_hbm, qp_ref.at[0:TOK]),
        (g_hbm, gp_ref.at[0:TOK]),
        (o_hbm, o_ref),
    )
    copies = [
        pltpu.make_async_copy(src, dst, in_sems.at[i]) for i, (src, dst) in enumerate(moves)
    ]
    for copy in copies:
        copy.start()
    for copy in copies[:4]:
        copy.wait()
    lane = lax.broadcasted_iota(jnp.int32, (1, TOK), 1)
    block = jnp.where(lane < BLK, order_ref[0], order_ref[1]).astype(F32)
    doc = seg_ref[...].astype(F32)
    kv_extra = jnp.concatenate([doc, block], axis=1)
    kv_ref[TOK:PAY, :] = jnp.broadcast_to(kv_extra, (EXTRA, 2 * HD)).astype(BF16)
    outs = [
        pltpu.make_async_copy(kv_ref, kvp_hbm.at[z], out_sems.at[z]) for z in range(ZS)
    ]
    for copy in outs:
        copy.start()
    for copy in copies[4:]:
        copy.wait()
    highs, lows = [], []
    for h in range(GROUP):
        cols = slice(h * HD, (h + 1) * HD)
        prod = gp_ref[0:TOK, cols].astype(F32) * o_ref[:, cols].astype(F32)
        delta = jnp.sum(prod.T, axis=0, keepdims=True)
        high = delta.astype(BF16).astype(F32)
        highs.append(high)
        lows.append(delta - high)
    zero = jnp.zeros_like(doc)
    q_extra = jnp.concatenate([doc, block, zero, zero], axis=1)
    qp_ref[TOK:PAY, :] = jnp.broadcast_to(q_extra, (EXTRA, GROUP * HD)).astype(BF16)
    row = lax.broadcasted_iota(jnp.int32, (EXTRA, GROUP * HD), 0)
    g_extra = jnp.where(
        row == 0, jnp.concatenate(highs, axis=1), jnp.concatenate(lows, axis=1)
    )
    gp_ref[TOK:PAY, :] = g_extra.astype(BF16)
    for copy in outs:
        copy.wait()


def code_of(doc, block):
    lane = lax.broadcasted_iota(jnp.int32, doc.shape, 1)
    within = jnp.where(lane < BLK, lane, lane - BLK).astype(F32)
    return doc * TOKENS + block * BLK + within


def load_queries(q_refs, qs, code):
    for x, q_ref in enumerate(q_refs):
        toks = slice(x * TOK, (x + 1) * TOK)
        for h in range(GROUP):
            qs[h, toks, :] = q_ref[0:TOK, h * HD : (h + 1) * HD]
        info = q_ref[TOK:PAY, :].astype(F32)
        doc, block = info[0:1, 0:TOK], info[0:1, TOK : 2 * TOK]
        code[0:1, toks] = code_of(doc, block)
        code[1:2, toks] = doc * TOKENS


def fill_bias(kv_ref, code, bias):
    for b in range(2):
        info = kv_ref[b, TOK:PAY, :].astype(F32)
        key_code = code_of(info[0:1, 0:TOK], info[0:1, TOK : 2 * TOK])
        key_code = jnp.broadcast_to(key_code, (TOK, TOK)).T
        for x in range(YS):
            toks = slice(x * TOK, (x + 1) * TOK)
            ok = (key_code <= code[0:1, toks]) & (key_code >= code[1:2, toks])
            bias[b * TOK : (b + 1) * TOK, toks] = jnp.where(ok, 0.0, MASKED)


def score_kernel(last, kv_ref, *rest):
    q_refs, rest = rest[:YS], rest[YS:]
    if last:
        y_ref, prev_ref, send_ref, mine_ref, qs, code, bias, keep = rest
    else:
        st_ref, qs, code, bias = rest
    step = pl.program_id(0)

    @pl.when(step == 0)
    def _():
        load_queries(q_refs, qs, code)

    fill_bias(kv_ref, code, bias)
    keys = jnp.concatenate([kv_ref[0, 0:TOK, 0:HD], kv_ref[1, 0:TOK, 0:HD]], axis=0)
    peaks, totals = [], []
    for h in range(GROUP):
        s = dot(keys, qs[h], NT) + bias[...]
        peak = jnp.maximum(jnp.max(s, axis=0, keepdims=True), FLOOR)
        peaks.append(peak)
        totals.append(jnp.sum(jnp.exp2((s - peak) * EXP2), axis=0, keepdims=True))
    stats = jnp.concatenate(peaks + totals, axis=0)
    if not last:
        st_ref[0] = stats
        return
    keep[pl.ds(step, 1)] = stats[None]

    @pl.when(step == STEPS - 1)
    def _():
        tiles = [ref[t] for ref in (prev_ref, keep) for t in range(STEPS)]
        top = functools.reduce(jnp.maximum, [t[0:GROUP] for t in tiles])
        total = sum(t[GROUP:] * jnp.exp2((t[0:GROUP] - top) * EXP2) for t in tiles)
        mine_ref[0:GROUP, :] = top
        mine_ref[GROUP : 2 * GROUP, :] = total
        for d in range(YS):
            for x in range(YS):
                to, of = slice(x * TOK, (x + 1) * TOK), slice((x ^ d) * TOK, ((x ^ d) + 1) * TOK)
                send_ref[y_ref[0] ^ d, 0:GROUP, to] = top[:, of]
                send_ref[y_ref[0] ^ d, GROUP : 2 * GROUP, to] = total[:, of]


def pair_kernel(own_ref, twin_ref, mine_ref, *rest):
    q_refs, g_refs, rest = rest[:YS], rest[YS : 2 * YS], rest[2 * YS :]
    pds_ref, dq_own, dq1, dq2, dq3, kv, qs, gs, code, delta, bias, dq = rest
    step = pl.program_id(0)

    @pl.when(step == 0)
    def _():
        load_queries(q_refs, qs, code)
        for x, g_ref in enumerate(g_refs):
            toks = slice(x * TOK, (x + 1) * TOK)
            info = g_ref[TOK:PAY, :].astype(F32)
            for h in range(GROUP):
                cols = slice(h * HD, (h + 1) * HD)
                gs[h, toks, :] = g_ref[0:TOK, cols]
                delta[h : h + 1, toks] = info[0:1, cols] + info[1:2, cols]
        dq[...] = jnp.zeros_like(dq)

    @pl.when(step < STEPS)
    def _():
        kv[...] = own_ref[...]

    @pl.when(step >= STEPS)
    def _():
        kv[...] = twin_ref[...]

    fill_bias(kv, code, bias)
    keys = jnp.concatenate([kv[0, 0:TOK, 0:HD], kv[1, 0:TOK, 0:HD]], axis=0)
    values = jnp.concatenate([kv[0, 0:TOK, HD : 2 * HD], kv[1, 0:TOK, HD : 2 * HD]], axis=0)
    for h in range(GROUP):
        s = dot(keys, qs[h], NT) + bias[...]
        p = jnp.exp2((s - mine_ref[h : h + 1, :]) * EXP2)
        dp = dot(values, gs[h], NT)
        ds = (p * (dp - delta[h : h + 1, :])).astype(BF16)
        pds_ref[:, h * QT : (h + 1) * QT] = p.astype(BF16)
        pds_ref[:, (GROUP + h) * QT : (GROUP + h + 1) * QT] = ds
        dq[h] += dot(keys, ds, TN)

    @pl.when(step == 2 * STEPS - 1)
    def _():
        for x, out in enumerate((dq_own, dq1, dq2, dq3)):
            for h in range(GROUP):
                part = dq[h, :, x * TOK : (x + 1) * TOK].T * SCALE
                out[:, h * HD : (h + 1) * HD] = part.astype(out.dtype)


def columns(rows):
    rows = jnp.concatenate(rows, axis=0)
    pad = jnp.zeros((TOK - rows.shape[0], TOK), F32)
    return jnp.concatenate([rows, pad], axis=0).T


def weigh(all_ref, mine_ref, y_ref, q_refs, g_refs, qw, gw, back_ref):
    top = functools.reduce(jnp.maximum, [all_ref[y, 0:GROUP] for y in range(YS)])
    total = sum(
        all_ref[y, GROUP : 2 * GROUP] * jnp.exp2((all_ref[y, 0:GROUP] - top) * EXP2)
        for y in range(YS)
    )
    mine = jnp.exp2((mine_ref[0:GROUP] - top) * EXP2) / total
    pieces = [(h, x) for h in range(GROUP) for x in range(YS)]
    weights = columns([mine[h : h + 1, x * TOK : (x + 1) * TOK] for h, x in pieces])
    for i, (h, x) in enumerate(pieces):
        cols, toks = slice(h * HD, (h + 1) * HD), slice(h * QT + x * TOK, h * QT + (x + 1) * TOK)
        weight = jnp.broadcast_to(weights[:, i : i + 1], (TOK, HD))
        qw[toks, :] = (q_refs[x][0:TOK, cols].astype(F32) * (weight * SCALE)).astype(BF16)
        gw[toks, :] = (g_refs[x][0:TOK, cols].astype(F32) * weight).astype(BF16)
    rows = []
    for x in range(YS):
        peak = all_ref[y_ref[0] ^ x, 0:GROUP, 0:TOK]
        back = jnp.exp2((peak - top[:, 0:TOK]) * EXP2) / total[:, 0:TOK]
        rows += [back[h : h + 1] for h in range(GROUP)]
    back_ref[...] = columns(rows)


def key_kernel(first, pds_ref, *rest):
    if first:
        all_ref, mine_ref, y_ref, *rest = rest
        q_refs, g_refs, rest = rest[:YS], rest[YS : 2 * YS], rest[2 * YS :]
        dkv_ref, qw, gw, back_ref = rest

        @pl.when(pl.program_id(0) == 0)
        def _():
            weigh(all_ref, mine_ref, y_ref, q_refs, g_refs, qw, gw, back_ref)
    else:
        qw, gw, dkv_ref = rest
    dv = dot(pds_ref[:, 0 : GROUP * QT], gw[...])
    dk = dot(pds_ref[:, GROUP * QT : 2 * GROUP * QT], qw[...])
    for b in range(2):
        rows = slice(b * TOK, (b + 1) * TOK)
        dkv_ref[b, :, 0:HD] = dk[rows].astype(dkv_ref.dtype)
        dkv_ref[b, :, HD : 2 * HD] = dv[rows].astype(dkv_ref.dtype)


def sum_kernel(back_ref, p0, p1, p2, p3, out_ref):
    for h in range(GROUP):
        cols = slice(h * HD, (h + 1) * HD)
        total = jnp.zeros((TOK, HD), F32)
        for x, part in enumerate((p0, p1, p2, p3)):
            i = x * GROUP + h
            weight = jnp.broadcast_to(back_ref[:, i : i + 1], (TOK, HD))
            total = total + part[:, cols].astype(F32) * weight
        out_ref[:, cols] = total.astype(BF16)


def whole(shape):
    return pl.BlockSpec(shape, lambda *_: (0,) * len(shape))


def shape_of(shape, dtype):
    return jax.ShapeDtypeStruct(shape, dtype)


def params(limit=VMEM_LIMIT):
    return pltpu.CompilerParams(vmem_limit_bytes=limit << 20)


def pack(order, seg, q, k, v, o, g):
    hbm = pl.BlockSpec(memory_space=pltpu.HBM)
    vm = pl.BlockSpec(memory_space=pltpu.VMEM)
    pay = shape_of((PAY, GROUP * HD), BF16)
    return pl.pallas_call(
        pack_kernel,
        out_shape=(shape_of((ZS, PAY, 2 * HD), BF16), pay, pay),
        in_specs=[hbm] * 7,
        out_specs=(hbm, vm, vm),
        scratch_shapes=[
            pltpu.SMEM((2,), jnp.int32),
            pltpu.VMEM((1, TOK), jnp.int32),
            pltpu.VMEM((PAY, 2 * HD), BF16),
            pltpu.VMEM((TOK, GROUP * HD), BF16),
            pltpu.SemaphoreType.DMA((7,)),
            pltpu.SemaphoreType.DMA((ZS,)),
        ],
        compiler_params=params(60),
        name="pack",
    )(order, seg, q, k, v, o, g)


STEPS = ZS // 2
PAIRS = ZS * TOK * GROUP * QT
SMEM = pl.BlockSpec(memory_space=pltpu.SMEM)
PAYS = [whole((PAY, GROUP * HD))] * YS
STATS = (2 * GROUP, QT)


def cost(flops):
    return pl.CostEstimate(flops=flops, bytes_accessed=1 << 16, transcendentals=0)


def scores(kv, queries, prev=None, y_index=None):
    in_specs = [pl.BlockSpec((2, PAY, 2 * HD), lambda i: (i, 0, 0)), *PAYS]
    args = [kv, *queries]
    scratch = [
        pltpu.VMEM((GROUP, QT, HD), BF16),
        pltpu.VMEM((8, QT), F32),
        pltpu.VMEM((KT, QT), F32),
    ]
    if prev is None:
        out_shape = shape_of((STEPS, *STATS), F32)
        out_specs = pl.BlockSpec((1, *STATS), lambda i: (i, 0, 0))
    else:
        in_specs += [SMEM, whole(prev.shape)]
        args += [y_index, prev]
        out_shape = (shape_of((YS, *STATS), F32), shape_of(STATS, F32))
        out_specs = (whole((YS, *STATS)), whole(STATS))
        scratch.append(pltpu.VMEM((STEPS, *STATS), F32))
    return pl.pallas_call(
        functools.partial(score_kernel, prev is not None),
        grid=(STEPS,),
        in_specs=in_specs,
        out_specs=out_specs,
        out_shape=out_shape,
        scratch_shapes=scratch,
        compiler_params=params(),
        cost_estimate=cost(PAIRS),
        name="scores",
    )(*args)


def pairs(kv_own, kv_twin, mine, queries, outs):
    dq_spec = whole((TOK, GROUP * HD))
    return pl.pallas_call(
        pair_kernel,
        grid=(2 * STEPS,),
        in_specs=[
            pl.BlockSpec((2, PAY, 2 * HD), lambda i: (jnp.minimum(i, STEPS - 1), 0, 0)),
            pl.BlockSpec((2, PAY, 2 * HD), lambda i: (jnp.maximum(i - STEPS, 0), 0, 0)),
            whole(STATS),
            *PAYS,
            *PAYS,
        ],
        out_specs=[pl.BlockSpec((KT, 2 * GROUP * QT), lambda i: (i, 0))] + [dq_spec] * YS,
        out_shape=[
            shape_of((2 * ZS * TOK, 2 * GROUP * QT), BF16),
            shape_of((TOK, GROUP * HD), F32),
        ]
        + [shape_of((TOK, GROUP * HD), BF16)] * (YS - 1),
        scratch_shapes=[
            pltpu.VMEM((2, PAY, 2 * HD), BF16),
            pltpu.VMEM((GROUP, QT, HD), BF16),
            pltpu.VMEM((GROUP, QT, HD), BF16),
            pltpu.VMEM((8, QT), F32),
            pltpu.VMEM((8, QT), F32),
            pltpu.VMEM((KT, QT), F32),
            pltpu.VMEM((GROUP, HD, QT), F32),
        ],
        compiler_params=params(PAIR_LIMIT),
        cost_estimate=cost(12 * PAIRS * HD),
        name="pairs",
    )(kv_own, kv_twin, mine, *queries, *outs)


def key_grads(pds, half, dtype, first=None, weighted=None):
    in_specs = [pl.BlockSpec((KT, 2 * GROUP * QT), lambda i: (i + half * STEPS, 0))]
    rows = (GROUP * QT, HD)
    out_shape = [shape_of((ZS, TOK, 2 * HD), dtype)]
    out_specs = [pl.BlockSpec((2, TOK, 2 * HD), lambda i: (i, 0, 0))]
    if first:
        all_stats, mine, y_index, queries, outs = first
        in_specs += [whole((YS, *STATS)), whole(STATS), SMEM, *PAYS, *PAYS]
        args = [all_stats, mine, y_index, *queries, *outs]
        out_shape += [shape_of(rows, BF16)] * 2 + [shape_of((TOK, TOK), F32)]
        out_specs += [whole(rows)] * 2 + [whole((TOK, TOK))]
    else:
        in_specs += [whole(rows)] * 2
        args = weighted
    return pl.pallas_call(
        functools.partial(key_kernel, bool(first)),
        grid=(STEPS,),
        in_specs=in_specs,
        out_specs=out_specs,
        out_shape=out_shape,
        compiler_params=params(PAIR_LIMIT),
        cost_estimate=cost(2 * PAIRS * HD),
        name="key_grads",
    )(pds, *args)


def sum_queries(back, parts):
    vm = pl.BlockSpec(memory_space=pltpu.VMEM)
    return pl.pallas_call(
        sum_kernel,
        in_specs=[vm] * 5,
        out_specs=vm,
        out_shape=shape_of((TOK, GROUP * HD), BF16),
        compiler_params=params(),
        name="sum_queries",
    )(back, *parts)


def per_device(query, key_rows, value_rows, output, grad_out, block_order, segment):
    n = lax.axis_size("ctx")
    z_groups = [[z * 2 * YS + r for z in range(ZS)] for r in range(2 * YS)]
    y_groups = [
        [z * 2 * YS + y * 2 + c for y in range(YS)] for z in range(ZS) for c in range(2)
    ]

    def swap(x, bits):
        return lax.ppermute(x, "ctx", [(i, i ^ bits) for i in range(n)])

    def exchange(x, groups):
        return lax.all_to_all(x, "ctx", 0, 0, tiled=True, axis_index_groups=groups)

    kv_pay, q_pay, g_pay = pack(
        block_order, segment.reshape(1, TOK), query, key_rows, value_rows, output, grad_out
    )
    kv_own = exchange(kv_pay, z_groups)
    g_far, g_near = swap(g_pay, 4), swap(g_pay, 2)
    queries = [q_pay] + [swap(q_pay, 2 * x) for x in range(1, YS)]
    kv_own, queries, g_near, g_far = lax.optimization_barrier((kv_own, queries, g_near, g_far))
    kv_twin = swap(kv_own, 1)
    outs = [g_pay, g_near, g_far, swap(g_far, 2)]
    st_own = scores(kv_own, queries)
    kv_twin, outs = lax.optimization_barrier((kv_twin, outs))
    y_index = (lax.axis_index("ctx").astype(jnp.int32) >> 1 & (YS - 1)).reshape(1)
    send, mine = scores(kv_twin, queries, st_own, y_index)
    all_stats = exchange(send, y_groups)
    pds, *dq_parts = pairs(kv_own, kv_twin, mine, queries, outs)
    first = (all_stats, mine, y_index, queries, outs)
    dkv_twin, qw, gw, back = key_grads(pds, 1, BF16, first=first)
    dkv_back = swap(dkv_twin, 1)
    (dkv_own,) = key_grads(pds, 0, F32, weighted=(qw, gw))
    dkv = (dkv_own + dkv_back.astype(F32)).astype(BF16)
    dkv_all = exchange(dkv, z_groups)
    parts = [dq_parts[0]] + [swap(part, 2 * x) for x, part in enumerate(dq_parts[1:], 1)]
    grad_query = sum_queries(back, parts)
    grad_kv = jnp.sum(dkv_all.astype(F32), axis=0).astype(BF16)
    return grad_query, grad_kv[:, 0:HD], grad_kv[:, HD : 2 * HD]


def solution(mesh):
    both = P("ctx", "kvh")
    return jax.shard_map(
        per_device,
        mesh=mesh,
        in_specs=(both, both, both, both, both, P("ctx"), P("ctx")),
        out_specs=(both, both, both),
        check_vma=False,
    )
```

time: 106 us -> 117 us (1.10)
  Pallas kernels: 20.8 us -> 35.5 us
  blocking collectives: 10.8 us -> 0 us
  starting transfers between devices: 53.8 us -> 56.6 us
  local copies, waits for them, and re-layouts: 2.44 us -> 5.17 us
  waiting for transfers between devices: 14.5 us -> 15.8 us
    pallas_call x4 -> x6, Pallas kernels: 18.4 us -> 33 us  [the longest x1 13.9 us: pairs(): pl.pallas_call(pair_kernel, grid=(2 * STEPS,), in_specs=[pl.BlockSpec((2,...]
    all_to_all x1 -> x0, blocking collectives: 10.8 us -> none  [exchange(): return lax.all_to_all(x, 'ctx', 0, 0, tiled=True, axis_index_groups=groups)]
    all_to_all x2 -> x3, starting transfers between devices: 17.5 us -> 21.6 us  [exchange(): return lax.all_to_all(x, 'ctx', 0, 0, tiled=True, axis_index_groups=groups)]
    unnamed x4 -> x10, local copies, waits for them, and re-layouts: 1.81 us -> 4.54 us
    ppermute x11, waiting for transfers between devices: 13 us -> 15.7 us  [swap(): return lax.ppermute(x, 'ctx', [(i, i ^ bits) for i in range(n)])]
    all_to_all x2 -> x3, waiting for transfers between devices: 1.5 us -> 0.01 us  [exchange(): return lax.all_to_all(x, 'ctx', 0, 0, tiled=True, axis_index_groups=groups)]
    ppermute x11, starting transfers between devices: 36.4 us -> 35 us  [swap(): return lax.ppermute(x, 'ctx', [(i, i ^ bits) for i in range(n)])]
  transfers between devices with their start and end apart: 13 -> 14, of which waited for: 5 -> 3; matrix products, arithmetic and copies ran while one was open for 1% -> 0% of each run, Pallas kernels for 9% -> 20%
where the time goes in v4:
time: 117 us; the launch traced here: 115 us
  starting transfers between devices  56.6 us (48%)
  Pallas kernels  35.5 us (30%)
  waiting for transfers between devices  15.8 us (14%)
  local copies, waits for them, and re-layouts  5.17 us (4%)
    ppermute x11, starting transfers between devices, swap(): return lax.ppermute(x, 'ctx', [(i, i ^ bits) for i in range(n)])  35 us
    all_to_all x3, starting transfers between devices, exchange(): return lax.all_to_all(x, 'ctx', 0, 0, tiled=True, axis_index_groups=groups)  21.6 us
    ppermute x11, waiting for transfers between devices, swap(): return lax.ppermute(x, 'ctx', [(i, i ^ bits) for i in range(n)])  15.7 us
    pallas_call x1, Pallas kernels, pairs(): pl.pallas_call(pair_kernel, grid=(2 * STEPS,), in_specs=[pl.BlockSpec((2,...  13.9 us
    pallas_call x2, Pallas kernels, key_grads(): pl.pallas_call(functools.partial(key_kernel, bool(first)), grid=(STEPS,),...  11.5 us
    pallas_call x2, Pallas kernels, scores(): pl.pallas_call(functools.partial(score_kernel, prev is not None), grid=(S...  6.62 us
    unnamed x10, local copies, waits for them, and re-layouts  4.54 us
    pallas_call x1, Pallas kernels, pack(): pl.pallas_call(pack_kernel, out_shape=(shape_of((ZS, PAY, 2 * HD), BF16),...  2.48 us
  transfers between devices with their start and end apart: 14, of which 3 were waited for; matrix products, arithmetic and copies ran while one was open for 0% of the time, Pallas kernels for 20%

profile of v4, /device:TPU:1, one launch (start us, length us, event | category | flops | bytes accessed | tf_op | source)
XLA Modules:
  0.0 114.8 jit_solution(7145388123361142578)
XLA Ops:
  0.6 2.5 %pack.1 = (bf16[8,144,256]{2,1,0:T(8,128)(2,1)}, bf16[144,512]{1,0:T(8,128)(2,1)}, bf16[144,512]{1,0:T(8,128)(2,1)}) custom-call(s32[2]{0:T(128)} %order_hbm.1, s32[1,128]{1,0:T(1,128)} %bitcast.2, bf16[128,512]{1,0:T(8,128)(2,1)} %q_hbm.1, bf16[128,128]{1,0:T(8,128)(2,1)} %k_hbm.1, bf16[128,128]{1,0:T(8,128)(2,1)} %v_hbm.1, bf16[128,512]{1,0:T(8,128)(2,1)} %o_hbm.1, ...), custom_call_target="tpu_custom_call" | custom-call | tf_op jit(solution)/shard_map/pack/pallas_call | solution.py:279
  3.1 10.9 %all-to-all-start = ((bf16[8,144,256]{2,1,0:T(8,128)(2,1)}), bf16[8,144,256]{2,1,0:T(8,128)(2,1)S(1)}, u32[]{:S(2)}, u32[]{:S(2)}) async-start(bf16[8,144,256]{2,1,0:T(8,128)(2,1)} %get-tuple-element.29), calls=%async_computation | async-start | bytes 1179648 | tf_op jit(solution)/shard_map/all_to_all | solution.py:420
  14.0 4.2 %collective-permute-start.4 = (bf16[144,512]{1,0:T(8,128)(2,1)}, bf16[144,512]{1,0:T(8,128)(2,1)S(1)}, u32[]{:S(2)}, u32[]{:S(2)}) collective-permute-start(bf16[144,512]{1,0:T(8,128)(2,1)} %get-tuple-element.41.rest_4_.rest_7_), channel_id=1, source_target_pairs={{0,32},{8,40},{16,48},{24,56},{32,0},{40,8},{48,16},{56,24},{64,96... | collective-permute-start | bytes 442376 | tf_op jit(solution)/shard_map/ppermute | solution.py:417
  18.2 3.2 %collective-permute-start.3 = (bf16[144,512]{1,0:T(8,128)(2,1)}, bf16[144,512]{1,0:T(8,128)(2,1)S(1)}, u32[]{:S(2)}, u32[]{:S(2)}) collective-permute-start(bf16[144,512]{1,0:T(8,128)(2,1)} %get-tuple-element.41.rest_4_.rest_7_), channel_id=1, source_target_pairs={{0,16},{8,24},{16,0},{24,8},{32,48},{40,56},{48,32},{56,40},{64,80... | collective-permute-start | bytes 442376 | tf_op jit(solution)/shard_map/ppermute | solution.py:417
  21.4 1.9 %collective-permute-start.2 = (bf16[144,512]{1,0:T(8,128)(2,1)}, bf16[144,512]{1,0:T(8,128)(2,1)S(1)}, u32[]{:S(2)}, u32[]{:S(2)}) collective-permute-start(bf16[144,512]{1,0:T(8,128)(2,1)} %get-tuple-element.36.rest_0_.rest_3_), channel_id=1, source_target_pairs={{0,48},{8,56},{16,32},{24,40},{32,16},{40,24},{48,0},{56,8},{64,11... | collective-permute-start | bytes 442376 | tf_op jit(solution)/shard_map/ppermute | solution.py:417
  23.4 3.2 %collective-permute-start.1 = (bf16[144,512]{1,0:T(8,128)(2,1)}, bf16[144,512]{1,0:T(8,128)(2,1)S(1)}, u32[]{:S(2)}, u32[]{:S(2)}) collective-permute-start(bf16[144,512]{1,0:T(8,128)(2,1)} %get-tuple-element.36.rest_0_.rest_3_), channel_id=1, source_target_pairs={{0,32},{8,40},{16,48},{24,56},{32,0},{40,8},{48,16},{56,24},{64,96... | collective-permute-start | bytes 442376 | tf_op jit(solution)/shard_map/ppermute | solution.py:417
  26.6 4.1 %collective-permute-start = (bf16[144,512]{1,0:T(8,128)(2,1)}, bf16[144,512]{1,0:T(8,128)(2,1)S(1)}, u32[]{:S(2)}, u32[]{:S(2)}) collective-permute-start(bf16[144,512]{1,0:T(8,128)(2,1)} %get-tuple-element.36.rest_0_.rest_3_), channel_id=1, source_target_pairs={{0,16},{8,24},{16,0},{24,8},{32,48},{40,56},{48,32},{56,40},{64,80... | collective-permute-start | bytes 442376 | tf_op jit(solution)/shard_map/ppermute | solution.py:417
  30.7 0.0 collective-permute-done.4.rest_6_.rest_9_
  30.7 0.0 collective-permute-done.3.rest_5_.rest_8_
  30.7 0.0 collective-permute-done.2.rest_3_.rest_6_
  30.7 6.9 %collective-permute-done.1.rest_2_.rest_5_ = bf16[144,512]{1,0:T(8,128)(2,1)S(1)} collective-permute-done((bf16[144,512]{1,0:T(8,128)(2,1)}, bf16[144,512]{1,0:T(8,128)(2,1)S(1)}, u32[]{:S(2)}, u32[]{:S(2)}) %collective-permute-start.1) | collective-permute-done | bytes 147488 | tf_op jit(solution)/shard_map/ppermute | solution.py:417
  37.6 0.0 collective-permute-done.rest_1_.rest_4_
  37.6 0.0 all-to-all-done.kv_ref.own_ref
  37.6 3.8 %collective-permute-start.5 = (bf16[8,144,256]{2,1,0:T(8,128)(2,1)S(1)}, bf16[8,144,256]{2,1,0:T(8,128)(2,1)S(1)}, u32[]{:S(2)}, u32[]{:S(2)}) collective-permute-start(bf16[8,144,256]{2,1,0:T(8,128)(2,1)S(1)} %all-to-all-done.kv_ref.own_ref), channel_id=1, source_target_pairs={{0,8},{8,0},{16,24},{24,16},{32,40},{40,32},{48,56},{56,48},{64,72... | collective-permute-start | bytes 1769480 | tf_op jit(solution)/shard_map/ppermute | solution.py:417
  41.4 2.0 %collective-permute-start.6 = (bf16[144,512]{1,0:T(8,128)(2,1)S(1)}, bf16[144,512]{1,0:T(8,128)(2,1)S(1)}, u32[]{:S(2)}, u32[]{:S(2)}) collective-permute-start(bf16[144,512]{1,0:T(8,128)(2,1)S(1)} %collective-permute-done.4.rest_6_.rest_9_), channel_id=1, source_target_pairs={{0,16},{8,24},{16,0},{24,8},{32,48},{40,56},{48,32},{56,40},{64,80... | collective-permute-start | bytes 442376 | tf_op jit(solution)/shard_map/ppermute | solution.py:417
  43.4 0.0 copy-start
  43.4 0.9 copy-done
  44.3 3.0 %scores.2.rest_5_ = f32[4,8,512]{2,1,0:T(8,128)S(1)} custom-call(bf16[8,144,256]{2,1,0:T(8,128)(2,1)S(1)} %all-to-all-done.kv_ref.own_ref, bf16[144,512]{1,0:T(8,128)(2,1)S(1)} %copy-done, bf16[144,512]{1,0:T(8,128)(2,1)S(1)} %collective-permute-done.rest_1_.rest_4_, bf16[144,512]{1,0:T(8,128)(2,1)S(1)} %collective-permute-done.1.rest_2_.rest_5_, ...), custom_call_target="tpu_custom_call" | custom-call | flops 2097152 | bytes 65536 | tf_op jit(solution)/shard_map/scores/pallas_call | solution.py:325
  47.3 1.4 %collective-permute-done.6.rest_7_.rest_10_ = bf16[144,512]{1,0:T(8,128)(2,1)S(1)} collective-permute-done((bf16[144,512]{1,0:T(8,128)(2,1)S(1)}, bf16[144,512]{1,0:T(8,128)(2,1)S(1)}, u32[]{:S(2)}, u32[]{:S(2)}) %collective-permute-start.6) | collective-permute-done | bytes 147488 | tf_op jit(solution)/shard_map/ppermute | solution.py:417
  48.8 0.0 collective-permute-done.5.kv_ref.twin_ref
  48.8 3.7 %scores.3 = (f32[4,8,512]{2,1,0:T(8,128)}, f32[8,512]{1,0:T(8,128)S(1)}) custom-call(bf16[8,144,256]{2,1,0:T(8,128)(2,1)S(1)} %collective-permute-done.5.kv_ref.twin_ref, bf16[144,512]{1,0:T(8,128)(2,1)S(1)} %copy-done, bf16[144,512]{1,0:T(8,128)(2,1)S(1)} %collective-permute-done.rest_1_.rest_4_, ...), custom_call_target="tpu_custom_call" | custom-call | flops 2097152 | bytes 65536 | tf_op jit(solution)/shard_map/scores/pallas_call | solution.py:325
  52.4 4.1 %all-to-all-start.1 = ((f32[4,8,512]{2,1,0:T(8,128)}), f32[4,8,512]{2,1,0:T(8,128)S(1)}, u32[]{:S(2)}, u32[]{:S(2)}) async-start(f32[4,8,512]{2,1,0:T(8,128)} %get-tuple-element.46), calls=%async_computation.1 | async-start | bytes 131072 | tf_op jit(solution)/shard_map/all_to_all | solution.py:420
  56.5 0.0 copy-start.1
  56.5 0.9 copy-done.1
  57.4 0.0 copy-start.3
  57.4 0.9 copy-done.3
  58.3 13.9 %pairs.1 = (bf16[2048,4096]{1,0:T(8,128)(2,1)}, f32[128,512]{1,0:T(8,128)S(1)}, bf16[128,512]{1,0:T(8,128)(2,1)S(1)}, bf16[128,512]{1,0:T(8,128)(2,1)S(1)}, bf16[128,512]{1,0:T(8,128)(2,1)S(1)}) custom-call(bf16[8,144,256]{2,1,0:T(8,128)(2,1)S(1)} %all-to-all-done.kv_ref.own_ref, bf16[8,144,256]{2,1,0:T(8,128)(2,1)S(1)} %collective-permute-done.5.kv_ref.twin_ref, ...), custom_call_target="tpu_custom_call" | custom-call | flops 3221225472 | bytes 65536 | tf_op jit(solution)/shard_map/pairs/pallas_call | solution.py:340
  72.2 0.0 all-to-all-done.1.rest_0_
  72.2 0.0 copy-start.2
  72.2 0.9 copy-done.2
  73.1 0.0 copy-start.4
  73.1 0.9 copy-done.4
  74.0 6.0 %key_grads.2 = (bf16[8,128,256]{2,1,0:T(8,128)(2,1)S(1)}, bf16[2048,128]{1,0:T(8,128)(2,1)S(1)}, bf16[2048,128]{1,0:T(8,128)(2,1)S(1)}, f32[128,128]{1,0:T(8,128)S(1)}) custom-call(bf16[2048,4096]{1,0:T(8,128)(2,1)} %get-tuple-element.45.pds_ref, f32[4,8,512]{2,1,0:T(8,128)S(1)} %all-to-all-done.1.rest_0_, f32[8,512]{1,0:T(8,128)S(1)} %get-tuple-element.40.mine_ref.rest_1_, ...), custom_call_target="tpu_custom_call" | custom-call | flops 536870912 | bytes 65536 | tf_op jit(solution)/shard_map/key_grads/pallas_call | solution.py:385
  80.1 3.0 %collective-permute-start.10 = (bf16[8,128,256]{2,1,0:T(8,128)(2,1)S(1)}, bf16[8,128,256]{2,1,0:T(8,128)(2,1)S(1)}, u32[]{:S(2)}, u32[]{:S(2)}) collective-permute-start(bf16[8,128,256]{2,1,0:T(8,128)(2,1)S(1)} %get-tuple-element.54), channel_id=1, source_target_pairs={{0,8},{8,0},{16,24},{24,16},{32,40},{40,32},{48,56},{56,48},{64,72... | collective-permute-start | bytes 1572872 | tf_op jit(solution)/shard_map/ppermute | solution.py:417
  83.0 5.5 %key_grads.3 = f32[8,128,256]{2,1,0:T(8,128)S(1)} custom-call(bf16[2048,4096]{1,0:T(8,128)(2,1)} %get-tuple-element.45.pds_ref, bf16[2048,128]{1,0:T(8,128)(2,1)S(1)} %get-tuple-element.52.rest_0_, bf16[2048,128]{1,0:T(8,128)(2,1)S(1)} %get-tuple-element.53.rest_1_), custom_call_target="tpu_custom_call" | custom-call | flops 536870912 | bytes 65536 | tf_op jit(solution)/shard_map/key_grads/pallas_call | solution.py:385
  88.5 0.0 collective-permute-done.10
  88.5 0.9 add_convert_fusion
  89.5 6.6 %all-to-all-start.2 = ((bf16[8,128,256]{2,1,0:T(8,128)(2,1)}), bf16[8,128,256]{2,1,0:T(8,128)(2,1)S(1)}, u32[]{:S(2)}, u32[]{:S(2)}) async-start(bf16[8,128,256]{2,1,0:T(8,128)(2,1)} %add_convert_fusion), calls=%async_computation.2 | async-start | bytes 1048576 | tf_op jit(solution)/shard_map/all_to_all | solution.py:420
  96.1 3.6 %collective-permute-start.7 = (bf16[128,512]{1,0:T(8,128)(2,1)S(1)}, bf16[128,512]{1,0:T(8,128)(2,1)S(1)}, u32[]{:S(2)}, u32[]{:S(2)}) collective-permute-start(bf16[128,512]{1,0:T(8,128)(2,1)S(1)} %get-tuple-element.49), channel_id=1, source_target_pairs={{0,16},{8,24},{16,0},{24,8},{32,48},{40,56},{48,32},{56,40},{64,80... | collective-permute-start | bytes 393224 | tf_op jit(solution)/shard_map/ppermute | solution.py:417
  99.7 4.0 %collective-permute-start.8 = (bf16[128,512]{1,0:T(8,128)(2,1)S(1)}, bf16[128,512]{1,0:T(8,128)(2,1)S(1)}, u32[]{:S(2)}, u32[]{:S(2)}) collective-permute-start(bf16[128,512]{1,0:T(8,128)(2,1)S(1)} %get-tuple-element.50), channel_id=1, source_target_pairs={{0,32},{8,40},{16,48},{24,56},{32,0},{40,8},{48,16},{56,24},{64,96... | collective-permute-start | bytes 393224 | tf_op jit(solution)/shard_map/ppermute | solution.py:417
  103.7 1.9 %collective-permute-start.9 = (bf16[128,512]{1,0:T(8,128)(2,1)S(1)}, bf16[128,512]{1,0:T(8,128)(2,1)S(1)}, u32[]{:S(2)}, u32[]{:S(2)}) collective-permute-start(bf16[128,512]{1,0:T(8,128)(2,1)S(1)} %get-tuple-element.51), channel_id=1, source_target_pairs={{0,48},{8,56},{16,32},{24,40},{32,16},{40,24},{48,0},{56,8},{64,11... | collective-permute-start | bytes 393224 | tf_op jit(solution)/shard_map/ppermute | solution.py:417
  105.7 0.0 collective-permute-done.7.p1
  105.7 7.4 %collective-permute-done.8.p2 = bf16[128,512]{1,0:T(8,128)(2,1)S(1)} collective-permute-done((bf16[128,512]{1,0:T(8,128)(2,1)S(1)}, bf16[128,512]{1,0:T(8,128)(2,1)S(1)}, u32[]{:S(2)}, u32[]{:S(2)}) %collective-permute-start.8) | collective-permute-done | bytes 131104 | tf_op jit(solution)/shard_map/ppermute | solution.py:417
  113.1 0.0 collective-permute-done.9.p3
  113.1 1.0 sum_queries.1
  114.1 0.0 all-to-all-done.2
  114.1 0.1 reduce_sum.12
  114.2 0.6 fusion
Async XLA Ops:
  3.1 34.5 %all-to-all-start = ((bf16[8,144,256]{2,1,0:T(8,128)(2,1)}), bf16[8,144,256]{2,1,0:T(8,128)(2,1)S(1)}, u32[]{:S(2)}, u32[]{:S(2)}) async-start(bf16[8,144,256]{2,1,0:T(8,128)(2,1)} %get-tuple-element.29), calls=%async_computation | async-start | bytes 1179648 | tf_op jit(solution)/shard_map/all_to_all | solution.py:420
  14.0 16.7 %collective-permute-start.4 = (bf16[144,512]{1,0:T(8,128)(2,1)}, bf16[144,512]{1,0:T(8,128)(2,1)S(1)}, u32[]{:S(2)}, u32[]{:S(2)}) collective-permute-start(bf16[144,512]{1,0:T(8,128)(2,1)} %get-tuple-element.41.rest_4_.rest_7_), channel_id=1, source_target_pairs={{0,32},{8,40},{16,48},{24,56},{32,0},{40,8},{48,16},{56,24},{64,96... | collective-permute-start | bytes 442376 | tf_op jit(solution)/shard_map/ppermute | solution.py:417
  18.2 12.5 %collective-permute-start.3 = (bf16[144,512]{1,0:T(8,128)(2,1)}, bf16[144,512]{1,0:T(8,128)(2,1)S(1)}, u32[]{:S(2)}, u32[]{:S(2)}) collective-permute-start(bf16[144,512]{1,0:T(8,128)(2,1)} %get-tuple-element.41.rest_4_.rest_7_), channel_id=1, source_target_pairs={{0,16},{8,24},{16,0},{24,8},{32,48},{40,56},{48,32},{56,40},{64,80... | collective-permute-start | bytes 442376 | tf_op jit(solution)/shard_map/ppermute | solution.py:417
  21.4 9.3 %collective-permute-start.2 = (bf16[144,512]{1,0:T(8,128)(2,1)}, bf16[144,512]{1,0:T(8,128)(2,1)S(1)}, u32[]{:S(2)}, u32[]{:S(2)}) collective-permute-start(bf16[144,512]{1,0:T(8,128)(2,1)} %get-tuple-element.36.rest_0_.rest_3_), channel_id=1, source_target_pairs={{0,48},{8,56},{16,32},{24,40},{32,16},{40,24},{48,0},{56,8},{64,11... | collective-permute-start | bytes 442376 | tf_op jit(solution)/shard_map/ppermute | solution.py:417
  23.4 14.2 %collective-permute-start.1 = (bf16[144,512]{1,0:T(8,128)(2,1)}, bf16[144,512]{1,0:T(8,128)(2,1)S(1)}, u32[]{:S(2)}, u32[]{:S(2)}) collective-permute-start(bf16[144,512]{1,0:T(8,128)(2,1)} %get-tuple-element.36.rest_0_.rest_3_), channel_id=1, source_target_pairs={{0,32},{8,40},{16,48},{24,56},{32,0},{40,8},{48,16},{56,24},{64,96... | collective-permute-start | bytes 442376 | tf_op jit(solution)/shard_map/ppermute | solution.py:417
  26.6 11.0 %collective-permute-start = (bf16[144,512]{1,0:T(8,128)(2,1)}, bf16[144,512]{1,0:T(8,128)(2,1)S(1)}, u32[]{:S(2)}, u32[]{:S(2)}) collective-permute-start(bf16[144,512]{1,0:T(8,128)(2,1)} %get-tuple-element.36.rest_0_.rest_3_), channel_id=1, source_target_pairs={{0,16},{8,24},{16,0},{24,8},{32,48},{40,56},{48,32},{56,40},{64,80... | collective-permute-start | bytes 442376 | tf_op jit(solution)/shard_map/ppermute | solution.py:417
  37.6 11.2 %collective-permute-start.5 = (bf16[8,144,256]{2,1,0:T(8,128)(2,1)S(1)}, bf16[8,144,256]{2,1,0:T(8,128)(2,1)S(1)}, u32[]{:S(2)}, u32[]{:S(2)}) collective-permute-start(bf16[8,144,256]{2,1,0:T(8,128)(2,1)S(1)} %all-to-all-done.kv_ref.own_ref), channel_id=1, source_target_pairs={{0,8},{8,0},{16,24},{24,16},{32,40},{40,32},{48,56},{56,48},{64,72... | collective-permute-start | bytes 1769480 | tf_op jit(solution)/shard_map/ppermute | solution.py:417
  41.4 7.4 %collective-permute-start.6 = (bf16[144,512]{1,0:T(8,128)(2,1)S(1)}, bf16[144,512]{1,0:T(8,128)(2,1)S(1)}, u32[]{:S(2)}, u32[]{:S(2)}) collective-permute-start(bf16[144,512]{1,0:T(8,128)(2,1)S(1)} %collective-permute-done.4.rest_6_.rest_9_), channel_id=1, source_target_pairs={{0,16},{8,24},{16,0},{24,8},{32,48},{40,56},{48,32},{56,40},{64,80... | collective-permute-start | bytes 442376 | tf_op jit(solution)/shard_map/ppermute | solution.py:417
  43.4 0.9 copy-start
  52.4 19.8 %all-to-all-start.1 = ((f32[4,8,512]{2,1,0:T(8,128)}), f32[4,8,512]{2,1,0:T(8,128)S(1)}, u32[]{:S(2)}, u32[]{:S(2)}) async-start(f32[4,8,512]{2,1,0:T(8,128)} %get-tuple-element.46), calls=%async_computation.1 | async-start | bytes 131072 | tf_op jit(solution)/shard_map/all_to_all | solution.py:420
  56.5 0.9 copy-start.1
  57.4 0.9 copy-start.3
  72.2 0.9 copy-start.2
  73.1 0.9 copy-start.4
  80.1 8.5 %collective-permute-start.10 = (bf16[8,128,256]{2,1,0:T(8,128)(2,1)S(1)}, bf16[8,128,256]{2,1,0:T(8,128)(2,1)S(1)}, u32[]{:S(2)}, u32[]{:S(2)}) collective-permute-start(bf16[8,128,256]{2,1,0:T(8,128)(2,1)S(1)} %get-tuple-element.54), channel_id=1, source_target_pairs={{0,8},{8,0},{16,24},{24,16},{32,40},{40,32},{48,56},{56,48},{64,72... | collective-permute-start | bytes 1572872 | tf_op jit(solution)/shard_map/ppermute | solution.py:417
  89.5 24.7 %all-to-all-start.2 = ((bf16[8,128,256]{2,1,0:T(8,128)(2,1)}), bf16[8,128,256]{2,1,0:T(8,128)(2,1)S(1)}, u32[]{:S(2)}, u32[]{:S(2)}) async-start(bf16[8,128,256]{2,1,0:T(8,128)(2,1)} %add_convert_fusion), calls=%async_computation.2 | async-start | bytes 1048576 | tf_op jit(solution)/shard_map/all_to_all | solution.py:420
  96.1 9.6 %collective-permute-start.7 = (bf16[128,512]{1,0:T(8,128)(2,1)S(1)}, bf16[128,512]{1,0:T(8,128)(2,1)S(1)}, u32[]{:S(2)}, u32[]{:S(2)}) collective-permute-start(bf16[128,512]{1,0:T(8,128)(2,1)S(1)} %get-tuple-element.49), channel_id=1, source_target_pairs={{0,16},{8,24},{16,0},{24,8},{32,48},{40,56},{48,32},{56,40},{64,80... | collective-permute-start | bytes 393224 | tf_op jit(solution)/shard_map/ppermute | solution.py:417
  99.7 13.4 %collective-permute-start.8 = (bf16[128,512]{1,0:T(8,128)(2,1)S(1)}, bf16[128,512]{1,0:T(8,128)(2,1)S(1)}, u32[]{:S(2)}, u32[]{:S(2)}) collective-permute-start(bf16[128,512]{1,0:T(8,128)(2,1)S(1)} %get-tuple-element.50), channel_id=1, source_target_pairs={{0,32},{8,40},{16,48},{24,56},{32,0},{40,8},{48,16},{56,24},{64,96... | collective-permute-start | bytes 393224 | tf_op jit(solution)/shard_map/ppermute | solution.py:417
  103.7 9.4 %collective-permute-start.9 = (bf16[128,512]{1,0:T(8,128)(2,1)S(1)}, bf16[128,512]{1,0:T(8,128)(2,1)S(1)}, u32[]{:S(2)}, u32[]{:S(2)}) collective-permute-start(bf16[128,512]{1,0:T(8,128)(2,1)S(1)} %get-tuple-element.51), channel_id=1, source_target_pairs={{0,48},{8,56},{16,32},{24,40},{32,16},{40,24},{48,0},{56,8},{64,11... | collective-permute-start | bytes 393224 | tf_op jit(solution)/shard_map/ppermute | solution.py:417

commit v5 on v3

--- a/solution.py
+++ b/solution.py
@@ -17,7 +17,9 @@
 EXTRA = 16
 PAY = TOK + EXTRA
 YS = 4
+TILE = (0, 2, 8, 10)
 ZS = 8
+WIDE = GROUP * HD
 QT = YS * TOK
 KT = 2 * TOK
 SCALE = HD**-0.5
@@ -37,7 +39,7 @@
 
 
 def pack_kernel(
-    order_hbm, seg_hbm, q_hbm, k_hbm, v_hbm, o_hbm, g_hbm, kvp_hbm, qp_ref, gp_ref,
+    order_hbm, seg_hbm, q_hbm, k_hbm, v_hbm, o_hbm, g_hbm, kvp_hbm, qp_ref,
     order_ref, seg_ref, kv_ref, o_ref, in_sems, out_sems,
 ):
     moves = (
@@ -45,8 +47,8 @@
         (seg_hbm, seg_ref),
         (k_hbm, kv_ref.at[0:TOK, 0:HD]),
         (v_hbm, kv_ref.at[0:TOK, HD : 2 * HD]),
-        (q_hbm, qp_ref.at[0:TOK]),
-        (g_hbm, gp_ref.at[0:TOK]),
+        (q_hbm, qp_ref.at[0:TOK, 0:WIDE]),
+        (g_hbm, qp_ref.at[0:TOK, WIDE : 2 * WIDE]),
         (o_hbm, o_ref),
     )
     copies = [
@@ -71,19 +73,16 @@
     highs, lows = [], []
     for h in range(GROUP):
         cols = slice(h * HD, (h + 1) * HD)
-        prod = gp_ref[0:TOK, cols].astype(F32) * o_ref[:, cols].astype(F32)
+        prod = qp_ref[0:TOK, WIDE + h * HD : WIDE + (h + 1) * HD].astype(F32) * o_ref[:, cols].astype(F32)
         delta = jnp.sum(prod.T, axis=0, keepdims=True)
         high = delta.astype(BF16).astype(F32)
         highs.append(high)
         lows.append(delta - high)
     zero = jnp.zeros_like(doc)
-    q_extra = jnp.concatenate([doc, block, zero, zero], axis=1)
-    qp_ref[TOK:PAY, :] = jnp.broadcast_to(q_extra, (EXTRA, GROUP * HD)).astype(BF16)
-    row = lax.broadcasted_iota(jnp.int32, (EXTRA, GROUP * HD), 0)
-    g_extra = jnp.where(
-        row == 0, jnp.concatenate(highs, axis=1), jnp.concatenate(lows, axis=1)
-    )
-    gp_ref[TOK:PAY, :] = g_extra.astype(BF16)
+    first = jnp.concatenate(highs + lows, axis=1)
+    second = jnp.concatenate([doc, block] + [zero] * 6, axis=1)
+    row = lax.broadcasted_iota(jnp.int32, (EXTRA, 2 * WIDE), 0)
+    qp_ref[TOK:PAY, :] = jnp.where(row == 0, first, second).astype(BF16)
     for copy in outs:
         copy.wait()
 
@@ -98,7 +97,7 @@
     kv_ref, *rest = refs
     q_refs, rest = rest[:YS], rest[YS:]
     if n_prev:
-        y_ref, prev_ref, pt_ref, st_ref, fin_ref, qs, code, bias, keep = rest
+        place_ref, prev_ref, pt_ref, st_ref, fin_ref, qs, code, bias, keep = rest
     else:
         pt_ref, st_ref, qs, code, bias = rest
     step = pl.program_id(0)
@@ -110,7 +109,7 @@
             for h in range(GROUP):
                 qs[h, toks, :] = q_ref[0:TOK, h * HD : (h + 1) * HD]
             info = q_ref[TOK:PAY, :].astype(F32)
-            doc, block = info[0:1, 0:TOK], info[0:1, TOK : 2 * TOK]
+            doc, block = info[1:2, 0:TOK], info[1:2, TOK : 2 * TOK]
             code[0:1, toks] = code_of(doc, block)
             code[1:2, toks] = doc * TOKENS
 
@@ -141,12 +140,12 @@
             for d in range(YS):
                 for x in range(YS):
                     to, of = slice(x * TOK, (x + 1) * TOK), slice((x ^ d) * TOK, ((x ^ d) + 1) * TOK)
-                    fin_ref[y_ref[0] ^ d, 0:GROUP, to] = top[:, of]
-                    fin_ref[y_ref[0] ^ d, GROUP : 2 * GROUP, to] = total[:, of]
+                    fin_ref[place_ref[0] ^ d, 0:GROUP, to] = top[:, of]
+                    fin_ref[place_ref[0] ^ d, GROUP : 2 * GROUP, to] = total[:, of]
 
 
 def grad_kernel(last, kv_ref, pt_ref, st_ref, all_ref, *rest):
-    q_refs, g_refs, rest = rest[:YS], rest[YS : 2 * YS], rest[2 * YS :]
+    q_refs, rest = rest[:YS], rest[YS:]
     if last:
         dq_in, dkv_ref, own_ref, send1, send2, send3, qs, gs, delta, dq = rest
     else:
@@ -155,14 +154,15 @@
 
     @pl.when(step == 0)
     def _():
-        for x, (q_ref, g_ref) in enumerate(zip(q_refs, g_refs)):
+        for x, q_ref in enumerate(q_refs):
             toks = slice(x * TOK, (x + 1) * TOK)
-            info = g_ref[TOK:PAY, :].astype(F32)
+            info = q_ref[TOK:PAY, :].astype(F32)
             for h in range(GROUP):
-                cols = slice(h * HD, (h + 1) * HD)
-                qs[h, toks, :] = q_ref[0:TOK, cols]
-                gs[h, toks, :] = g_ref[0:TOK, cols]
-                delta[h : h + 1, toks] = info[0:1, cols] + info[1:2, cols]
+                qs[h, toks, :] = q_ref[0:TOK, h * HD : (h + 1) * HD]
+                gs[h, toks, :] = q_ref[0:TOK, WIDE + h * HD : WIDE + (h + 1) * HD]
+                high = info[0:1, h * TOK : (h + 1) * TOK]
+                low = info[0:1, (GROUP + h) * TOK : (GROUP + h + 1) * TOK]
+                delta[h : h + 1, toks] = high + low
         dq[...] = dq_in[...] if last else jnp.zeros_like(dq)
 
     top = functools.reduce(jnp.maximum, [all_ref[y, 0:GROUP] for y in range(YS)])
@@ -215,12 +215,11 @@
 def pack(order, seg, q, k, v, o, g):
     hbm = pl.BlockSpec(memory_space=pltpu.HBM)
     vm = pl.BlockSpec(memory_space=pltpu.VMEM)
-    pay = shape_of((PAY, GROUP * HD), BF16)
     return pl.pallas_call(
         pack_kernel,
-        out_shape=(shape_of((ZS, PAY, 2 * HD), BF16), pay, pay),
+        out_shape=(shape_of((ZS, PAY, 2 * HD), BF16), shape_of((PAY, 2 * WIDE), BF16)),
         in_specs=[hbm] * 7,
-        out_specs=(hbm, vm, vm),
+        out_specs=(hbm, vm),
         scratch_shapes=[
             pltpu.SMEM((2,), jnp.int32),
             pltpu.VMEM((1, TOK), jnp.int32),
@@ -238,9 +237,9 @@
 PAIRS = ZS * TOK * GROUP * QT
 
 
-def scores(kv, queries, prev=None, y_index=None):
+def scores(kv, queries, prev=None, place=None):
     in_specs = [pl.BlockSpec((2, PAY, 2 * HD), lambda i: (i, 0, 0))]
-    in_specs += [whole((PAY, GROUP * HD))] * YS
+    in_specs += [whole((PAY, 2 * WIDE))] * YS
     args = [kv, *queries]
     out_shape = [
         shape_of((ZS * TOK, GROUP * QT), BF16),
@@ -257,7 +256,7 @@
     ]
     if prev is not None:
         in_specs += [pl.BlockSpec(memory_space=pltpu.SMEM), whole(prev.shape)]
-        args += [y_index, prev]
+        args += [place, prev]
         out_shape.append(shape_of((YS, 2 * GROUP, QT), F32))
         out_specs.append(whole((YS, 2 * GROUP, QT)))
         scratch.append(pltpu.VMEM((STEPS, 2 * GROUP, QT), F32))
@@ -276,15 +275,15 @@
     )(*args)
 
 
-def grads(kv, probs, stats, all_stats, queries, outs, dq_in=None):
+def grads(kv, probs, stats, all_stats, queries, dq_in=None):
     last = dq_in is not None
     in_specs = [
         pl.BlockSpec((2, PAY, 2 * HD), lambda i: (i, 0, 0)),
         pl.BlockSpec((KT, GROUP * QT), lambda i: (i, 0)),
         pl.BlockSpec((1, 2 * GROUP, QT), lambda i: (i, 0, 0)),
         whole((YS, 2 * GROUP, QT)),
-    ] + [whole((PAY, GROUP * HD))] * (2 * YS)
-    args = [kv, probs, stats, all_stats, *queries, *outs]
+    ] + [whole((PAY, 2 * WIDE))] * YS
+    args = [kv, probs, stats, all_stats, *queries]
     dkv_type = F32 if last else BF16
     out_shape = [shape_of((ZS, TOK, 2 * HD), dkv_type)]
     out_specs = [pl.BlockSpec((2, TOK, 2 * HD), lambda i: (i, 0, 0))]
@@ -321,9 +320,13 @@
 
 def per_device(query, key_rows, value_rows, output, grad_out, block_order, segment):
     n = lax.axis_size("ctx")
-    z_groups = [[z * 2 * YS + r for z in range(ZS)] for r in range(2 * YS)]
-    y_groups = [
-        [z * 2 * YS + y * 2 + c for y in range(YS)] for z in range(ZS) for c in range(2)
+    near = [c + 2 * y + 8 * z for z in range(2) for y in range(2) for c in range(2)]
+    key_groups = [[r + 4 * y + 16 * z for z in range(4) for y in range(2)] for r in near]
+    tile_groups = [
+        [c + 4 * y + 16 * z + bits for bits in TILE]
+        for z in range(4)
+        for y in range(2)
+        for c in range(2)
     ]
 
     def swap(x, bits):
@@ -332,26 +335,24 @@
     def exchange(x, groups):
         return lax.all_to_all(x, "ctx", 0, 0, tiled=True, axis_index_groups=groups)
 
-    kv_pay, q_pay, g_pay = pack(
+    kv_pay, q_pay = pack(
         block_order, segment.reshape(1, TOK), query, key_rows, value_rows, output, grad_out
     )
-    kv_own = exchange(kv_pay, z_groups)
-    q_far, q_near = swap(q_pay, 4), swap(q_pay, 2)
-    g_far, g_near = swap(g_pay, 4), swap(g_pay, 2)
-    queries = [q_pay, q_near, q_far, swap(q_far, 2)]
-    outs = [g_pay, g_near, g_far, swap(g_far, 2)]
-    kv_own, queries, outs = lax.optimization_barrier((kv_own, queries, outs))
+    kv_own = exchange(kv_pay, key_groups)
+    queries = [q_pay] + [swap(q_pay, bits) for bits in TILE[1:]]
+    kv_own, queries = lax.optimization_barrier((kv_own, queries))
     kv_twin = swap(kv_own, 1)
     p_own, st_own = scores(kv_own, queries)
-    y_index = (lax.axis_index("ctx") // 2 % YS).astype(jnp.int32).reshape(1)
-    p_twin, st_twin, stats = scores(kv_twin, queries, st_own, y_index)
-    all_stats = exchange(stats, y_groups)
-    dkv_twin, dq = grads(kv_twin, p_twin, st_twin, all_stats, queries, outs)
+    index = lax.axis_index("ctx").astype(jnp.int32)
+    place = ((index >> 1 & 1) + 2 * (index >> 3 & 1)).reshape(1)
+    p_twin, st_twin, stats = scores(kv_twin, queries, st_own, place)
+    all_stats = exchange(stats, tile_groups)
+    dkv_twin, dq = grads(kv_twin, p_twin, st_twin, all_stats, queries)
     dkv_back = swap(dkv_twin, 1)
-    dkv_own, dq_own, *dq_send = grads(kv_own, p_own, st_own, all_stats, queries, outs, dq)
+    dkv_own, dq_own, *dq_send = grads(kv_own, p_own, st_own, all_stats, queries, dq)
     dkv = (dkv_own + dkv_back.astype(F32)).astype(BF16)
-    dkv_all = exchange(dkv, z_groups)
-    dq_parts = [swap(part, 2 * x) for x, part in enumerate(dq_send, 1)]
+    dkv_all = exchange(dkv, key_groups)
+    dq_parts = [swap(part, bits) for part, bits in zip(dq_send, TILE[1:])]
     grad_query = dq_own + sum(part.astype(F32) for part in dq_parts)
     grad_kv = jnp.sum(dkv_all.astype(F32), axis=0).astype(BF16)
     return grad_query.astype(BF16), grad_kv[:, 0:HD], grad_kv[:, HD : 2 * HD]

time: 106 us -> 106 us (level)
  waiting for transfers between devices: 14.5 us -> 29.4 us
  starting transfers between devices: 53.8 us -> 44.3 us
  blocking collectives: 10.8 us -> 6.45 us
    ppermute x11 -> x8, waiting for transfers between devices: 13 us -> 29.4 us  [swap(): return lax.ppermute(x, 'ctx', [(i, i ^ bits) for i in range(n)])]
    ppermute x11 -> x8, starting transfers between devices: 36.4 us -> 23.3 us  [swap(): return lax.ppermute(x, 'ctx', [(i, i ^ bits) for i in range(n)])]
    all_to_all x1, blocking collectives: 10.8 us -> 6.45 us  [exchange(): return lax.all_to_all(x, 'ctx', 0, 0, tiled=True, axis_index_groups=groups)]
    all_to_all x2, starting transfers between devices: 17.5 us -> 21 us  [exchange(): return lax.all_to_all(x, 'ctx', 0, 0, tiled=True, axis_index_groups=groups)]
    all_to_all x2, waiting for transfers between devices: 1.5 us -> 0.01 us  [exchange(): return lax.all_to_all(x, 'ctx', 0, 0, tiled=True, axis_index_groups=groups)]
  transfers between devices with their start and end apart: 13 -> 10, of which waited for: 5 -> 5; matrix products, arithmetic and copies ran while one was open for 1% -> 1% of each run, Pallas kernels for 9% -> 9%
where the time goes in v5:
time: 106 us; the launch traced here: 105 us
  starting transfers between devices  44.3 us (42%)
  waiting for transfers between devices  29.4 us (28%)
  Pallas kernels  20.8 us (20%)
  blocking collectives  6.45 us (6%)
  other arithmetic  1.71 us (2%)
  local copies, waits for them, and re-layouts  1.59 us (2%)
    ppermute x8, waiting for transfers between devices, swap(): return lax.ppermute(x, 'ctx', [(i, i ^ bits) for i in range(n)])  29.4 us
    ppermute x8, starting transfers between devices, swap(): return lax.ppermute(x, 'ctx', [(i, i ^ bits) for i in range(n)])  23.3 us
    all_to_all x2, starting transfers between devices, exchange(): return lax.all_to_all(x, 'ctx', 0, 0, tiled=True, axis_index_groups=groups)  21 us
    pallas_call x2, Pallas kernels, grads(): pl.pallas_call(functools.partial(grad_kernel, last), grid=(STEPS,), in_sp...  11.2 us
    pallas_call x2, Pallas kernels, scores(): pl.pallas_call(functools.partial(score_kernel, 0 if prev is None else STE...  7.18 us
    all_to_all x1, blocking collectives, exchange(): return lax.all_to_all(x, 'ctx', 0, 0, tiled=True, axis_index_groups=groups)  6.45 us
    pallas_call x1, Pallas kernels, pack(): pl.pallas_call(pack_kernel, out_shape=(shape_of((ZS, PAY, 2 * HD), BF16),...  2.45 us
  transfers between devices with their start and end apart: 10, of which 5 were waited for; matrix products, arithmetic and copies ran while one was open for 1% of the time, Pallas kernels for 9%

profile of v5, /device:TPU:1, one launch (start us, length us, event | category | flops | bytes accessed | tf_op | source)
XLA Modules:
  0.0 104.9 jit_solution(10477957357656175520)
XLA Ops:
  0.6 2.5 %pack.1 = (bf16[8,144,256]{2,1,0:T(8,128)(2,1)}, bf16[144,1024]{1,0:T(8,128)(2,1)}) custom-call(s32[2]{0:T(128)} %order_hbm.1, s32[1,128]{1,0:T(1,128)} %bitcast.2, bf16[128,512]{1,0:T(8,128)(2,1)} %q_hbm.1, bf16[128,128]{1,0:T(8,128)(2,1)} %k_hbm.1, bf16[128,128]{1,0:T(8,128)(2,1)} %v_hbm.1, bf16[128,512]{1,0:T(8,128)(2,1)} %o_hbm.1, bf16[128,512]{1,0:T(8,128)(2,1)} %g_hbm.1), custom_call_target="tpu_custom_call" | custom-call | tf_op jit(solution)/shard_map/pack/pallas_call | solution.py:218
  3.1 12.9 %all-to-all-start = ((bf16[8,144,256]{2,1,0:T(8,128)(2,1)}), bf16[8,144,256]{2,1,0:T(8,128)(2,1)S(1)}, u32[]{:S(2)}, u32[]{:S(2)}) async-start(bf16[8,144,256]{2,1,0:T(8,128)(2,1)} %get-tuple-element.22), calls=%async_computation | async-start | bytes 1179648 | tf_op jit(solution)/shard_map/all_to_all | solution.py:336
  16.0 4.1 %collective-permute-start.2 = (bf16[144,1024]{1,0:T(8,128)(2,1)}, bf16[144,1024]{1,0:T(8,128)(2,1)S(1)}, u32[]{:S(2)}, u32[]{:S(2)}) collective-permute-start(bf16[144,1024]{1,0:T(8,128)(2,1)} %get-tuple-element.25.refs_1_.rest_0_), channel_id=1, source_target_pairs={{0,80},{8,88},{16,64},{24,72},{32,112},{40,120},{48,96},{56,104},{... | collective-permute-start | bytes 884744 | tf_op jit(solution)/shard_map/ppermute | solution.py:333
  20.1 2.2 %collective-permute-start.1 = (bf16[144,1024]{1,0:T(8,128)(2,1)}, bf16[144,1024]{1,0:T(8,128)(2,1)S(1)}, u32[]{:S(2)}, u32[]{:S(2)}) collective-permute-start(bf16[144,1024]{1,0:T(8,128)(2,1)} %get-tuple-element.25.refs_1_.rest_0_), channel_id=1, source_target_pairs={{0,64},{8,72},{16,80},{24,88},{32,96},{40,104},{48,112},{56,120},{... | collective-permute-start | bytes 884744 | tf_op jit(solution)/shard_map/ppermute | solution.py:333
  22.3 2.1 %collective-permute-start = (bf16[144,1024]{1,0:T(8,128)(2,1)}, bf16[144,1024]{1,0:T(8,128)(2,1)S(1)}, u32[]{:S(2)}, u32[]{:S(2)}) collective-permute-start(bf16[144,1024]{1,0:T(8,128)(2,1)} %get-tuple-element.25.refs_1_.rest_0_), channel_id=1, source_target_pairs={{0,16},{8,24},{16,0},{24,8},{32,48},{40,56},{48,32},{56,40},{64,80... | collective-permute-start | bytes 884744 | tf_op jit(solution)/shard_map/ppermute | solution.py:333
  24.4 10.9 %collective-permute-done.2.refs_4_.rest_3_ = bf16[144,1024]{1,0:T(8,128)(2,1)S(1)} collective-permute-done((bf16[144,1024]{1,0:T(8,128)(2,1)}, bf16[144,1024]{1,0:T(8,128)(2,1)S(1)}, u32[]{:S(2)}, u32[]{:S(2)}) %collective-permute-start.2) | collective-permute-done | bytes 294944 | tf_op jit(solution)/shard_map/ppermute | solution.py:333
  35.2 7.7 %collective-permute-done.1.refs_3_.rest_2_ = bf16[144,1024]{1,0:T(8,128)(2,1)S(1)} collective-permute-done((bf16[144,1024]{1,0:T(8,128)(2,1)}, bf16[144,1024]{1,0:T(8,128)(2,1)S(1)}, u32[]{:S(2)}, u32[]{:S(2)}) %collective-permute-start.1) | collective-permute-done | bytes 294944 | tf_op jit(solution)/shard_map/ppermute | solution.py:333
  43.0 0.0 collective-permute-done.refs_2_.rest_1_
  43.0 0.0 all-to-all-done.refs_0_.kv_ref
  43.0 3.2 %collective-permute-start.3 = (bf16[8,144,256]{2,1,0:T(8,128)(2,1)S(1)}, bf16[8,144,256]{2,1,0:T(8,128)(2,1)S(1)}, u32[]{:S(2)}, u32[]{:S(2)}) collective-permute-start(bf16[8,144,256]{2,1,0:T(8,128)(2,1)S(1)} %all-to-all-done.refs_0_.kv_ref), channel_id=1, source_target_pairs={{0,8},{8,0},{16,24},{24,16},{32,40},{40,32},{48,56},{56,48},{64,72... | collective-permute-start | bytes 1769480 | tf_op jit(solution)/shard_map/ppermute | solution.py:333
  46.2 0.0 copy-start
  46.2 1.0 copy-done
  47.2 3.5 %scores.2 = (bf16[1024,2048]{1,0:T(8,128)(2,1)S(1)}, f32[4,8,512]{2,1,0:T(8,128)S(1)}) custom-call(bf16[8,144,256]{2,1,0:T(8,128)(2,1)S(1)} %all-to-all-done.refs_0_.kv_ref, bf16[144,1024]{1,0:T(8,128)(2,1)S(1)} %copy-done, bf16[144,1024]{1,0:T(8,128)(2,1)S(1)} %collective-permute-done.refs_2_.rest_1_, ...), custom_call_target="tpu_custom_call" | custom-call | flops 2097152 | bytes 65536 | tf_op jit(solution)/shard_map/scores/pallas_call | solution.py:263
  50.7 0.0 collective-permute-done.3.refs_0_.kv_ref
  50.8 3.6 %scores.3 = (bf16[1024,2048]{1,0:T(8,128)(2,1)S(1)}, f32[4,8,512]{2,1,0:T(8,128)S(1)}, f32[4,8,512]{2,1,0:T(8,128)S(1)}) custom-call(bf16[8,144,256]{2,1,0:T(8,128)(2,1)S(1)} %collective-permute-done.3.refs_0_.kv_ref, bf16[144,1024]{1,0:T(8,128)(2,1)S(1)} %copy-done, bf16[144,1024]{1,0:T(8,128)(2,1)S(1)} %collective-permute-done.refs_2_.rest_1_, ...), custom_call_target="tpu_custom_call" | custom-call | flops 2097152 | bytes 65536 | tf_op jit(solution)/shard_map/scores/pallas_call | solution.py:263
  54.4 6.4 %all_to_all.15.all_ref = f32[4,8,512]{2,1,0:T(8,128)S(1)} all-to-all(f32[4,8,512]{2,1,0:T(8,128)S(1)} %get-tuple-element.31), channel_id=1, replica_groups={{0,16,64,80},{8,24,72,88},{32,48,96,112},{40,56,104,120},{128,144,192,2..., dimensions={0} | all-to-all | bytes 131072 | tf_op jit(solution)/shard_map/all_to_all | solution.py:336
  60.8 5.4 %grads.2 = (bf16[8,128,256]{2,1,0:T(8,128)(2,1)S(1)}, f32[4,128,512]{2,1,0:T(8,128)S(1)}) custom-call(bf16[8,144,256]{2,1,0:T(8,128)(2,1)S(1)} %collective-permute-done.3.refs_0_.kv_ref, bf16[1024,2048]{1,0:T(8,128)(2,1)S(1)} %get-tuple-element.32.pt_ref, f32[4,8,512]{2,1,0:T(8,128)S(1)} %get-tuple-element.33.st_ref, f32[4,8,512]{2,1,0:T(8,128)S(1)} %all_to_all.15.all_ref, ...), custom_call_target="tpu_custom_call" | custom-call | flops 4294967296 | bytes 4194304 | tf_op jit(solution)/shard_map/grads/pallas_call | solution.py:306
  66.2 3.3 %collective-permute-start.7 = (bf16[8,128,256]{2,1,0:T(8,128)(2,1)S(1)}, bf16[8,128,256]{2,1,0:T(8,128)(2,1)S(1)}, u32[]{:S(2)}, u32[]{:S(2)}) collective-permute-start(bf16[8,128,256]{2,1,0:T(8,128)(2,1)S(1)} %get-tuple-element.40), channel_id=1, source_target_pairs={{0,8},{8,0},{16,24},{24,16},{32,40},{40,32},{48,56},{56,48},{64,72... | collective-permute-start | bytes 1572872 | tf_op jit(solution)/shard_map/ppermute | solution.py:333
  69.6 5.8 %grads.3 = (f32[8,128,256]{2,1,0:T(8,128)S(1)}, f32[128,512]{1,0:T(8,128)S(1)}, bf16[128,512]{1,0:T(8,128)(2,1)S(1)}, bf16[128,512]{1,0:T(8,128)(2,1)S(1)}, bf16[128,512]{1,0:T(8,128)(2,1)S(1)}) custom-call(bf16[8,144,256]{2,1,0:T(8,128)(2,1)S(1)} %all-to-all-done.refs_0_.kv_ref, bf16[1024,2048]{1,0:T(8,128)(2,1)S(1)} %get-tuple-element.29.pt_ref, ...), custom_call_target="tpu_custom_call" | custom-call | flops 4294967296 | bytes 4194304 | tf_op jit(solution)/shard_map/grads/pallas_call | solution.py:306
  75.3 0.0 collective-permute-done.7
  75.4 0.9 add_convert_fusion
  76.3 8.1 %all-to-all-start.2 = ((bf16[8,128,256]{2,1,0:T(8,128)(2,1)}), bf16[8,128,256]{2,1,0:T(8,128)(2,1)S(1)}, u32[]{:S(2)}, u32[]{:S(2)}) async-start(bf16[8,128,256]{2,1,0:T(8,128)(2,1)} %add_convert_fusion), calls=%async_computation.2 | async-start | bytes 1048576 | tf_op jit(solution)/shard_map/all_to_all | solution.py:336
  84.4 2.4 %collective-permute-start.4 = (bf16[128,512]{1,0:T(8,128)(2,1)S(1)}, bf16[128,512]{1,0:T(8,128)(2,1)S(1)}, u32[]{:S(2)}, u32[]{:S(2)}) collective-permute-start(bf16[128,512]{1,0:T(8,128)(2,1)S(1)} %get-tuple-element.36), channel_id=1, source_target_pairs={{0,16},{8,24},{16,0},{24,8},{32,48},{40,56},{48,32},{56,40},{64,80... | collective-permute-start | bytes 393224 | tf_op jit(solution)/shard_map/ppermute | solution.py:333
  86.7 2.0 %collective-permute-start.5 = (bf16[128,512]{1,0:T(8,128)(2,1)S(1)}, bf16[128,512]{1,0:T(8,128)(2,1)S(1)}, u32[]{:S(2)}, u32[]{:S(2)}) collective-permute-start(bf16[128,512]{1,0:T(8,128)(2,1)S(1)} %get-tuple-element.37), channel_id=1, source_target_pairs={{0,64},{8,72},{16,80},{24,88},{32,96},{40,104},{48,112},{56,120},{... | collective-permute-start | bytes 393224 | tf_op jit(solution)/shard_map/ppermute | solution.py:333
  88.7 4.0 %collective-permute-start.6 = (bf16[128,512]{1,0:T(8,128)(2,1)S(1)}, bf16[128,512]{1,0:T(8,128)(2,1)S(1)}, u32[]{:S(2)}, u32[]{:S(2)}) collective-permute-start(bf16[128,512]{1,0:T(8,128)(2,1)S(1)} %get-tuple-element.38), channel_id=1, source_target_pairs={{0,80},{8,88},{16,64},{24,72},{32,112},{40,120},{48,96},{56,104},{... | collective-permute-start | bytes 393224 | tf_op jit(solution)/shard_map/ppermute | solution.py:333
  92.7 1.4 %collective-permute-done.4 = bf16[128,512]{1,0:T(8,128)(2,1)S(1)} collective-permute-done((bf16[128,512]{1,0:T(8,128)(2,1)S(1)}, bf16[128,512]{1,0:T(8,128)(2,1)S(1)}, u32[]{:S(2)}, u32[]{:S(2)}) %collective-permute-start.4) | collective-permute-done | bytes 131104 | tf_op jit(solution)/shard_map/ppermute | solution.py:333
  94.1 4.3 %collective-permute-done.5 = bf16[128,512]{1,0:T(8,128)(2,1)S(1)} collective-permute-done((bf16[128,512]{1,0:T(8,128)(2,1)S(1)}, bf16[128,512]{1,0:T(8,128)(2,1)S(1)}, u32[]{:S(2)}, u32[]{:S(2)}) %collective-permute-start.5) | collective-permute-done | bytes 131104 | tf_op jit(solution)/shard_map/ppermute | solution.py:333
  98.5 5.1 %collective-permute-done.6 = bf16[128,512]{1,0:T(8,128)(2,1)S(1)} collective-permute-done((bf16[128,512]{1,0:T(8,128)(2,1)S(1)}, bf16[128,512]{1,0:T(8,128)(2,1)S(1)}, u32[]{:S(2)}, u32[]{:S(2)}) %collective-permute-start.6) | collective-permute-done | bytes 131104 | tf_op jit(solution)/shard_map/ppermute | solution.py:333
  103.5 0.7 add_convert_fusion.1
  104.2 0.0 all-to-all-done.2
  104.2 0.1 reduce_sum.12
  104.3 0.6 fusion
Async XLA Ops:
  3.1 39.9 %all-to-all-start = ((bf16[8,144,256]{2,1,0:T(8,128)(2,1)}), bf16[8,144,256]{2,1,0:T(8,128)(2,1)S(1)}, u32[]{:S(2)}, u32[]{:S(2)}) async-start(bf16[8,144,256]{2,1,0:T(8,128)(2,1)} %get-tuple-element.22), calls=%async_computation | async-start | bytes 1179648 | tf_op jit(solution)/shard_map/all_to_all | solution.py:336
  16.0 19.2 %collective-permute-start.2 = (bf16[144,1024]{1,0:T(8,128)(2,1)}, bf16[144,1024]{1,0:T(8,128)(2,1)S(1)}, u32[]{:S(2)}, u32[]{:S(2)}) collective-permute-start(bf16[144,1024]{1,0:T(8,128)(2,1)} %get-tuple-element.25.refs_1_.rest_0_), channel_id=1, source_target_pairs={{0,80},{8,88},{16,64},{24,72},{32,112},{40,120},{48,96},{56,104},{... | collective-permute-start | bytes 884744 | tf_op jit(solution)/shard_map/ppermute | solution.py:333
  20.1 22.9 %collective-permute-start.1 = (bf16[144,1024]{1,0:T(8,128)(2,1)}, bf16[144,1024]{1,0:T(8,128)(2,1)S(1)}, u32[]{:S(2)}, u32[]{:S(2)}) collective-permute-start(bf16[144,1024]{1,0:T(8,128)(2,1)} %get-tuple-element.25.refs_1_.rest_0_), channel_id=1, source_target_pairs={{0,64},{8,72},{16,80},{24,88},{32,96},{40,104},{48,112},{56,120},{... | collective-permute-start | bytes 884744 | tf_op jit(solution)/shard_map/ppermute | solution.py:333
  22.3 20.7 %collective-permute-start = (bf16[144,1024]{1,0:T(8,128)(2,1)}, bf16[144,1024]{1,0:T(8,128)(2,1)S(1)}, u32[]{:S(2)}, u32[]{:S(2)}) collective-permute-start(bf16[144,1024]{1,0:T(8,128)(2,1)} %get-tuple-element.25.refs_1_.rest_0_), channel_id=1, source_target_pairs={{0,16},{8,24},{16,0},{24,8},{32,48},{40,56},{48,32},{56,40},{64,80... | collective-permute-start | bytes 884744 | tf_op jit(solution)/shard_map/ppermute | solution.py:333
  43.0 7.8 %collective-permute-start.3 = (bf16[8,144,256]{2,1,0:T(8,128)(2,1)S(1)}, bf16[8,144,256]{2,1,0:T(8,128)(2,1)S(1)}, u32[]{:S(2)}, u32[]{:S(2)}) collective-permute-start(bf16[8,144,256]{2,1,0:T(8,128)(2,1)S(1)} %all-to-all-done.refs_0_.kv_ref), channel_id=1, source_target_pairs={{0,8},{8,0},{16,24},{24,16},{32,40},{40,32},{48,56},{56,48},{64,72... | collective-permute-start | bytes 1769480 | tf_op jit(solution)/shard_map/ppermute | solution.py:333
  46.2 1.0 copy-start
  66.2 9.1 %collective-permute-start.7 = (bf16[8,128,256]{2,1,0:T(8,128)(2,1)S(1)}, bf16[8,128,256]{2,1,0:T(8,128)(2,1)S(1)}, u32[]{:S(2)}, u32[]{:S(2)}) collective-permute-start(bf16[8,128,256]{2,1,0:T(8,128)(2,1)S(1)} %get-tuple-element.40), channel_id=1, source_target_pairs={{0,8},{8,0},{16,24},{24,16},{32,40},{40,32},{48,56},{56,48},{64,72... | collective-permute-start | bytes 1572872 | tf_op jit(solution)/shard_map/ppermute | solution.py:333
  76.3 28.0 %all-to-all-start.2 = ((bf16[8,128,256]{2,1,0:T(8,128)(2,1)}), bf16[8,128,256]{2,1,0:T(8,128)(2,1)S(1)}, u32[]{:S(2)}, u32[]{:S(2)}) async-start(bf16[8,128,256]{2,1,0:T(8,128)(2,1)} %add_convert_fusion), calls=%async_computation.2 | async-start | bytes 1048576 | tf_op jit(solution)/shard_map/all_to_all | solution.py:336
  84.4 9.8 %collective-permute-start.4 = (bf16[128,512]{1,0:T(8,128)(2,1)S(1)}, bf16[128,512]{1,0:T(8,128)(2,1)S(1)}, u32[]{:S(2)}, u32[]{:S(2)}) collective-permute-start(bf16[128,512]{1,0:T(8,128)(2,1)S(1)} %get-tuple-element.36), channel_id=1, source_target_pairs={{0,16},{8,24},{16,0},{24,8},{32,48},{40,56},{48,32},{56,40},{64,80... | collective-permute-start | bytes 393224 | tf_op jit(solution)/shard_map/ppermute | solution.py:333
  86.7 11.7 %collective-permute-start.5 = (bf16[128,512]{1,0:T(8,128)(2,1)S(1)}, bf16[128,512]{1,0:T(8,128)(2,1)S(1)}, u32[]{:S(2)}, u32[]{:S(2)}) collective-permute-start(bf16[128,512]{1,0:T(8,128)(2,1)S(1)} %get-tuple-element.37), channel_id=1, source_target_pairs={{0,64},{8,72},{16,80},{24,88},{32,96},{40,104},{48,112},{56,120},{... | collective-permute-start | bytes 393224 | tf_op jit(solution)/shard_map/ppermute | solution.py:333
  88.7 14.8 %collective-permute-start.6 = (bf16[128,512]{1,0:T(8,128)(2,1)S(1)}, bf16[128,512]{1,0:T(8,128)(2,1)S(1)}, u32[]{:S(2)}, u32[]{:S(2)}) collective-permute-start(bf16[128,512]{1,0:T(8,128)(2,1)S(1)} %get-tuple-element.38), channel_id=1, source_target_pairs={{0,80},{8,88},{16,64},{24,72},{32,112},{40,120},{48,96},{56,104},{... | collective-permute-start | bytes 393224 | tf_op jit(solution)/shard_map/ppermute | solution.py:333

commit v6 on v5

v6 whole, which is shorter than its diff:
```python
import functools

import jax
import jax.numpy as jnp
from jax import lax
from jax.experimental import pallas as pl
from jax.experimental.pallas import tpu as pltpu
from jax.sharding import PartitionSpec as P

HEADS = 32
KV_HEADS = 8
HD = 128
GROUP = HEADS // KV_HEADS
BLK = 64
TOKENS = 8192
TOK = 128
EXTRA = 16
PAY = TOK + EXTRA
YS = 4
TILE = (0, 2, 8, 10)
ZS = 8
WIDE = GROUP * HD
QT = YS * TOK
KT = 2 * TOK
SCALE = HD**-0.5
EXP2 = SCALE * 1.4426950408889634
MASKED = -1e30
FLOOR = -1e25
F32 = jnp.float32
BF16 = jnp.bfloat16
VMEM_LIMIT = 24

NT = (((1,), (1,)), ((), ()))
TN = (((0,), (0,)), ((), ()))


def dot(a, b, dims=(((1,), (0,)), ((), ()))):
    return lax.dot_general(a, b, dims, preferred_element_type=F32)


def pack_kernel(
    order_hbm, seg_hbm, q_hbm, k_hbm, v_hbm, o_hbm, g_hbm, kvp_hbm, qp_ref,
    order_ref, seg_ref, kv_ref, o_ref, in_sems, out_sems,
):
    moves = (
        (order_hbm, order_ref),
        (seg_hbm, seg_ref),
        (k_hbm, kv_ref.at[0:TOK, 0:HD]),
        (v_hbm, kv_ref.at[0:TOK, HD : 2 * HD]),
        (q_hbm, qp_ref.at[0:TOK, 0:WIDE]),
        (g_hbm, qp_ref.at[0:TOK, WIDE : 2 * WIDE]),
        (o_hbm, o_ref),
    )
    copies = [
        pltpu.make_async_copy(src, dst, in_sems.at[i]) for i, (src, dst) in enumerate(moves)
    ]
    for copy in copies:
        copy.start()
    for copy in copies[:4]:
        copy.wait()
    lane = lax.broadcasted_iota(jnp.int32, (1, TOK), 1)
    block = jnp.where(lane < BLK, order_ref[0], order_ref[1]).astype(F32)
    doc = seg_ref[...].astype(F32)
    kv_extra = jnp.concatenate([doc, block], axis=1)
    kv_ref[TOK:PAY, :] = jnp.broadcast_to(kv_extra, (EXTRA, 2 * HD)).astype(BF16)
    outs = [
        pltpu.make_async_copy(kv_ref, kvp_hbm.at[z], out_sems.at[z]) for z in range(ZS)
    ]
    for copy in outs:
        copy.start()
    for copy in copies[4:]:
        copy.wait()
    highs, lows = [], []
    for h in range(GROUP):
        cols = slice(h * HD, (h + 1) * HD)
        prod = qp_ref[0:TOK, WIDE + h * HD : WIDE + (h + 1) * HD].astype(F32) * o_ref[:, cols].astype(F32)
        delta = jnp.sum(prod.T, axis=0, keepdims=True)
        high = delta.astype(BF16).astype(F32)
        highs.append(high)
        lows.append(delta - high)
    zero = jnp.zeros_like(doc)
    first = jnp.concatenate(highs + lows, axis=1)
    second = jnp.concatenate([doc, block] + [zero] * 6, axis=1)
    row = lax.broadcasted_iota(jnp.int32, (EXTRA, 2 * WIDE), 0)
    qp_ref[TOK:PAY, :] = jnp.where(row == 0, first, second).astype(BF16)
    for copy in outs:
        copy.wait()


def code_of(doc, block):
    lane = lax.broadcasted_iota(jnp.int32, doc.shape, 1)
    within = jnp.where(lane < BLK, lane, lane - BLK).astype(F32)
    return doc * TOKENS + block * BLK + within


def score_kernel(n_q, last, kv_ref, *refs):
    q_refs, refs = refs[:n_q], refs[n_q:]
    if last:
        place_ref, near_ref, far_ref, pt_ref, st_ref, fin_ref, qs, code, bias = refs
    else:
        pt_ref, st_ref, qs, code, bias = refs
    width = n_q * TOK
    for x, q_ref in enumerate(q_refs):
        toks = slice(x * TOK, (x + 1) * TOK)
        for h in range(GROUP):
            qs[h, toks, :] = q_ref[0:TOK, h * HD : (h + 1) * HD]
        info = q_ref[TOK:PAY, :].astype(F32)
        doc, block = info[1:2, 0:TOK], info[1:2, TOK : 2 * TOK]
        code[0:1, toks] = code_of(doc, block)
        code[1:2, toks] = doc * TOKENS

    for step in range(STEPS):
        for b in range(2):
            info = kv_ref[2 * step + b, TOK:PAY, :].astype(F32)
            key_code = code_of(info[0:1, 0:TOK], info[0:1, TOK : 2 * TOK])
            key_code = jnp.broadcast_to(key_code, (TOK, TOK)).T
            for x in range(n_q):
                toks = slice(x * TOK, (x + 1) * TOK)
                ok = (key_code <= code[0:1, toks]) & (key_code >= code[1:2, toks])
                bias[step % 2, b * TOK : (b + 1) * TOK, toks] = jnp.where(ok, 0.0, MASKED)
        rows = slice(step * KT, (step + 1) * KT)
        keys = jnp.concatenate([kv_ref[2 * step + b, 0:TOK, 0:HD] for b in range(2)], axis=0)
        for h in range(GROUP):
            s = dot(keys, qs[h], NT) + bias[step % 2]
            peak = jnp.maximum(jnp.max(s, axis=0, keepdims=True), FLOOR)
            p = jnp.exp2((s - peak) * EXP2)
            st_ref[step, h : h + 1, :] = peak
            st_ref[step, GROUP + h : GROUP + h + 1, :] = jnp.sum(p, axis=0, keepdims=True)
            pt_ref[rows, h * width : (h + 1) * width] = p.astype(BF16)
    if last:
        tiles = [jnp.concatenate([near_ref[t], far_ref[t]], axis=1) for t in range(STEPS)]
        tiles += [st_ref[t] for t in range(STEPS)]
        top = functools.reduce(jnp.maximum, [t[0:GROUP] for t in tiles])
        total = sum(t[GROUP:] * jnp.exp2((t[0:GROUP] - top) * EXP2) for t in tiles)
        for d in range(YS):
            for x in range(YS):
                to, of = slice(x * TOK, (x + 1) * TOK), slice((x ^ d) * TOK, ((x ^ d) + 1) * TOK)
                fin_ref[place_ref[0] ^ d, 0:GROUP, to] = top[:, of]
                fin_ref[place_ref[0] ^ d, GROUP : 2 * GROUP, to] = total[:, of]


def grad_kernel(last, n_parts, kv_ref, all_ref, *refs):
    p_refs, refs = refs[:n_parts], refs[n_parts:]
    st_refs, refs = refs[:n_parts], refs[n_parts:]
    q_refs, refs = refs[:YS], refs[YS:]
    if last:
        dq_in, dkv_ref, own_ref, send1, send2, send3, qs, gs, delta, dq = refs
    else:
        dkv_ref, dq, qs, gs, delta = refs
    for x, q_ref in enumerate(q_refs):
        toks = slice(x * TOK, (x + 1) * TOK)
        info = q_ref[TOK:PAY, :].astype(F32)
        for h in range(GROUP):
            qs[h, toks, :] = q_ref[0:TOK, h * HD : (h + 1) * HD]
            gs[h, toks, :] = q_ref[0:TOK, WIDE + h * HD : WIDE + (h + 1) * HD]
            high = info[0:1, h * TOK : (h + 1) * TOK]
            low = info[0:1, (GROUP + h) * TOK : (GROUP + h + 1) * TOK]
            delta[h : h + 1, toks] = high + low
    dq[...] = dq_in[...] if last else jnp.zeros_like(dq)
    width = QT // n_parts

    top = functools.reduce(jnp.maximum, [all_ref[y, 0:GROUP] for y in range(YS)])
    total = sum(
        all_ref[y, GROUP : 2 * GROUP] * jnp.exp2((all_ref[y, 0:GROUP] - top) * EXP2)
        for y in range(YS)
    )
    for step in range(STEPS):
        rows = slice(step * KT, (step + 1) * KT)
        peaks = jnp.concatenate([st_ref[step, 0:GROUP] for st_ref in st_refs], axis=1)
        weight = jnp.exp2((peaks - top) * EXP2) / total
        pair = [kv_ref[2 * step + b, 0:TOK] for b in range(2)]
        keys = jnp.concatenate([part[:, 0:HD] for part in pair], axis=0)
        values = jnp.concatenate([part[:, HD : 2 * HD] for part in pair], axis=0)
        dk = jnp.zeros((KT, HD), F32)
        dv = jnp.zeros((KT, HD), F32)
        for h in range(GROUP):
            cols = slice(h * width, (h + 1) * width)
            dp = dot(values, gs[h], NT)
            p = jnp.concatenate([p_ref[rows, cols] for p_ref in p_refs], axis=1)
            p = p.astype(F32) * weight[h : h + 1]
            ds = (p * (dp - delta[h : h + 1, :])).astype(BF16)
            dv = dv + dot(p.astype(BF16), gs[h])
            dk = dk + dot(ds, qs[h])
            dq[h] += dot(keys, ds, TN)
        dk = dk * SCALE
        for b in range(2):
            half = slice(b * TOK, (b + 1) * TOK)
            dkv_ref[2 * step + b, :, 0:HD] = dk[half].astype(dkv_ref.dtype)
            dkv_ref[2 * step + b, :, HD : 2 * HD] = dv[half].astype(dkv_ref.dtype)

    if last:
        for x, out in enumerate((own_ref, send1, send2, send3)):
            for h in range(GROUP):
                part = dq[h, :, x * TOK : (x + 1) * TOK].T * SCALE
                out[:, h * HD : (h + 1) * HD] = part.astype(out.dtype)


def shape_of(shape, dtype):
    return jax.ShapeDtypeStruct(shape, dtype)


def params(limit=VMEM_LIMIT):
    return pltpu.CompilerParams(vmem_limit_bytes=limit << 20)


def pack(order, seg, q, k, v, o, g):
    hbm = pl.BlockSpec(memory_space=pltpu.HBM)
    vm = pl.BlockSpec(memory_space=pltpu.VMEM)
    return pl.pallas_call(
        pack_kernel,
        out_shape=(shape_of((ZS, PAY, 2 * HD), BF16), shape_of((PAY, 2 * WIDE), BF16)),
        in_specs=[hbm] * 7,
        out_specs=(hbm, vm),
        scratch_shapes=[
            pltpu.SMEM((2,), jnp.int32),
            pltpu.VMEM((1, TOK), jnp.int32),
            pltpu.VMEM((PAY, 2 * HD), BF16),
            pltpu.VMEM((TOK, GROUP * HD), BF16),
            pltpu.SemaphoreType.DMA((7,)),
            pltpu.SemaphoreType.DMA((ZS,)),
        ],
        compiler_params=params(60),
        name="pack",
    )(order, seg, q, k, v, o, g)


STEPS = ZS // 2
VMEM = pl.BlockSpec(memory_space=pltpu.VMEM)
SMEM = pl.BlockSpec(memory_space=pltpu.SMEM)
STATS = (2 * GROUP, QT)
STATED = {"near": 10**8, "far": 46 * 10**8, "twin": 46 * 10**8, "grads": 6 * 10**9}


def cost(kind):
    return pl.CostEstimate(flops=STATED[kind], bytes_accessed=1 << 16, transcendentals=0)


def scores(kind, kv, queries, prev=None, place=None):
    width = len(queries) * TOK
    args = [kv, *queries]
    in_specs = [VMEM] * len(args)
    out_shape = [
        shape_of((ZS * TOK, GROUP * width), BF16),
        shape_of((STEPS, 2 * GROUP, width), F32),
    ]
    if prev is not None:
        args += [place, *prev]
        in_specs += [SMEM, VMEM, VMEM]
        out_shape.append(shape_of((YS, *STATS), F32))
    return pl.pallas_call(
        functools.partial(score_kernel, len(queries), prev is not None),
        in_specs=in_specs,
        out_specs=[VMEM] * len(out_shape),
        out_shape=out_shape,
        scratch_shapes=[
            pltpu.VMEM((GROUP, width, HD), BF16),
            pltpu.VMEM((8, width), F32),
            pltpu.VMEM((2, KT, width), F32),
        ],
        compiler_params=params(),
        cost_estimate=cost(kind),
        name="scores_" + kind,
    )(*args)


def grads(kv, probs, stats, all_stats, queries, dq_in=None):
    last = dq_in is not None
    dq_shape = (GROUP, HD, QT)
    args = [kv, all_stats, *probs, *stats, *queries]
    out_shape = [shape_of((ZS, TOK, 2 * HD), F32 if last else BF16)]
    scratch = [
        pltpu.VMEM((GROUP, QT, HD), BF16),
        pltpu.VMEM((GROUP, QT, HD), BF16),
        pltpu.VMEM((8, QT), F32),
    ]
    if last:
        args.append(dq_in)
        out_shape += [shape_of((TOK, WIDE), F32)] + [shape_of((TOK, WIDE), BF16)] * (YS - 1)
        scratch.append(pltpu.VMEM(dq_shape, F32))
    else:
        out_shape.append(shape_of(dq_shape, F32))
    return pl.pallas_call(
        functools.partial(grad_kernel, last, len(probs)),
        in_specs=[VMEM] * len(args),
        out_specs=[VMEM] * len(out_shape),
        out_shape=out_shape,
        scratch_shapes=scratch,
        compiler_params=params(),
        cost_estimate=cost("grads"),
        name="grads",
    )(*args)


def per_device(query, key_rows, value_rows, output, grad_out, block_order, segment):
    n = lax.axis_size("ctx")
    near = [c + 2 * y + 8 * z for z in range(2) for y in range(2) for c in range(2)]
    key_groups = [[r + 4 * y + 16 * z for z in range(4) for y in range(2)] for r in near]
    tile_groups = [
        [c + 4 * y + 16 * z + bits for bits in TILE]
        for z in range(4)
        for y in range(2)
        for c in range(2)
    ]

    def swap(x, bits):
        return lax.ppermute(x, "ctx", [(i, i ^ bits) for i in range(n)])

    def exchange(x, groups):
        return lax.all_to_all(x, "ctx", 0, 0, tiled=True, axis_index_groups=groups)

    kv_pay, q_pay = pack(
        block_order, segment.reshape(1, TOK), query, key_rows, value_rows, output, grad_out
    )
    kv_own = exchange(kv_pay, key_groups)
    queries = [q_pay] + [swap(q_pay, bits) for bits in TILE[1:]]
    kv_twin = swap(kv_own, 1)
    index = lax.axis_index("ctx").astype(jnp.int32)
    place = ((index >> 1 & 1) + 2 * (index >> 3 & 1)).reshape(1)
    p_near, st_near = scores("near", kv_own, queries[:2])
    st_near, far = lax.optimization_barrier((st_near, queries[2:]))
    queries = queries[:2] + far
    p_far, st_far = scores("far", kv_own, far)
    p_twin, st_twin, stats = scores("twin", kv_twin, queries, (st_near, st_far), place)
    all_stats = exchange(stats, tile_groups)
    dkv_twin, dq = grads(kv_twin, [p_twin], [st_twin], all_stats, queries)
    dkv_back = swap(dkv_twin, 1)
    dkv_own, dq_own, *dq_send = grads(
        kv_own, [p_near, p_far], [st_near, st_far], all_stats, queries, dq
    )
    dkv = (dkv_own + dkv_back.astype(F32)).astype(BF16)
    dkv_all = exchange(dkv, key_groups)
    dq_parts = [swap(part, bits) for part, bits in zip(dq_send, TILE[1:])]
    grad_query = dq_own + sum(part.astype(F32) for part in dq_parts)
    grad_kv = jnp.sum(dkv_all.astype(F32), axis=0).astype(BF16)
    return grad_query.astype(BF16), grad_kv[:, 0:HD], grad_kv[:, HD : 2 * HD]


def solution(mesh):
    both = P("ctx", "kvh")
    return jax.shard_map(
        per_device,
        mesh=mesh,
        in_specs=(both, both, both, both, both, P("ctx"), P("ctx")),
        out_specs=(both, both, both),
        check_vma=False,
    )
```

time: 106 us -> 100 us (0.943)
  waiting for transfers between devices: 29.4 us -> 23.6 us
  blocking collectives: 6.45 us -> 9.62 us
  Pallas kernels: 20.8 us -> 18.5 us
    ppermute x8, waiting for transfers between devices: 29.4 us -> 13.2 us  [swap(): return lax.ppermute(x, 'ctx', [(i, i ^ bits) for i in range(n)])]
    all_to_all x2, waiting for transfers between devices: 0.01 us -> 10.4 us  [exchange(): return lax.all_to_all(x, 'ctx', 0, 0, tiled=True, axis_index_groups=groups)]
    all_to_all x1, blocking collectives: 6.45 us -> 9.62 us  [exchange(): return lax.all_to_all(x, 'ctx', 0, 0, tiled=True, axis_index_groups=groups)]
    pallas_call x4 -> x5, Pallas kernels: 18.3 us -> 16 us  [the longest x2 9.53 us: grads(): pl.pallas_call(functools.partial(grad_kernel, last, len(probs)), in_specs...]
    all_to_all x2, starting transfers between devices: 21 us -> 19 us  [exchange(): return lax.all_to_all(x, 'ctx', 0, 0, tiled=True, axis_index_groups=groups)]
    ppermute x8, starting transfers between devices: 23.3 us -> 24.9 us  [swap(): return lax.ppermute(x, 'ctx', [(i, i ^ bits) for i in range(n)])]
  transfers between devices with their start and end apart: 10 -> 10, of which waited for: 5 -> 5; matrix products, arithmetic and copies ran while one was open for 1% -> 1% of each run, Pallas kernels for 9% -> 8%
where the time goes in v6:
time: 100 us; the launch traced here: 99.7 us
  starting transfers between devices  43.9 us (44%)
  waiting for transfers between devices  23.6 us (24%)
  Pallas kernels  18.5 us (18%)
  blocking collectives  9.62 us (10%)
  other arithmetic  1.71 us (2%)
  local copies, waits for them, and re-layouts  1.59 us (2%)
    ppermute x8, starting transfers between devices, swap(): return lax.ppermute(x, 'ctx', [(i, i ^ bits) for i in range(n)])  24.9 us
    all_to_all x2, starting transfers between devices, exchange(): return lax.all_to_all(x, 'ctx', 0, 0, tiled=True, axis_index_groups=groups)  19 us
    ppermute x8, waiting for transfers between devices, swap(): return lax.ppermute(x, 'ctx', [(i, i ^ bits) for i in range(n)])  13.2 us
    all_to_all x2, waiting for transfers between devices, exchange(): return lax.all_to_all(x, 'ctx', 0, 0, tiled=True, axis_index_groups=groups)  10.4 us
    all_to_all x1, blocking collectives, exchange(): return lax.all_to_all(x, 'ctx', 0, 0, tiled=True, axis_index_groups=groups)  9.62 us
    pallas_call x2, Pallas kernels, grads(): pl.pallas_call(functools.partial(grad_kernel, last, len(probs)), in_specs...  9.53 us
    pallas_call x3, Pallas kernels, scores(): pl.pallas_call(functools.partial(score_kernel, len(queries), prev is not...  6.51 us
    pallas_call x1, Pallas kernels, pack(): pl.pallas_call(pack_kernel, out_shape=(shape_of((ZS, PAY, 2 * HD), BF16),...  2.46 us
  transfers between devices with their start and end apart: 10, of which 5 were waited for; matrix products, arithmetic and copies ran while one was open for 1% of the time, Pallas kernels for 8%

profile of v6, /device:TPU:1, one launch (start us, length us, event | category | flops | bytes accessed | tf_op | source)
XLA Modules:
  0.0 99.7 jit_solution(17057360491512440028)
XLA Ops:
  0.6 2.5 %pack.1 = (bf16[8,144,256]{2,1,0:T(8,128)(2,1)}, bf16[144,1024]{1,0:T(8,128)(2,1)}) custom-call(s32[2]{0:T(128)} %order_hbm.1, s32[1,128]{1,0:T(1,128)} %bitcast.2, bf16[128,512]{1,0:T(8,128)(2,1)} %q_hbm.1, bf16[128,128]{1,0:T(8,128)(2,1)} %k_hbm.1, bf16[128,128]{1,0:T(8,128)(2,1)} %v_hbm.1, bf16[128,512]{1,0:T(8,128)(2,1)} %o_hbm.1, bf16[128,512]{1,0:T(8,128)(2,1)} %g_hbm.1), custom_call_target="tpu_custom_call" | custom-call | tf_op jit(solution)/shard_map/pack/pallas_call | solution.py:209
  3.1 12.9 %all-to-all-start = ((bf16[8,144,256]{2,1,0:T(8,128)(2,1)}), bf16[8,144,256]{2,1,0:T(8,128)(2,1)S(1)}, u32[]{:S(2)}, u32[]{:S(2)}) async-start(bf16[8,144,256]{2,1,0:T(8,128)(2,1)} %get-tuple-element.22), calls=%async_computation | async-start | bytes 1179648 | tf_op jit(solution)/shard_map/all_to_all | solution.py:309
  16.0 3.2 %collective-permute-start.1 = (bf16[144,1024]{1,0:T(8,128)(2,1)}, bf16[144,1024]{1,0:T(8,128)(2,1)S(1)}, u32[]{:S(2)}, u32[]{:S(2)}) collective-permute-start(bf16[144,1024]{1,0:T(8,128)(2,1)} %get-tuple-element.23.refs_0_.refs_2_.refs_4_), channel_id=1, source_target_pairs={{0,16},{8,24},{16,0},{24,8},{32,48},{40,56},{48,32},{56,40},{64,80... | collective-permute-start | bytes 884744 | tf_op jit(solution)/shard_map/ppermute | solution.py:306
  19.2 3.0 %collective-permute-start.3 = (bf16[144,1024]{1,0:T(8,128)(2,1)}, bf16[144,1024]{1,0:T(8,128)(2,1)S(1)}, u32[]{:S(2)}, u32[]{:S(2)}) collective-permute-start(bf16[144,1024]{1,0:T(8,128)(2,1)} %get-tuple-element.23.refs_0_.refs_2_.refs_4_), channel_id=1, source_target_pairs={{0,80},{8,88},{16,64},{24,72},{32,112},{40,120},{48,96},{56,104},{... | collective-permute-start | bytes 884744 | tf_op jit(solution)/shard_map/ppermute | solution.py:306
  22.2 2.2 %collective-permute-start.2 = (bf16[144,1024]{1,0:T(8,128)(2,1)}, bf16[144,1024]{1,0:T(8,128)(2,1)S(1)}, u32[]{:S(2)}, u32[]{:S(2)}) collective-permute-start(bf16[144,1024]{1,0:T(8,128)(2,1)} %get-tuple-element.23.refs_0_.refs_2_.refs_4_), channel_id=1, source_target_pairs={{0,64},{8,72},{16,80},{24,88},{32,96},{40,104},{48,112},{56,120},{... | collective-permute-start | bytes 884744 | tf_op jit(solution)/shard_map/ppermute | solution.py:306
  24.4 10.4 %all-to-all-done.kv_ref = bf16[8,144,256]{2,1,0:T(8,128)(2,1)S(1)} async-done(((bf16[8,144,256]{2,1,0:T(8,128)(2,1)}), bf16[8,144,256]{2,1,0:T(8,128)(2,1)S(1)}, u32[]{:S(2)}, u32[]{:S(2)}) %all-to-all-start) | async-done | bytes 589856 | tf_op jit(solution)/shard_map/all_to_all | solution.py:309
  34.8 4.7 %collective-permute-start = (bf16[8,144,256]{2,1,0:T(8,128)(2,1)S(1)}, bf16[8,144,256]{2,1,0:T(8,128)(2,1)S(1)}, u32[]{:S(2)}, u32[]{:S(2)}) collective-permute-start(bf16[8,144,256]{2,1,0:T(8,128)(2,1)S(1)} %all-to-all-done.kv_ref), channel_id=1, source_target_pairs={{0,8},{8,0},{16,24},{24,16},{32,40},{40,32},{48,56},{56,48},{64,72... | collective-permute-start | bytes 1769480 | tf_op jit(solution)/shard_map/ppermute | solution.py:306
  39.4 0.0 collective-permute-done.1.refs_1_.refs_3_.refs_5_
  39.5 0.0 copy-start
  39.5 1.0 copy-done
  40.4 1.6 %scores_near.1 = (bf16[1024,1024]{1,0:T(8,128)(2,1)S(1)}, f32[4,8,256]{2,1,0:T(8,128)S(1)}) custom-call(bf16[8,144,256]{2,1,0:T(8,128)(2,1)S(1)} %all-to-all-done.kv_ref, bf16[144,1024]{1,0:T(8,128)(2,1)S(1)} %copy-done, bf16[144,1024]{1,0:T(8,128)(2,1)S(1)} %collective-permute-done.1.refs_1_.refs_3_.refs_5_), custom_call_target="tpu_custom_call" | custom-call | flops 100000000 | bytes 65536 | tf_op jit(solution)/shard_map/scores_near/pallas_call | solution.py:250
  42.0 0.0 collective-permute-done.3.refs_1_.refs_3_.refs_5_.refs_7_
  42.0 2.4 %collective-permute-done.2.refs_0_.refs_2_.refs_4_.refs_6_ = bf16[144,1024]{1,0:T(8,128)(2,1)S(1)} collective-permute-done((bf16[144,1024]{1,0:T(8,128)(2,1)}, bf16[144,1024]{1,0:T(8,128)(2,1)S(1)}, u32[]{:S(2)}, u32[]{:S(2)}) %collective-permute-start.2) | collective-permute-done | bytes 294944 | tf_op jit(solution)/shard_map/ppermute | solution.py:306
  44.4 1.6 %scores_far.1 = (bf16[1024,1024]{1,0:T(8,128)(2,1)S(1)}, f32[4,8,256]{2,1,0:T(8,128)S(1)}) custom-call(bf16[8,144,256]{2,1,0:T(8,128)(2,1)S(1)} %all-to-all-done.kv_ref, bf16[144,1024]{1,0:T(8,128)(2,1)S(1)} %collective-permute-done.2.refs_0_.refs_2_.refs_4_.refs_6_, bf16[144,1024]{1,0:T(8,128)(2,1)S(1)} %collective-permute-done.3.refs_1_.refs_3_.refs_5_.refs_7_), custom_call_target="tpu_custom_call" | custom-call | flops 4600000000 | bytes 65536 | tf_op jit(solution)/shard_map/scores_far/pallas_call | solution.py:250
  46.0 0.0 collective-permute-done.kv_ref
  46.0 3.3 %scores_twin.1 = (bf16[1024,2048]{1,0:T(8,128)(2,1)S(1)}, f32[4,8,512]{2,1,0:T(8,128)S(1)}, f32[4,8,512]{2,1,0:T(8,128)S(1)}) custom-call(bf16[8,144,256]{2,1,0:T(8,128)(2,1)S(1)} %collective-permute-done.kv_ref, bf16[144,1024]{1,0:T(8,128)(2,1)S(1)} %copy-done, bf16[144,1024]{1,0:T(8,128)(2,1)S(1)} %collective-permute-done.1.refs_1_.refs_3_.refs_5_, ...), custom_call_target="tpu_custom_call" | custom-call | flops 4600000000 | bytes 65536 | tf_op jit(solution)/shard_map/scores_twin/pallas_call | solution.py:250
  49.3 9.6 %all_to_all.15.all_ref = f32[4,8,512]{2,1,0:T(8,128)S(1)} all-to-all(f32[4,8,512]{2,1,0:T(8,128)S(1)} %get-tuple-element.29), channel_id=1, replica_groups={{0,16,64,80},{8,24,72,88},{32,48,96,112},{40,56,104,120},{128,144,192,2..., dimensions={0} | all-to-all | bytes 131072 | tf_op jit(solution)/shard_map/all_to_all | solution.py:309
  59.0 4.7 %grads.2 = (bf16[8,128,256]{2,1,0:T(8,128)(2,1)S(1)}, f32[4,128,512]{2,1,0:T(8,128)S(1)}) custom-call(bf16[8,144,256]{2,1,0:T(8,128)(2,1)S(1)} %collective-permute-done.kv_ref, f32[4,8,512]{2,1,0:T(8,128)S(1)} %all_to_all.15.all_ref, bf16[1024,2048]{1,0:T(8,128)(2,1)S(1)} %get-tuple-element.32.refs_0_, f32[4,8,512]{2,1,0:T(8,128)S(1)} %get-tuple-element.33.refs_1_, ...), custom_call_target="tpu_custom_call" | custom-call | flops 6000000000 | bytes 65536 | tf_op jit(solution)/shard_map/grads/pallas_call | solution.py:282
  63.6 3.5 %collective-permute-start.7 = (bf16[8,128,256]{2,1,0:T(8,128)(2,1)S(1)}, bf16[8,128,256]{2,1,0:T(8,128)(2,1)S(1)}, u32[]{:S(2)}, u32[]{:S(2)}) collective-permute-start(bf16[8,128,256]{2,1,0:T(8,128)(2,1)S(1)} %get-tuple-element.40), channel_id=1, source_target_pairs={{0,8},{8,0},{16,24},{24,16},{32,40},{40,32},{48,56},{56,48},{64,72... | collective-permute-start | bytes 1572872 | tf_op jit(solution)/shard_map/ppermute | solution.py:306
  67.1 4.9 %grads.3 = (f32[8,128,256]{2,1,0:T(8,128)S(1)}, f32[128,512]{1,0:T(8,128)S(1)}, bf16[128,512]{1,0:T(8,128)(2,1)S(1)}, bf16[128,512]{1,0:T(8,128)(2,1)S(1)}, bf16[128,512]{1,0:T(8,128)(2,1)S(1)}) custom-call(bf16[8,144,256]{2,1,0:T(8,128)(2,1)S(1)} %all-to-all-done.kv_ref, f32[4,8,512]{2,1,0:T(8,128)S(1)} %all_to_all.15.all_ref, ...), custom_call_target="tpu_custom_call" | custom-call | flops 6000000000 | bytes 65536 | tf_op jit(solution)/shard_map/grads/pallas_call | solution.py:282
  72.0 0.0 collective-permute-done.7
  72.0 0.9 add_convert_fusion
  72.9 6.1 %all-to-all-start.2 = ((bf16[8,128,256]{2,1,0:T(8,128)(2,1)}), bf16[8,128,256]{2,1,0:T(8,128)(2,1)S(1)}, u32[]{:S(2)}, u32[]{:S(2)}) async-start(bf16[8,128,256]{2,1,0:T(8,128)(2,1)} %add_convert_fusion), calls=%async_computation.2 | async-start | bytes 1048576 | tf_op jit(solution)/shard_map/all_to_all | solution.py:309
  79.1 2.4 %collective-permute-start.4 = (bf16[128,512]{1,0:T(8,128)(2,1)S(1)}, bf16[128,512]{1,0:T(8,128)(2,1)S(1)}, u32[]{:S(2)}, u32[]{:S(2)}) collective-permute-start(bf16[128,512]{1,0:T(8,128)(2,1)S(1)} %get-tuple-element.36), channel_id=1, source_target_pairs={{0,16},{8,24},{16,0},{24,8},{32,48},{40,56},{48,32},{56,40},{64,80... | collective-permute-start | bytes 393224 | tf_op jit(solution)/shard_map/ppermute | solution.py:306
  81.4 2.0 %collective-permute-start.5 = (bf16[128,512]{1,0:T(8,128)(2,1)S(1)}, bf16[128,512]{1,0:T(8,128)(2,1)S(1)}, u32[]{:S(2)}, u32[]{:S(2)}) collective-permute-start(bf16[128,512]{1,0:T(8,128)(2,1)S(1)} %get-tuple-element.37), channel_id=1, source_target_pairs={{0,64},{8,72},{16,80},{24,88},{32,96},{40,104},{48,112},{56,120},{... | collective-permute-start | bytes 393224 | tf_op jit(solution)/shard_map/ppermute | solution.py:306
  83.5 4.0 %collective-permute-start.6 = (bf16[128,512]{1,0:T(8,128)(2,1)S(1)}, bf16[128,512]{1,0:T(8,128)(2,1)S(1)}, u32[]{:S(2)}, u32[]{:S(2)}) collective-permute-start(bf16[128,512]{1,0:T(8,128)(2,1)S(1)} %get-tuple-element.38), channel_id=1, source_target_pairs={{0,80},{8,88},{16,64},{24,72},{32,112},{40,120},{48,96},{56,104},{... | collective-permute-start | bytes 393224 | tf_op jit(solution)/shard_map/ppermute | solution.py:306
  87.5 1.4 %collective-permute-done.4 = bf16[128,512]{1,0:T(8,128)(2,1)S(1)} collective-permute-done((bf16[128,512]{1,0:T(8,128)(2,1)S(1)}, bf16[128,512]{1,0:T(8,128)(2,1)S(1)}, u32[]{:S(2)}, u32[]{:S(2)}) %collective-permute-start.4) | collective-permute-done | bytes 131104 | tf_op jit(solution)/shard_map/ppermute | solution.py:306
  88.9 4.3 %collective-permute-done.5 = bf16[128,512]{1,0:T(8,128)(2,1)S(1)} collective-permute-done((bf16[128,512]{1,0:T(8,128)(2,1)S(1)}, bf16[128,512]{1,0:T(8,128)(2,1)S(1)}, u32[]{:S(2)}, u32[]{:S(2)}) %collective-permute-start.5) | collective-permute-done | bytes 131104 | tf_op jit(solution)/shard_map/ppermute | solution.py:306
  93.2 5.1 %collective-permute-done.6 = bf16[128,512]{1,0:T(8,128)(2,1)S(1)} collective-permute-done((bf16[128,512]{1,0:T(8,128)(2,1)S(1)}, bf16[128,512]{1,0:T(8,128)(2,1)S(1)}, u32[]{:S(2)}, u32[]{:S(2)}) %collective-permute-start.6) | collective-permute-done | bytes 131104 | tf_op jit(solution)/shard_map/ppermute | solution.py:306
  98.3 0.7 add_convert_fusion.1
  99.0 0.0 all-to-all-done.2
  99.0 0.1 reduce_sum.12
  99.1 0.6 fusion
Async XLA Ops:
  3.1 31.7 %all-to-all-start = ((bf16[8,144,256]{2,1,0:T(8,128)(2,1)}), bf16[8,144,256]{2,1,0:T(8,128)(2,1)S(1)}, u32[]{:S(2)}, u32[]{:S(2)}) async-start(bf16[8,144,256]{2,1,0:T(8,128)(2,1)} %get-tuple-element.22), calls=%async_computation | async-start | bytes 1179648 | tf_op jit(solution)/shard_map/all_to_all | solution.py:309
  16.0 23.5 %collective-permute-start.1 = (bf16[144,1024]{1,0:T(8,128)(2,1)}, bf16[144,1024]{1,0:T(8,128)(2,1)S(1)}, u32[]{:S(2)}, u32[]{:S(2)}) collective-permute-start(bf16[144,1024]{1,0:T(8,128)(2,1)} %get-tuple-element.23.refs_0_.refs_2_.refs_4_), channel_id=1, source_target_pairs={{0,16},{8,24},{16,0},{24,8},{32,48},{40,56},{48,32},{56,40},{64,80... | collective-permute-start | bytes 884744 | tf_op jit(solution)/shard_map/ppermute | solution.py:306
  19.2 22.8 %collective-permute-start.3 = (bf16[144,1024]{1,0:T(8,128)(2,1)}, bf16[144,1024]{1,0:T(8,128)(2,1)S(1)}, u32[]{:S(2)}, u32[]{:S(2)}) collective-permute-start(bf16[144,1024]{1,0:T(8,128)(2,1)} %get-tuple-element.23.refs_0_.refs_2_.refs_4_), channel_id=1, source_target_pairs={{0,80},{8,88},{16,64},{24,72},{32,112},{40,120},{48,96},{56,104},{... | collective-permute-start | bytes 884744 | tf_op jit(solution)/shard_map/ppermute | solution.py:306
  22.2 22.2 %collective-permute-start.2 = (bf16[144,1024]{1,0:T(8,128)(2,1)}, bf16[144,1024]{1,0:T(8,128)(2,1)S(1)}, u32[]{:S(2)}, u32[]{:S(2)}) collective-permute-start(bf16[144,1024]{1,0:T(8,128)(2,1)} %get-tuple-element.23.refs_0_.refs_2_.refs_4_), channel_id=1, source_target_pairs={{0,64},{8,72},{16,80},{24,88},{32,96},{40,104},{48,112},{56,120},{... | collective-permute-start | bytes 884744 | tf_op jit(solution)/shard_map/ppermute | solution.py:306
  34.8 11.3 %collective-permute-start = (bf16[8,144,256]{2,1,0:T(8,128)(2,1)S(1)}, bf16[8,144,256]{2,1,0:T(8,128)(2,1)S(1)}, u32[]{:S(2)}, u32[]{:S(2)}) collective-permute-start(bf16[8,144,256]{2,1,0:T(8,128)(2,1)S(1)} %all-to-all-done.kv_ref), channel_id=1, source_target_pairs={{0,8},{8,0},{16,24},{24,16},{32,40},{40,32},{48,56},{56,48},{64,72... | collective-permute-start | bytes 1769480 | tf_op jit(solution)/shard_map/ppermute | solution.py:306
  39.5 1.0 copy-start
  63.6 8.4 %collective-permute-start.7 = (bf16[8,128,256]{2,1,0:T(8,128)(2,1)S(1)}, bf16[8,128,256]{2,1,0:T(8,128)(2,1)S(1)}, u32[]{:S(2)}, u32[]{:S(2)}) collective-permute-start(bf16[8,128,256]{2,1,0:T(8,128)(2,1)S(1)} %get-tuple-element.40), channel_id=1, source_target_pairs={{0,8},{8,0},{16,24},{24,16},{32,40},{40,32},{48,56},{56,48},{64,72... | collective-permute-start | bytes 1572872 | tf_op jit(solution)/shard_map/ppermute | solution.py:306
  72.9 26.0 %all-to-all-start.2 = ((bf16[8,128,256]{2,1,0:T(8,128)(2,1)}), bf16[8,128,256]{2,1,0:T(8,128)(2,1)S(1)}, u32[]{:S(2)}, u32[]{:S(2)}) async-start(bf16[8,128,256]{2,1,0:T(8,128)(2,1)} %add_convert_fusion), calls=%async_computation.2 | async-start | bytes 1048576 | tf_op jit(solution)/shard_map/all_to_all | solution.py:309
  79.1 9.8 %collective-permute-start.4 = (bf16[128,512]{1,0:T(8,128)(2,1)S(1)}, bf16[128,512]{1,0:T(8,128)(2,1)S(1)}, u32[]{:S(2)}, u32[]{:S(2)}) collective-permute-start(bf16[128,512]{1,0:T(8,128)(2,1)S(1)} %get-tuple-element.36), channel_id=1, source_target_pairs={{0,16},{8,24},{16,0},{24,8},{32,48},{40,56},{48,32},{56,40},{64,80... | collective-permute-start | bytes 393224 | tf_op jit(solution)/shard_map/ppermute | solution.py:306
  81.4 11.7 %collective-permute-start.5 = (bf16[128,512]{1,0:T(8,128)(2,1)S(1)}, bf16[128,512]{1,0:T(8,128)(2,1)S(1)}, u32[]{:S(2)}, u32[]{:S(2)}) collective-permute-start(bf16[128,512]{1,0:T(8,128)(2,1)S(1)} %get-tuple-element.37), channel_id=1, source_target_pairs={{0,64},{8,72},{16,80},{24,88},{32,96},{40,104},{48,112},{56,120},{... | collective-permute-start | bytes 393224 | tf_op jit(solution)/shard_map/ppermute | solution.py:306
  83.5 14.8 %collective-permute-start.6 = (bf16[128,512]{1,0:T(8,128)(2,1)S(1)}, bf16[128,512]{1,0:T(8,128)(2,1)S(1)}, u32[]{:S(2)}, u32[]{:S(2)}) collective-permute-start(bf16[128,512]{1,0:T(8,128)(2,1)S(1)} %get-tuple-element.38), channel_id=1, source_target_pairs={{0,80},{8,88},{16,64},{24,72},{32,112},{40,120},{48,96},{56,104},{... | collective-permute-start | bytes 393224 | tf_op jit(solution)/shard_map/ppermute | solution.py:306

commit v7 on v6

--- a/solution.py
+++ b/solution.py
@@ -17,7 +17,7 @@
 EXTRA = 16
 PAY = TOK + EXTRA
 YS = 4
-TILE = (0, 2, 8, 10)
+TILE = (0, 2, 4, 6)
 ZS = 8
 WIDE = GROUP * HD
 QT = YS * TOK
@@ -293,14 +293,8 @@
 
 def per_device(query, key_rows, value_rows, output, grad_out, block_order, segment):
     n = lax.axis_size("ctx")
-    near = [c + 2 * y + 8 * z for z in range(2) for y in range(2) for c in range(2)]
-    key_groups = [[r + 4 * y + 16 * z for z in range(4) for y in range(2)] for r in near]
-    tile_groups = [
-        [c + 4 * y + 16 * z + bits for bits in TILE]
-        for z in range(4)
-        for y in range(2)
-        for c in range(2)
-    ]
+    key_groups = [[r + 8 * z for z in range(ZS)] for r in range(ZS)]
+    tile_groups = [[c + 8 * z + bits for bits in TILE] for z in range(ZS) for c in range(2)]
 
     def swap(x, bits):
         return lax.ppermute(x, "ctx", [(i, i ^ bits) for i in range(n)])
@@ -312,10 +306,11 @@
         block_order, segment.reshape(1, TOK), query, key_rows, value_rows, output, grad_out
     )
     kv_own = exchange(kv_pay, key_groups)
-    queries = [q_pay] + [swap(q_pay, bits) for bits in TILE[1:]]
+    q_far, q_near = swap(q_pay, TILE[2]), swap(q_pay, TILE[1])
+    queries = [q_pay, q_near, q_far, swap(q_far, TILE[1])]
     kv_twin = swap(kv_own, 1)
     index = lax.axis_index("ctx").astype(jnp.int32)
-    place = ((index >> 1 & 1) + 2 * (index >> 3 & 1)).reshape(1)
+    place = (index >> 1 & (YS - 1)).reshape(1)
     p_near, st_near = scores("near", kv_own, queries[:2])
     st_near, far = lax.optimization_barrier((st_near, queries[2:]))
     queries = queries[:2] + far
@@ -329,7 +324,7 @@
     )
     dkv = (dkv_own + dkv_back.astype(F32)).astype(BF16)
     dkv_all = exchange(dkv, key_groups)
-    dq_parts = [swap(part, bits) for part, bits in zip(dq_send, TILE[1:])]
+    dq_parts = [swap(part, bits) for part, bits in zip(dq_send[::-1], TILE[:0:-1])]
     grad_query = dq_own + sum(part.astype(F32) for part in dq_parts)
     grad_kv = jnp.sum(dkv_all.astype(F32), axis=0).astype(BF16)
     return grad_query.astype(BF16), grad_kv[:, 0:HD], grad_kv[:, HD : 2 * HD]

time: 100 us -> 97.3 us (0.973)
  waiting for transfers between devices: 23.6 us -> 18.4 us
  starting transfers between devices: 43.9 us -> 45.3 us
    all_to_all x2, waiting for transfers between devices: 10.4 us -> 1.83 us  [exchange(): return lax.all_to_all(x, 'ctx', 0, 0, tiled=True, axis_index_groups=groups)]
    ppermute x8, waiting for transfers between devices: 13.2 us -> 16.6 us  [swap(): return lax.ppermute(x, 'ctx', [(i, i ^ bits) for i in range(n)])]
    ppermute x8, starting transfers between devices: 24.9 us -> 27.7 us  [swap(): return lax.ppermute(x, 'ctx', [(i, i ^ bits) for i in range(n)])]
    all_to_all x2, starting transfers between devices: 19 us -> 17.5 us  [exchange(): return lax.all_to_all(x, 'ctx', 0, 0, tiled=True, axis_index_groups=groups)]
  transfers between devices with their start and end apart: 10 -> 10, of which waited for: 5 -> 4; matrix products, arithmetic and copies ran while one was open for 1% -> 1% of each run, Pallas kernels for 8% -> 8%
where the time goes in v7:
time: 97.3 us; the launch traced here: 96.7 us
  starting transfers between devices  45.3 us (47%)
  Pallas kernels  18.5 us (19%)
  waiting for transfers between devices  18.4 us (19%)
  blocking collectives  10.5 us (11%)
  other arithmetic  1.71 us (2%)
  local copies, waits for them, and re-layouts  1.59 us (2%)
    ppermute x8, starting transfers between devices, swap(): return lax.ppermute(x, 'ctx', [(i, i ^ bits) for i in range(n)])  27.7 us
    all_to_all x2, starting transfers between devices, exchange(): return lax.all_to_all(x, 'ctx', 0, 0, tiled=True, axis_index_groups=groups)  17.5 us
    ppermute x8, waiting for transfers between devices, swap(): return lax.ppermute(x, 'ctx', [(i, i ^ bits) for i in range(n)])  16.6 us
    all_to_all x1, blocking collectives, exchange(): return lax.all_to_all(x, 'ctx', 0, 0, tiled=True, axis_index_groups=groups)  10.5 us
    pallas_call x2, Pallas kernels, grads(): pl.pallas_call(functools.partial(grad_kernel, last, len(probs)), in_specs...  9.53 us
    pallas_call x3, Pallas kernels, scores(): pl.pallas_call(functools.partial(score_kernel, len(queries), prev is not...  6.5 us
    pallas_call x1, Pallas kernels, pack(): pl.pallas_call(pack_kernel, out_shape=(shape_of((ZS, PAY, 2 * HD), BF16),...  2.46 us
  transfers between devices with their start and end apart: 10, of which 4 were waited for; matrix products, arithmetic and copies ran while one was open for 1% of the time, Pallas kernels for 8%

profile of v7, /device:TPU:1, one launch (start us, length us, event | category | flops | bytes accessed | tf_op | source)
XLA Modules:
  0.0 96.7 jit_solution(6304043230353518014)
XLA Ops:
  0.6 2.5 %pack.1 = (bf16[8,144,256]{2,1,0:T(8,128)(2,1)}, bf16[144,1024]{1,0:T(8,128)(2,1)}) custom-call(s32[2]{0:T(128)} %order_hbm.1, s32[1,128]{1,0:T(1,128)} %bitcast.2, bf16[128,512]{1,0:T(8,128)(2,1)} %q_hbm.1, bf16[128,128]{1,0:T(8,128)(2,1)} %k_hbm.1, bf16[128,128]{1,0:T(8,128)(2,1)} %v_hbm.1, bf16[128,512]{1,0:T(8,128)(2,1)} %o_hbm.1, bf16[128,512]{1,0:T(8,128)(2,1)} %g_hbm.1), custom_call_target="tpu_custom_call" | custom-call | tf_op jit(solution)/shard_map/pack/pallas_call | solution.py:209
  3.1 10.9 %all-to-all-start = ((bf16[8,144,256]{2,1,0:T(8,128)(2,1)}), bf16[8,144,256]{2,1,0:T(8,128)(2,1)S(1)}, u32[]{:S(2)}, u32[]{:S(2)}) async-start(bf16[8,144,256]{2,1,0:T(8,128)(2,1)} %get-tuple-element.22), calls=%async_computation | async-start | bytes 1179648 | tf_op jit(solution)/shard_map/all_to_all | solution.py:303
  14.0 4.2 %collective-permute-start.2 = (bf16[144,1024]{1,0:T(8,128)(2,1)}, bf16[144,1024]{1,0:T(8,128)(2,1)S(1)}, u32[]{:S(2)}, u32[]{:S(2)}) collective-permute-start(bf16[144,1024]{1,0:T(8,128)(2,1)} %get-tuple-element.23.refs_0_.refs_2_.refs_4_), channel_id=1, source_target_pairs={{0,32},{8,40},{16,48},{24,56},{32,0},{40,8},{48,16},{56,24},{64,96... | collective-permute-start | bytes 884744 | tf_op jit(solution)/shard_map/ppermute | solution.py:300
  18.2 3.2 %collective-permute-start.1 = (bf16[144,1024]{1,0:T(8,128)(2,1)}, bf16[144,1024]{1,0:T(8,128)(2,1)S(1)}, u32[]{:S(2)}, u32[]{:S(2)}) collective-permute-start(bf16[144,1024]{1,0:T(8,128)(2,1)} %get-tuple-element.23.refs_0_.refs_2_.refs_4_), channel_id=1, source_target_pairs={{0,16},{8,24},{16,0},{24,8},{32,48},{40,56},{48,32},{56,40},{64,80... | collective-permute-start | bytes 884744 | tf_op jit(solution)/shard_map/ppermute | solution.py:300
  21.4 9.8 %collective-permute-done.2.refs_0_.refs_2_.refs_4_.refs_6_ = bf16[144,1024]{1,0:T(8,128)(2,1)S(1)} collective-permute-done((bf16[144,1024]{1,0:T(8,128)(2,1)}, bf16[144,1024]{1,0:T(8,128)(2,1)S(1)}, u32[]{:S(2)}, u32[]{:S(2)}) %collective-permute-start.2) | collective-permute-done | bytes 294944 | tf_op jit(solution)/shard_map/ppermute | solution.py:300
  31.2 3.5 %collective-permute-start.3 = (bf16[144,1024]{1,0:T(8,128)(2,1)S(1)}, bf16[144,1024]{1,0:T(8,128)(2,1)S(1)}, u32[]{:S(2)}, u32[]{:S(2)}) collective-permute-start(bf16[144,1024]{1,0:T(8,128)(2,1)S(1)} %collective-permute-done.2.refs_0_.refs_2_.refs_4_.refs_6_), channel_id=1, source_target_pairs={{0,16},{8,24},{16,0},{24,8},{32,48},{40,56},{48,32},{56,40},{64,80... | collective-permute-start | bytes 884744 | tf_op jit(solution)/shard_map/ppermute | solution.py:300
  34.7 0.0 all-to-all-done.kv_ref
  34.7 2.7 %collective-permute-start = (bf16[8,144,256]{2,1,0:T(8,128)(2,1)S(1)}, bf16[8,144,256]{2,1,0:T(8,128)(2,1)S(1)}, u32[]{:S(2)}, u32[]{:S(2)}) collective-permute-start(bf16[8,144,256]{2,1,0:T(8,128)(2,1)S(1)} %all-to-all-done.kv_ref), channel_id=1, source_target_pairs={{0,8},{8,0},{16,24},{24,16},{32,40},{40,32},{48,56},{56,48},{64,72... | collective-permute-start | bytes 1769480 | tf_op jit(solution)/shard_map/ppermute | solution.py:300
  37.4 0.0 collective-permute-done.1.refs_1_.refs_3_.refs_5_
  37.4 0.0 copy-start
  37.4 1.0 copy-done
  38.3 1.6 %scores_near.1 = (bf16[1024,1024]{1,0:T(8,128)(2,1)S(1)}, f32[4,8,256]{2,1,0:T(8,128)S(1)}) custom-call(bf16[8,144,256]{2,1,0:T(8,128)(2,1)S(1)} %all-to-all-done.kv_ref, bf16[144,1024]{1,0:T(8,128)(2,1)S(1)} %copy-done, bf16[144,1024]{1,0:T(8,128)(2,1)S(1)} %collective-permute-done.1.refs_1_.refs_3_.refs_5_), custom_call_target="tpu_custom_call" | custom-call | flops 100000000 | bytes 65536 | tf_op jit(solution)/shard_map/scores_near/pallas_call | solution.py:250
  39.9 0.6 collective-permute-done.3.refs_1_.refs_3_.refs_5_.refs_7_
  40.5 1.6 %scores_far.1 = (bf16[1024,1024]{1,0:T(8,128)(2,1)S(1)}, f32[4,8,256]{2,1,0:T(8,128)S(1)}) custom-call(bf16[8,144,256]{2,1,0:T(8,128)(2,1)S(1)} %all-to-all-done.kv_ref, bf16[144,1024]{1,0:T(8,128)(2,1)S(1)} %collective-permute-done.2.refs_0_.refs_2_.refs_4_.refs_6_, bf16[144,1024]{1,0:T(8,128)(2,1)S(1)} %collective-permute-done.3.refs_1_.refs_3_.refs_5_.refs_7_), custom_call_target="tpu_custom_call" | custom-call | flops 4600000000 | bytes 65536 | tf_op jit(solution)/shard_map/scores_far/pallas_call | solution.py:250
  42.1 0.0 collective-permute-done.kv_ref
  42.1 3.3 %scores_twin.1 = (bf16[1024,2048]{1,0:T(8,128)(2,1)S(1)}, f32[4,8,512]{2,1,0:T(8,128)S(1)}, f32[4,8,512]{2,1,0:T(8,128)S(1)}) custom-call(bf16[8,144,256]{2,1,0:T(8,128)(2,1)S(1)} %collective-permute-done.kv_ref, bf16[144,1024]{1,0:T(8,128)(2,1)S(1)} %copy-done, bf16[144,1024]{1,0:T(8,128)(2,1)S(1)} %collective-permute-done.1.refs_1_.refs_3_.refs_5_, ...), custom_call_target="tpu_custom_call" | custom-call | flops 4600000000 | bytes 65536 | tf_op jit(solution)/shard_map/scores_twin/pallas_call | solution.py:250
  45.5 10.5 %all_to_all.15.all_ref = f32[4,8,512]{2,1,0:T(8,128)S(1)} all-to-all(f32[4,8,512]{2,1,0:T(8,128)S(1)} %get-tuple-element.29), channel_id=1, replica_groups={{0,16,32,48},{8,24,40,56},{64,80,96,112},{72,88,104,120},{128,144,160,1..., dimensions={0} | all-to-all | bytes 131072 | tf_op jit(solution)/shard_map/all_to_all | solution.py:303
  56.0 4.7 %grads.2 = (bf16[8,128,256]{2,1,0:T(8,128)(2,1)S(1)}, f32[4,128,512]{2,1,0:T(8,128)S(1)}) custom-call(bf16[8,144,256]{2,1,0:T(8,128)(2,1)S(1)} %collective-permute-done.kv_ref, f32[4,8,512]{2,1,0:T(8,128)S(1)} %all_to_all.15.all_ref, bf16[1024,2048]{1,0:T(8,128)(2,1)S(1)} %get-tuple-element.32.refs_0_, f32[4,8,512]{2,1,0:T(8,128)S(1)} %get-tuple-element.33.refs_1_, ...), custom_call_target="tpu_custom_call" | custom-call | flops 6000000000 | bytes 65536 | tf_op jit(solution)/shard_map/grads/pallas_call | solution.py:282
  60.6 4.9 %collective-permute-start.7 = (bf16[8,128,256]{2,1,0:T(8,128)(2,1)S(1)}, bf16[8,128,256]{2,1,0:T(8,128)(2,1)S(1)}, u32[]{:S(2)}, u32[]{:S(2)}) collective-permute-start(bf16[8,128,256]{2,1,0:T(8,128)(2,1)S(1)} %get-tuple-element.40), channel_id=1, source_target_pairs={{0,8},{8,0},{16,24},{24,16},{32,40},{40,32},{48,56},{56,48},{64,72... | collective-permute-start | bytes 1572872 | tf_op jit(solution)/shard_map/ppermute | solution.py:300
  65.6 4.9 %grads.3 = (f32[8,128,256]{2,1,0:T(8,128)S(1)}, f32[128,512]{1,0:T(8,128)S(1)}, bf16[128,512]{1,0:T(8,128)(2,1)S(1)}, bf16[128,512]{1,0:T(8,128)(2,1)S(1)}, bf16[128,512]{1,0:T(8,128)(2,1)S(1)}) custom-call(bf16[8,144,256]{2,1,0:T(8,128)(2,1)S(1)} %all-to-all-done.kv_ref, f32[4,8,512]{2,1,0:T(8,128)S(1)} %all_to_all.15.all_ref, ...), custom_call_target="tpu_custom_call" | custom-call | flops 6000000000 | bytes 65536 | tf_op jit(solution)/shard_map/grads/pallas_call | solution.py:282
  70.4 0.0 collective-permute-done.7
  70.4 0.9 add_convert_fusion
  71.4 6.6 %all-to-all-start.2 = ((bf16[8,128,256]{2,1,0:T(8,128)(2,1)}), bf16[8,128,256]{2,1,0:T(8,128)(2,1)S(1)}, u32[]{:S(2)}, u32[]{:S(2)}) async-start(bf16[8,128,256]{2,1,0:T(8,128)(2,1)} %add_convert_fusion), calls=%async_computation.2 | async-start | bytes 1048576 | tf_op jit(solution)/shard_map/all_to_all | solution.py:303
  78.0 2.4 %collective-permute-start.4 = (bf16[128,512]{1,0:T(8,128)(2,1)S(1)}, bf16[128,512]{1,0:T(8,128)(2,1)S(1)}, u32[]{:S(2)}, u32[]{:S(2)}) collective-permute-start(bf16[128,512]{1,0:T(8,128)(2,1)S(1)} %get-tuple-element.36), channel_id=1, source_target_pairs={{0,48},{8,56},{16,32},{24,40},{32,16},{40,24},{48,0},{56,8},{64,11... | collective-permute-start | bytes 393224 | tf_op jit(solution)/shard_map/ppermute | solution.py:300
  80.4 3.3 %collective-permute-start.5 = (bf16[128,512]{1,0:T(8,128)(2,1)S(1)}, bf16[128,512]{1,0:T(8,128)(2,1)S(1)}, u32[]{:S(2)}, u32[]{:S(2)}) collective-permute-start(bf16[128,512]{1,0:T(8,128)(2,1)S(1)} %get-tuple-element.37), channel_id=1, source_target_pairs={{0,32},{8,40},{16,48},{24,56},{32,0},{40,8},{48,16},{56,24},{64,96... | collective-permute-start | bytes 393224 | tf_op jit(solution)/shard_map/ppermute | solution.py:300
  83.6 3.6 %collective-permute-start.6 = (bf16[128,512]{1,0:T(8,128)(2,1)S(1)}, bf16[128,512]{1,0:T(8,128)(2,1)S(1)}, u32[]{:S(2)}, u32[]{:S(2)}) collective-permute-start(bf16[128,512]{1,0:T(8,128)(2,1)S(1)} %get-tuple-element.38), channel_id=1, source_target_pairs={{0,16},{8,24},{16,0},{24,8},{32,48},{40,56},{48,32},{56,40},{64,80... | collective-permute-start | bytes 393224 | tf_op jit(solution)/shard_map/ppermute | solution.py:300
  87.3 0.0 collective-permute-done.4
  87.3 6.2 %collective-permute-done.5 = bf16[128,512]{1,0:T(8,128)(2,1)S(1)} collective-permute-done((bf16[128,512]{1,0:T(8,128)(2,1)S(1)}, bf16[128,512]{1,0:T(8,128)(2,1)S(1)}, u32[]{:S(2)}, u32[]{:S(2)}) %collective-permute-start.5) | collective-permute-done | bytes 131104 | tf_op jit(solution)/shard_map/ppermute | solution.py:300
  93.5 0.0 collective-permute-done.6
  93.5 0.7 add_convert_fusion.1
  94.2 1.8 %all-to-all-done.2 = bf16[8,128,256]{2,1,0:T(8,128)(2,1)S(1)} async-done(((bf16[8,128,256]{2,1,0:T(8,128)(2,1)}), bf16[8,128,256]{2,1,0:T(8,128)(2,1)S(1)}, u32[]{:S(2)}, u32[]{:S(2)}) %all-to-all-start.2) | async-done | bytes 524320 | tf_op jit(solution)/shard_map/all_to_all | solution.py:303
  96.0 0.1 reduce_sum.12
  96.1 0.6 fusion
Async XLA Ops:
  3.1 31.6 %all-to-all-start = ((bf16[8,144,256]{2,1,0:T(8,128)(2,1)}), bf16[8,144,256]{2,1,0:T(8,128)(2,1)S(1)}, u32[]{:S(2)}, u32[]{:S(2)}) async-start(bf16[8,144,256]{2,1,0:T(8,128)(2,1)} %get-tuple-element.22), calls=%async_computation | async-start | bytes 1179648 | tf_op jit(solution)/shard_map/all_to_all | solution.py:303
  14.0 17.2 %collective-permute-start.2 = (bf16[144,1024]{1,0:T(8,128)(2,1)}, bf16[144,1024]{1,0:T(8,128)(2,1)S(1)}, u32[]{:S(2)}, u32[]{:S(2)}) collective-permute-start(bf16[144,1024]{1,0:T(8,128)(2,1)} %get-tuple-element.23.refs_0_.refs_2_.refs_4_), channel_id=1, source_target_pairs={{0,32},{8,40},{16,48},{24,56},{32,0},{40,8},{48,16},{56,24},{64,96... | collective-permute-start | bytes 884744 | tf_op jit(solution)/shard_map/ppermute | solution.py:300
  18.2 19.2 %collective-permute-start.1 = (bf16[144,1024]{1,0:T(8,128)(2,1)}, bf16[144,1024]{1,0:T(8,128)(2,1)S(1)}, u32[]{:S(2)}, u32[]{:S(2)}) collective-permute-start(bf16[144,1024]{1,0:T(8,128)(2,1)} %get-tuple-element.23.refs_0_.refs_2_.refs_4_), channel_id=1, source_target_pairs={{0,16},{8,24},{16,0},{24,8},{32,48},{40,56},{48,32},{56,40},{64,80... | collective-permute-start | bytes 884744 | tf_op jit(solution)/shard_map/ppermute | solution.py:300
  31.2 9.3 %collective-permute-start.3 = (bf16[144,1024]{1,0:T(8,128)(2,1)S(1)}, bf16[144,1024]{1,0:T(8,128)(2,1)S(1)}, u32[]{:S(2)}, u32[]{:S(2)}) collective-permute-start(bf16[144,1024]{1,0:T(8,128)(2,1)S(1)} %collective-permute-done.2.refs_0_.refs_2_.refs_4_.refs_6_), channel_id=1, source_target_pairs={{0,16},{8,24},{16,0},{24,8},{32,48},{40,56},{48,32},{56,40},{64,80... | collective-permute-start | bytes 884744 | tf_op jit(solution)/shard_map/ppermute | solution.py:300
  34.7 7.5 %collective-permute-start = (bf16[8,144,256]{2,1,0:T(8,128)(2,1)S(1)}, bf16[8,144,256]{2,1,0:T(8,128)(2,1)S(1)}, u32[]{:S(2)}, u32[]{:S(2)}) collective-permute-start(bf16[8,144,256]{2,1,0:T(8,128)(2,1)S(1)} %all-to-all-done.kv_ref), channel_id=1, source_target_pairs={{0,8},{8,0},{16,24},{24,16},{32,40},{40,32},{48,56},{56,48},{64,72... | collective-permute-start | bytes 1769480 | tf_op jit(solution)/shard_map/ppermute | solution.py:300
  37.4 1.0 copy-start
  60.6 9.8 %collective-permute-start.7 = (bf16[8,128,256]{2,1,0:T(8,128)(2,1)S(1)}, bf16[8,128,256]{2,1,0:T(8,128)(2,1)S(1)}, u32[]{:S(2)}, u32[]{:S(2)}) collective-permute-start(bf16[8,128,256]{2,1,0:T(8,128)(2,1)S(1)} %get-tuple-element.40), channel_id=1, source_target_pairs={{0,8},{8,0},{16,24},{24,16},{32,40},{40,32},{48,56},{56,48},{64,72... | collective-permute-start | bytes 1572872 | tf_op jit(solution)/shard_map/ppermute | solution.py:300
  71.4 24.7 %all-to-all-start.2 = ((bf16[8,128,256]{2,1,0:T(8,128)(2,1)}), bf16[8,128,256]{2,1,0:T(8,128)(2,1)S(1)}, u32[]{:S(2)}, u32[]{:S(2)}) async-start(bf16[8,128,256]{2,1,0:T(8,128)(2,1)} %add_convert_fusion), calls=%async_computation.2 | async-start | bytes 1048576 | tf_op jit(solution)/shard_map/all_to_all | solution.py:303
  78.0 9.3 %collective-permute-start.4 = (bf16[128,512]{1,0:T(8,128)(2,1)S(1)}, bf16[128,512]{1,0:T(8,128)(2,1)S(1)}, u32[]{:S(2)}, u32[]{:S(2)}) collective-permute-start(bf16[128,512]{1,0:T(8,128)(2,1)S(1)} %get-tuple-element.36), channel_id=1, source_target_pairs={{0,48},{8,56},{16,32},{24,40},{32,16},{40,24},{48,0},{56,8},{64,11... | collective-permute-start | bytes 393224 | tf_op jit(solution)/shard_map/ppermute | solution.py:300
  80.4 13.1 %collective-permute-start.5 = (bf16[128,512]{1,0:T(8,128)(2,1)S(1)}, bf16[128,512]{1,0:T(8,128)(2,1)S(1)}, u32[]{:S(2)}, u32[]{:S(2)}) collective-permute-start(bf16[128,512]{1,0:T(8,128)(2,1)S(1)} %get-tuple-element.37), channel_id=1, source_target_pairs={{0,32},{8,40},{16,48},{24,56},{32,0},{40,8},{48,16},{56,24},{64,96... | collective-permute-start | bytes 393224 | tf_op jit(solution)/shard_map/ppermute | solution.py:300
  83.6 9.8 %collective-permute-start.6 = (bf16[128,512]{1,0:T(8,128)(2,1)S(1)}, bf16[128,512]{1,0:T(8,128)(2,1)S(1)}, u32[]{:S(2)}, u32[]{:S(2)}) collective-permute-start(bf16[128,512]{1,0:T(8,128)(2,1)S(1)} %get-tuple-element.38), channel_id=1, source_target_pairs={{0,16},{8,24},{16,0},{24,8},{32,48},{40,56},{48,32},{56,40},{64,80... | collective-permute-start | bytes 393224 | tf_op jit(solution)/shard_map/ppermute | solution.py:300

commit v8 on v7

--- a/solution.py
+++ b/solution.py
@@ -96,7 +96,7 @@
 def score_kernel(n_q, last, kv_ref, *refs):
     q_refs, refs = refs[:n_q], refs[n_q:]
     if last:
-        place_ref, near_ref, far_ref, pt_ref, st_ref, fin_ref, qs, code, bias = refs
+        place_ref, near_own, near_twin, far_own, pt_ref, st_ref, fin_ref, qs, code, bias = refs
     else:
         pt_ref, st_ref, qs, code, bias = refs
     width = n_q * TOK
@@ -128,8 +128,11 @@
             st_ref[step, GROUP + h : GROUP + h + 1, :] = jnp.sum(p, axis=0, keepdims=True)
             pt_ref[rows, h * width : (h + 1) * width] = p.astype(BF16)
     if last:
-        tiles = [jnp.concatenate([near_ref[t], far_ref[t]], axis=1) for t in range(STEPS)]
-        tiles += [st_ref[t] for t in range(STEPS)]
+        tiles = [
+            jnp.concatenate([near_ref[t], far_ref[t]], axis=1)
+            for near_ref, far_ref in ((near_own, far_own), (near_twin, st_ref))
+            for t in range(STEPS)
+        ]
         top = functools.reduce(jnp.maximum, [t[0:GROUP] for t in tiles])
         total = sum(t[GROUP:] * jnp.exp2((t[0:GROUP] - top) * EXP2) for t in tiles)
         for d in range(YS):
@@ -157,7 +160,6 @@
             low = info[0:1, (GROUP + h) * TOK : (GROUP + h + 1) * TOK]
             delta[h : h + 1, toks] = high + low
     dq[...] = dq_in[...] if last else jnp.zeros_like(dq)
-    width = QT // n_parts
 
     top = functools.reduce(jnp.maximum, [all_ref[y, 0:GROUP] for y in range(YS)])
     total = sum(
@@ -174,9 +176,11 @@
         dk = jnp.zeros((KT, HD), F32)
         dv = jnp.zeros((KT, HD), F32)
         for h in range(GROUP):
-            cols = slice(h * width, (h + 1) * width)
             dp = dot(values, gs[h], NT)
-            p = jnp.concatenate([p_ref[rows, cols] for p_ref in p_refs], axis=1)
+            widths = [st_ref.shape[2] for st_ref in st_refs]
+            p = jnp.concatenate(
+                [ref[rows, h * w : (h + 1) * w] for ref, w in zip(p_refs, widths)], axis=1
+            )
             p = p.astype(F32) * weight[h : h + 1]
             ds = (p * (dp - delta[h : h + 1, :])).astype(BF16)
             dv = dv + dot(p.astype(BF16), gs[h])
@@ -228,7 +232,7 @@
 VMEM = pl.BlockSpec(memory_space=pltpu.VMEM)
 SMEM = pl.BlockSpec(memory_space=pltpu.SMEM)
 STATS = (2 * GROUP, QT)
-STATED = {"near": 10**8, "far": 46 * 10**8, "twin": 46 * 10**8, "grads": 6 * 10**9}
+STATED = {"near": 69 * 10**8, "near_twin": 10**8, "far": 10**8, "far_twin": 10**8, "grads": 6 * 10**9}
 
 
 def cost(kind):
@@ -245,7 +249,7 @@
     ]
     if prev is not None:
         args += [place, *prev]
-        in_specs += [SMEM, VMEM, VMEM]
+        in_specs += [SMEM, VMEM, VMEM, VMEM]
         out_shape.append(shape_of((YS, *STATS), F32))
     return pl.pallas_call(
         functools.partial(score_kernel, len(queries), prev is not None),
@@ -311,13 +315,18 @@
     kv_twin = swap(kv_own, 1)
     index = lax.axis_index("ctx").astype(jnp.int32)
     place = (index >> 1 & (YS - 1)).reshape(1)
-    p_near, st_near = scores("near", kv_own, queries[:2])
-    st_near, far = lax.optimization_barrier((st_near, queries[2:]))
-    queries = queries[:2] + far
+    near, far = queries[:3], queries[3:]
+    p_near, st_near = scores("near", kv_own, near)
+    p_near_twin, st_near_twin = scores("near_twin", kv_twin, near)
+    st_near_twin, far = lax.optimization_barrier((st_near_twin, far))
+    queries = near + far
     p_far, st_far = scores("far", kv_own, far)
-    p_twin, st_twin, stats = scores("twin", kv_twin, queries, (st_near, st_far), place)
+    prev = (st_near, st_near_twin, st_far)
+    p_far_twin, st_far_twin, stats = scores("far_twin", kv_twin, far, prev, place)
     all_stats = exchange(stats, tile_groups)
-    dkv_twin, dq = grads(kv_twin, [p_twin], [st_twin], all_stats, queries)
+    dkv_twin, dq = grads(
+        kv_twin, [p_near_twin, p_far_twin], [st_near_twin, st_far_twin], all_stats, queries
+    )
     dkv_back = swap(dkv_twin, 1)
     dkv_own, dq_own, *dq_send = grads(
         kv_own, [p_near, p_far], [st_near, st_far], all_stats, queries, dq

time: 97.3 us -> 94.2 us (0.968)
  blocking collectives: 10.5 us -> 8.72 us
    all_to_all x1, blocking collectives: 10.5 us -> 8.72 us  [exchange(): return lax.all_to_all(x, 'ctx', 0, 0, tiled=True, axis_index_groups=groups)]
    pallas_call x3 -> x4, Pallas kernels: 6.5 us -> 6.32 us  [scores(): pl.pallas_call(functools.partial(score_kernel, len(queries), prev is not...]
  transfers between devices with their start and end apart: 10 -> 10, of which waited for: 4 -> 3; matrix products, arithmetic and copies ran while one was open for 1% -> 1% of each run, Pallas kernels for 8% -> 10%
where the time goes in v8:
time: 94.2 us; the launch traced here: 93.6 us
  starting transfers between devices  44.7 us (47%)
  Pallas kernels  18.3 us (19%)
  waiting for transfers between devices  17.8 us (19%)
  blocking collectives  8.72 us (9%)
  other arithmetic  1.71 us (2%)
  local copies, waits for them, and re-layouts  1.59 us (2%)
    ppermute x8, starting transfers between devices, swap(): return lax.ppermute(x, 'ctx', [(i, i ^ bits) for i in range(n)])  27.2 us
    all_to_all x2, starting transfers between devices, exchange(): return lax.all_to_all(x, 'ctx', 0, 0, tiled=True, axis_index_groups=groups)  17.5 us
    ppermute x8, waiting for transfers between devices, swap(): return lax.ppermute(x, 'ctx', [(i, i ^ bits) for i in range(n)])  16 us
    pallas_call x2, Pallas kernels, grads(): pl.pallas_call(functools.partial(grad_kernel, last, len(probs)), in_specs...  9.52 us
    all_to_all x1, blocking collectives, exchange(): return lax.all_to_all(x, 'ctx', 0, 0, tiled=True, axis_index_groups=groups)  8.72 us
    pallas_call x4, Pallas kernels, scores(): pl.pallas_call(functools.partial(score_kernel, len(queries), prev is not...  6.32 us
    pallas_call x1, Pallas kernels, pack(): pl.pallas_call(pack_kernel, out_shape=(shape_of((ZS, PAY, 2 * HD), BF16),...  2.45 us
  transfers between devices with their start and end apart: 10, of which 3 were waited for; matrix products, arithmetic and copies ran while one was open for 1% of the time, Pallas kernels for 10%

profile of v8, /device:TPU:1, one launch (start us, length us, event | category | flops | bytes accessed | tf_op | source)
XLA Modules:
  0.0 93.6 jit_solution(3940382072776227776)
XLA Ops:
  0.6 2.5 %pack.1 = (bf16[8,144,256]{2,1,0:T(8,128)(2,1)}, bf16[144,1024]{1,0:T(8,128)(2,1)}) custom-call(s32[2]{0:T(128)} %order_hbm.1, s32[1,128]{1,0:T(1,128)} %bitcast.2, bf16[128,512]{1,0:T(8,128)(2,1)} %q_hbm.1, bf16[128,128]{1,0:T(8,128)(2,1)} %k_hbm.1, bf16[128,128]{1,0:T(8,128)(2,1)} %v_hbm.1, bf16[128,512]{1,0:T(8,128)(2,1)} %o_hbm.1, bf16[128,512]{1,0:T(8,128)(2,1)} %g_hbm.1), custom_call_target="tpu_custom_call" | custom-call | tf_op jit(solution)/shard_map/pack/pallas_call | solution.py:213
  3.1 10.9 %all-to-all-start = ((bf16[8,144,256]{2,1,0:T(8,128)(2,1)}), bf16[8,144,256]{2,1,0:T(8,128)(2,1)S(1)}, u32[]{:S(2)}, u32[]{:S(2)}) async-start(bf16[8,144,256]{2,1,0:T(8,128)(2,1)} %get-tuple-element.23), calls=%async_computation | async-start | bytes 1179648 | tf_op jit(solution)/shard_map/all_to_all | solution.py:307
  14.0 4.2 %collective-permute-start.2 = (bf16[144,1024]{1,0:T(8,128)(2,1)}, bf16[144,1024]{1,0:T(8,128)(2,1)S(1)}, u32[]{:S(2)}, u32[]{:S(2)}) collective-permute-start(bf16[144,1024]{1,0:T(8,128)(2,1)} %get-tuple-element.24.refs_0_.refs_4_), channel_id=1, source_target_pairs={{0,32},{8,40},{16,48},{24,56},{32,0},{40,8},{48,16},{56,24},{64,96... | collective-permute-start | bytes 884744 | tf_op jit(solution)/shard_map/ppermute | solution.py:304
  18.2 3.2 %collective-permute-start.1 = (bf16[144,1024]{1,0:T(8,128)(2,1)}, bf16[144,1024]{1,0:T(8,128)(2,1)S(1)}, u32[]{:S(2)}, u32[]{:S(2)}) collective-permute-start(bf16[144,1024]{1,0:T(8,128)(2,1)} %get-tuple-element.24.refs_0_.refs_4_), channel_id=1, source_target_pairs={{0,16},{8,24},{16,0},{24,8},{32,48},{40,56},{48,32},{56,40},{64,80... | collective-permute-start | bytes 884744 | tf_op jit(solution)/shard_map/ppermute | solution.py:304
  21.4 9.8 %collective-permute-done.2.refs_2_.refs_6_ = bf16[144,1024]{1,0:T(8,128)(2,1)S(1)} collective-permute-done((bf16[144,1024]{1,0:T(8,128)(2,1)}, bf16[144,1024]{1,0:T(8,128)(2,1)S(1)}, u32[]{:S(2)}, u32[]{:S(2)}) %collective-permute-start.2) | collective-permute-done | bytes 294944 | tf_op jit(solution)/shard_map/ppermute | solution.py:304
  31.2 3.5 %collective-permute-start.3 = (bf16[144,1024]{1,0:T(8,128)(2,1)S(1)}, bf16[144,1024]{1,0:T(8,128)(2,1)S(1)}, u32[]{:S(2)}, u32[]{:S(2)}) collective-permute-start(bf16[144,1024]{1,0:T(8,128)(2,1)S(1)} %collective-permute-done.2.refs_2_.refs_6_), channel_id=1, source_target_pairs={{0,16},{8,24},{16,0},{24,8},{32,48},{40,56},{48,32},{56,40},{64,80... | collective-permute-start | bytes 884744 | tf_op jit(solution)/shard_map/ppermute | solution.py:304
  34.7 0.0 all-to-all-done.kv_ref
  34.7 2.7 %collective-permute-start = (bf16[8,144,256]{2,1,0:T(8,128)(2,1)S(1)}, bf16[8,144,256]{2,1,0:T(8,128)(2,1)S(1)}, u32[]{:S(2)}, u32[]{:S(2)}) collective-permute-start(bf16[8,144,256]{2,1,0:T(8,128)(2,1)S(1)} %all-to-all-done.kv_ref), channel_id=1, source_target_pairs={{0,8},{8,0},{16,24},{24,16},{32,40},{40,32},{48,56},{56,48},{64,72... | collective-permute-start | bytes 1769480 | tf_op jit(solution)/shard_map/ppermute | solution.py:304
  37.4 0.0 collective-permute-done.1.refs_1_.refs_5_
  37.4 0.0 copy-start
  37.4 1.0 %copy-done = bf16[144,1024]{1,0:T(8,128)(2,1)S(1)} copy-done((bf16[144,1024]{1,0:T(8,128)(2,1)S(1)}, bf16[144,1024]{1,0:T(8,128)(2,1)}, u32[]{:S(2)}) %copy-start) | copy-done | bytes 294936
  38.3 2.2 %scores_near.1 = (bf16[1024,1536]{1,0:T(8,128)(2,1)S(1)}, f32[4,8,384]{2,1,0:T(8,128)S(1)}) custom-call(bf16[8,144,256]{2,1,0:T(8,128)(2,1)S(1)} %all-to-all-done.kv_ref, bf16[144,1024]{1,0:T(8,128)(2,1)S(1)} %copy-done, bf16[144,1024]{1,0:T(8,128)(2,1)S(1)} %collective-permute-done.1.refs_1_.refs_5_, ...), custom_call_target="tpu_custom_call" | custom-call | flops 6899999744 | bytes 65536 | tf_op jit(solution)/shard_map/scores_near/pallas_call | solution.py:254
  40.6 0.0 copy-start.1
  40.6 0.0 collective-permute-done.kv_ref
  40.6 2.2 %scores_near_twin.1 = (bf16[1024,1536]{1,0:T(8,128)(2,1)S(1)}, f32[4,8,384]{2,1,0:T(8,128)S(1)}) custom-call(bf16[8,144,256]{2,1,0:T(8,128)(2,1)S(1)} %collective-permute-done.kv_ref, bf16[144,1024]{1,0:T(8,128)(2,1)S(1)} %copy-done, bf16[144,1024]{1,0:T(8,128)(2,1)S(1)} %collective-permute-done.1.refs_1_.refs_5_, ...), custom_call_target="tpu_custom_call" | custom-call | flops 100000000 | bytes 65536 | tf_op jit(solution)/shard_map/scores_near_twin/pallas_call | solution.py:254
  42.8 0.0 collective-permute-done.3.refs_0_.refs_7_
  42.9 0.9 scores_far.1
  43.8 0.9 scores_far_twin.1
  44.7 8.7 %all_to_all.15.all_ref = f32[4,8,512]{2,1,0:T(8,128)S(1)} all-to-all(f32[4,8,512]{2,1,0:T(8,128)S(1)} %get-tuple-element.30), channel_id=1, replica_groups={{0,16,32,48},{8,24,40,56},{64,80,96,112},{72,88,104,120},{128,144,160,1..., dimensions={0} | all-to-all | bytes 131072 | tf_op jit(solution)/shard_map/all_to_all | solution.py:307
  53.4 0.0 copy-done.1
  53.4 4.7 %grads.2 = (bf16[8,128,256]{2,1,0:T(8,128)(2,1)S(1)}, f32[4,128,512]{2,1,0:T(8,128)S(1)}) custom-call(bf16[8,144,256]{2,1,0:T(8,128)(2,1)S(1)} %collective-permute-done.kv_ref, f32[4,8,512]{2,1,0:T(8,128)S(1)} %all_to_all.15.all_ref, bf16[1024,1536]{1,0:T(8,128)(2,1)S(1)} %get-tuple-element.33.refs_0_, bf16[1024,512]{1,0:T(8,128)(2,1)S(1)} %get-tuple-element.34.refs_1_, ...), custom_call_target="tpu_custom_call" | custom-call | flops 6000000000 | bytes 65536 | tf_op jit(solution)/shard_map/grads/pallas_call | solution.py:286
  58.1 4.4 %collective-permute-start.7 = (bf16[8,128,256]{2,1,0:T(8,128)(2,1)S(1)}, bf16[8,128,256]{2,1,0:T(8,128)(2,1)S(1)}, u32[]{:S(2)}, u32[]{:S(2)}) collective-permute-start(bf16[8,128,256]{2,1,0:T(8,128)(2,1)S(1)} %get-tuple-element.42), channel_id=1, source_target_pairs={{0,8},{8,0},{16,24},{24,16},{32,40},{40,32},{48,56},{56,48},{64,72... | collective-permute-start | bytes 1572872 | tf_op jit(solution)/shard_map/ppermute | solution.py:304
  62.4 4.9 %grads.3 = (f32[8,128,256]{2,1,0:T(8,128)S(1)}, f32[128,512]{1,0:T(8,128)S(1)}, bf16[128,512]{1,0:T(8,128)(2,1)S(1)}, bf16[128,512]{1,0:T(8,128)(2,1)S(1)}, bf16[128,512]{1,0:T(8,128)(2,1)S(1)}) custom-call(bf16[8,144,256]{2,1,0:T(8,128)(2,1)S(1)} %all-to-all-done.kv_ref, f32[4,8,512]{2,1,0:T(8,128)S(1)} %all_to_all.15.all_ref, ...), custom_call_target="tpu_custom_call" | custom-call | flops 6000000000 | bytes 65536 | tf_op jit(solution)/shard_map/grads/pallas_call | solution.py:286
  67.3 0.0 collective-permute-done.7
  67.3 0.9 add_convert_fusion
  68.3 6.7 %all-to-all-start.2 = ((bf16[8,128,256]{2,1,0:T(8,128)(2,1)}), bf16[8,128,256]{2,1,0:T(8,128)(2,1)S(1)}, u32[]{:S(2)}, u32[]{:S(2)}) async-start(bf16[8,128,256]{2,1,0:T(8,128)(2,1)} %add_convert_fusion), calls=%async_computation.2 | async-start | bytes 1048576 | tf_op jit(solution)/shard_map/all_to_all | solution.py:307
  74.9 2.4 %collective-permute-start.4 = (bf16[128,512]{1,0:T(8,128)(2,1)S(1)}, bf16[128,512]{1,0:T(8,128)(2,1)S(1)}, u32[]{:S(2)}, u32[]{:S(2)}) collective-permute-start(bf16[128,512]{1,0:T(8,128)(2,1)S(1)} %get-tuple-element.38), channel_id=1, source_target_pairs={{0,48},{8,56},{16,32},{24,40},{32,16},{40,24},{48,0},{56,8},{64,11... | collective-permute-start | bytes 393224 | tf_op jit(solution)/shard_map/ppermute | solution.py:304
  77.3 3.3 %collective-permute-start.5 = (bf16[128,512]{1,0:T(8,128)(2,1)S(1)}, bf16[128,512]{1,0:T(8,128)(2,1)S(1)}, u32[]{:S(2)}, u32[]{:S(2)}) collective-permute-start(bf16[128,512]{1,0:T(8,128)(2,1)S(1)} %get-tuple-element.39), channel_id=1, source_target_pairs={{0,32},{8,40},{16,48},{24,56},{32,0},{40,8},{48,16},{56,24},{64,96... | collective-permute-start | bytes 393224 | tf_op jit(solution)/shard_map/ppermute | solution.py:304
  80.5 3.6 %collective-permute-start.6 = (bf16[128,512]{1,0:T(8,128)(2,1)S(1)}, bf16[128,512]{1,0:T(8,128)(2,1)S(1)}, u32[]{:S(2)}, u32[]{:S(2)}) collective-permute-start(bf16[128,512]{1,0:T(8,128)(2,1)S(1)} %get-tuple-element.40), channel_id=1, source_target_pairs={{0,16},{8,24},{16,0},{24,8},{32,48},{40,56},{48,32},{56,40},{64,80... | collective-permute-start | bytes 393224 | tf_op jit(solution)/shard_map/ppermute | solution.py:304
  84.2 0.0 collective-permute-done.4
  84.2 6.2 %collective-permute-done.5 = bf16[128,512]{1,0:T(8,128)(2,1)S(1)} collective-permute-done((bf16[128,512]{1,0:T(8,128)(2,1)S(1)}, bf16[128,512]{1,0:T(8,128)(2,1)S(1)}, u32[]{:S(2)}, u32[]{:S(2)}) %collective-permute-start.5) | collective-permute-done | bytes 131104 | tf_op jit(solution)/shard_map/ppermute | solution.py:304
  90.4 0.0 collective-permute-done.6
  90.4 0.7 add_convert_fusion.1
  91.1 1.8 %all-to-all-done.2 = bf16[8,128,256]{2,1,0:T(8,128)(2,1)S(1)} async-done(((bf16[8,128,256]{2,1,0:T(8,128)(2,1)}), bf16[8,128,256]{2,1,0:T(8,128)(2,1)S(1)}, u32[]{:S(2)}, u32[]{:S(2)}) %all-to-all-start.2) | async-done | bytes 524320 | tf_op jit(solution)/shard_map/all_to_all | solution.py:307
  92.9 0.1 reduce_sum.12
  93.0 0.6 fusion
Async XLA Ops:
  3.1 31.6 %all-to-all-start = ((bf16[8,144,256]{2,1,0:T(8,128)(2,1)}), bf16[8,144,256]{2,1,0:T(8,128)(2,1)S(1)}, u32[]{:S(2)}, u32[]{:S(2)}) async-start(bf16[8,144,256]{2,1,0:T(8,128)(2,1)} %get-tuple-element.23), calls=%async_computation | async-start | bytes 1179648 | tf_op jit(solution)/shard_map/all_to_all | solution.py:307
  14.0 17.2 %collective-permute-start.2 = (bf16[144,1024]{1,0:T(8,128)(2,1)}, bf16[144,1024]{1,0:T(8,128)(2,1)S(1)}, u32[]{:S(2)}, u32[]{:S(2)}) collective-permute-start(bf16[144,1024]{1,0:T(8,128)(2,1)} %get-tuple-element.24.refs_0_.refs_4_), channel_id=1, source_target_pairs={{0,32},{8,40},{16,48},{24,56},{32,0},{40,8},{48,16},{56,24},{64,96... | collective-permute-start | bytes 884744 | tf_op jit(solution)/shard_map/ppermute | solution.py:304
  18.2 19.2 %collective-permute-start.1 = (bf16[144,1024]{1,0:T(8,128)(2,1)}, bf16[144,1024]{1,0:T(8,128)(2,1)S(1)}, u32[]{:S(2)}, u32[]{:S(2)}) collective-permute-start(bf16[144,1024]{1,0:T(8,128)(2,1)} %get-tuple-element.24.refs_0_.refs_4_), channel_id=1, source_target_pairs={{0,16},{8,24},{16,0},{24,8},{32,48},{40,56},{48,32},{56,40},{64,80... | collective-permute-start | bytes 884744 | tf_op jit(solution)/shard_map/ppermute | solution.py:304
  31.2 11.7 %collective-permute-start.3 = (bf16[144,1024]{1,0:T(8,128)(2,1)S(1)}, bf16[144,1024]{1,0:T(8,128)(2,1)S(1)}, u32[]{:S(2)}, u32[]{:S(2)}) collective-permute-start(bf16[144,1024]{1,0:T(8,128)(2,1)S(1)} %collective-permute-done.2.refs_2_.refs_6_), channel_id=1, source_target_pairs={{0,16},{8,24},{16,0},{24,8},{32,48},{40,56},{48,32},{56,40},{64,80... | collective-permute-start | bytes 884744 | tf_op jit(solution)/shard_map/ppermute | solution.py:304
  34.7 5.9 %collective-permute-start = (bf16[8,144,256]{2,1,0:T(8,128)(2,1)S(1)}, bf16[8,144,256]{2,1,0:T(8,128)(2,1)S(1)}, u32[]{:S(2)}, u32[]{:S(2)}) collective-permute-start(bf16[8,144,256]{2,1,0:T(8,128)(2,1)S(1)} %all-to-all-done.kv_ref), channel_id=1, source_target_pairs={{0,8},{8,0},{16,24},{24,16},{32,40},{40,32},{48,56},{56,48},{64,72... | collective-permute-start | bytes 1769480 | tf_op jit(solution)/shard_map/ppermute | solution.py:304
  37.4 1.0 %copy-start = (bf16[144,1024]{1,0:T(8,128)(2,1)S(1)}, bf16[144,1024]{1,0:T(8,128)(2,1)}, u32[]{:S(2)}) copy-start(bf16[144,1024]{1,0:T(8,128)(2,1)} %get-tuple-element.24.refs_0_.refs_4_) | copy-start | bytes 884740
  40.6 12.8 %copy-start.1 = (bf16[144,1024]{1,0:T(8,128)(2,1)S(1)}, bf16[144,1024]{1,0:T(8,128)(2,1)}, u32[]{:S(2)}) copy-start(bf16[144,1024]{1,0:T(8,128)(2,1)} %get-tuple-element.24.refs_0_.refs_4_) | copy-start | bytes 884740
  58.1 9.3 %collective-permute-start.7 = (bf16[8,128,256]{2,1,0:T(8,128)(2,1)S(1)}, bf16[8,128,256]{2,1,0:T(8,128)(2,1)S(1)}, u32[]{:S(2)}, u32[]{:S(2)}) collective-permute-start(bf16[8,128,256]{2,1,0:T(8,128)(2,1)S(1)} %get-tuple-element.42), channel_id=1, source_target_pairs={{0,8},{8,0},{16,24},{24,16},{32,40},{40,32},{48,56},{56,48},{64,72... | collective-permute-start | bytes 1572872 | tf_op jit(solution)/shard_map/ppermute | solution.py:304
  68.3 24.7 %all-to-all-start.2 = ((bf16[8,128,256]{2,1,0:T(8,128)(2,1)}), bf16[8,128,256]{2,1,0:T(8,128)(2,1)S(1)}, u32[]{:S(2)}, u32[]{:S(2)}) async-start(bf16[8,128,256]{2,1,0:T(8,128)(2,1)} %add_convert_fusion), calls=%async_computation.2 | async-start | bytes 1048576 | tf_op jit(solution)/shard_map/all_to_all | solution.py:307
  74.9 9.3 %collective-permute-start.4 = (bf16[128,512]{1,0:T(8,128)(2,1)S(1)}, bf16[128,512]{1,0:T(8,128)(2,1)S(1)}, u32[]{:S(2)}, u32[]{:S(2)}) collective-permute-start(bf16[128,512]{1,0:T(8,128)(2,1)S(1)} %get-tuple-element.38), channel_id=1, source_target_pairs={{0,48},{8,56},{16,32},{24,40},{32,16},{40,24},{48,0},{56,8},{64,11... | collective-permute-start | bytes 393224 | tf_op jit(solution)/shard_map/ppermute | solution.py:304
  77.3 13.1 %collective-permute-start.5 = (bf16[128,512]{1,0:T(8,128)(2,1)S(1)}, bf16[128,512]{1,0:T(8,128)(2,1)S(1)}, u32[]{:S(2)}, u32[]{:S(2)}) collective-permute-start(bf16[128,512]{1,0:T(8,128)(2,1)S(1)} %get-tuple-element.39), channel_id=1, source_target_pairs={{0,32},{8,40},{16,48},{24,56},{32,0},{40,8},{48,16},{56,24},{64,96... | collective-permute-start | bytes 393224 | tf_op jit(solution)/shard_map/ppermute | solution.py:304
  80.5 9.8 %collective-permute-start.6 = (bf16[128,512]{1,0:T(8,128)(2,1)S(1)}, bf16[128,512]{1,0:T(8,128)(2,1)S(1)}, u32[]{:S(2)}, u32[]{:S(2)}) collective-permute-start(bf16[128,512]{1,0:T(8,128)(2,1)S(1)} %get-tuple-element.40), channel_id=1, source_target_pairs={{0,16},{8,24},{16,0},{24,8},{32,48},{40,56},{48,32},{56,40},{64,80... | collective-permute-start | bytes 393224 | tf_op jit(solution)/shard_map/ppermute | solution.py:304

commit v9 on v8

--- a/solution.py
+++ b/solution.py
@@ -39,17 +39,17 @@
 
 
 def pack_kernel(
-    order_hbm, seg_hbm, q_hbm, k_hbm, v_hbm, o_hbm, g_hbm, kvp_hbm, qp_ref,
-    order_ref, seg_ref, kv_ref, o_ref, in_sems, out_sems,
+    order_hbm, seg_hbm, q_hbm, k_hbm, v_hbm, o_hbm, g_hbm, kvp_hbm, qp_hbm,
+    order_ref, seg_ref, kv_ref, o_ref, g_ref, q_ref, extra_ref, in_sems, out_sems,
 ):
     moves = (
         (order_hbm, order_ref),
         (seg_hbm, seg_ref),
         (k_hbm, kv_ref.at[0:TOK, 0:HD]),
         (v_hbm, kv_ref.at[0:TOK, HD : 2 * HD]),
-        (q_hbm, qp_ref.at[0:TOK, 0:WIDE]),
-        (g_hbm, qp_ref.at[0:TOK, WIDE : 2 * WIDE]),
         (o_hbm, o_ref),
+        (g_hbm, g_ref),
+        (q_hbm, q_ref),
     )
     copies = [
         pltpu.make_async_copy(src, dst, in_sems.at[i]) for i, (src, dst) in enumerate(moves)
@@ -70,10 +70,13 @@
         copy.start()
     for copy in copies[4:]:
         copy.wait()
+    for src, dst in ((q_ref, qp_hbm.at[0:TOK, 0:WIDE]), (g_ref, qp_hbm.at[0:TOK, WIDE : 2 * WIDE])):
+        outs.append(pltpu.make_async_copy(src, dst, out_sems.at[len(outs)]))
+        outs[-1].start()
     highs, lows = [], []
     for h in range(GROUP):
         cols = slice(h * HD, (h + 1) * HD)
-        prod = qp_ref[0:TOK, WIDE + h * HD : WIDE + (h + 1) * HD].astype(F32) * o_ref[:, cols].astype(F32)
+        prod = g_ref[:, cols].astype(F32) * o_ref[:, cols].astype(F32)
         delta = jnp.sum(prod.T, axis=0, keepdims=True)
         high = delta.astype(BF16).astype(F32)
         highs.append(high)
@@ -82,7 +85,9 @@
     first = jnp.concatenate(highs + lows, axis=1)
     second = jnp.concatenate([doc, block] + [zero] * 6, axis=1)
     row = lax.broadcasted_iota(jnp.int32, (EXTRA, 2 * WIDE), 0)
-    qp_ref[TOK:PAY, :] = jnp.where(row == 0, first, second).astype(BF16)
+    extra_ref[...] = jnp.where(row == 0, first, second).astype(BF16)
+    outs.append(pltpu.make_async_copy(extra_ref, qp_hbm.at[TOK:PAY], out_sems.at[len(outs)]))
+    outs[-1].start()
     for copy in outs:
         copy.wait()
 
@@ -166,31 +171,37 @@
         all_ref[y, GROUP : 2 * GROUP] * jnp.exp2((all_ref[y, 0:GROUP] - top) * EXP2)
         for y in range(YS)
     )
-    for step in range(STEPS):
-        rows = slice(step * KT, (step + 1) * KT)
-        peaks = jnp.concatenate([st_ref[step, 0:GROUP] for st_ref in st_refs], axis=1)
-        weight = jnp.exp2((peaks - top) * EXP2) / total
-        pair = [kv_ref[2 * step + b, 0:TOK] for b in range(2)]
-        keys = jnp.concatenate([part[:, 0:HD] for part in pair], axis=0)
-        values = jnp.concatenate([part[:, HD : 2 * HD] for part in pair], axis=0)
-        dk = jnp.zeros((KT, HD), F32)
-        dv = jnp.zeros((KT, HD), F32)
+    for first in range(0, STEPS, 2):
+        tiles = (first, first + 1)
+        weights = []
+        for tile in tiles:
+            peaks = jnp.concatenate([st_ref[tile, 0:GROUP] for st_ref in st_refs], axis=1)
+            weights.append(jnp.exp2((peaks - top) * EXP2) / total)
+        blocks = range(2 * first, 2 * first + 4)
+        keys = jnp.concatenate([kv_ref[b, 0:TOK, 0:HD] for b in blocks], axis=0)
+        values = jnp.concatenate([kv_ref[b, 0:TOK, HD : 2 * HD] for b in blocks], axis=0)
+        dk = jnp.zeros((2 * KT, HD), F32)
+        dv = jnp.zeros((2 * KT, HD), F32)
         for h in range(GROUP):
             dp = dot(values, gs[h], NT)
-            widths = [st_ref.shape[2] for st_ref in st_refs]
-            p = jnp.concatenate(
-                [ref[rows, h * w : (h + 1) * w] for ref, w in zip(p_refs, widths)], axis=1
-            )
-            p = p.astype(F32) * weight[h : h + 1]
+            parts = []
+            for tile, weight in zip(tiles, weights):
+                rows = slice(tile * KT, (tile + 1) * KT)
+                widths = [st_ref.shape[2] for st_ref in st_refs]
+                part = jnp.concatenate(
+                    [ref[rows, h * w : (h + 1) * w] for ref, w in zip(p_refs, widths)], axis=1
+                )
+                parts.append(part.astype(F32) * weight[h : h + 1])
+            p = jnp.concatenate(parts, axis=0)
             ds = (p * (dp - delta[h : h + 1, :])).astype(BF16)
             dv = dv + dot(p.astype(BF16), gs[h])
             dk = dk + dot(ds, qs[h])
             dq[h] += dot(keys, ds, TN)
         dk = dk * SCALE
-        for b in range(2):
-            half = slice(b * TOK, (b + 1) * TOK)
-            dkv_ref[2 * step + b, :, 0:HD] = dk[half].astype(dkv_ref.dtype)
-            dkv_ref[2 * step + b, :, HD : 2 * HD] = dv[half].astype(dkv_ref.dtype)
+        for i, b in enumerate(blocks):
+            rows = slice(i * TOK, (i + 1) * TOK)
+            dkv_ref[b, :, 0:HD] = dk[rows].astype(dkv_ref.dtype)
+            dkv_ref[b, :, HD : 2 * HD] = dv[rows].astype(dkv_ref.dtype)
 
     if last:
         for x, out in enumerate((own_ref, send1, send2, send3)):
@@ -209,19 +220,21 @@
 
 def pack(order, seg, q, k, v, o, g):
     hbm = pl.BlockSpec(memory_space=pltpu.HBM)
-    vm = pl.BlockSpec(memory_space=pltpu.VMEM)
     return pl.pallas_call(
         pack_kernel,
         out_shape=(shape_of((ZS, PAY, 2 * HD), BF16), shape_of((PAY, 2 * WIDE), BF16)),
         in_specs=[hbm] * 7,
-        out_specs=(hbm, vm),
+        out_specs=(hbm, hbm),
         scratch_shapes=[
             pltpu.SMEM((2,), jnp.int32),
             pltpu.VMEM((1, TOK), jnp.int32),
             pltpu.VMEM((PAY, 2 * HD), BF16),
-            pltpu.VMEM((TOK, GROUP * HD), BF16),
+            pltpu.VMEM((TOK, WIDE), BF16),
+            pltpu.VMEM((TOK, WIDE), BF16),
+            pltpu.VMEM((TOK, WIDE), BF16),
+            pltpu.VMEM((EXTRA, 2 * WIDE), BF16),
             pltpu.SemaphoreType.DMA((7,)),
-            pltpu.SemaphoreType.DMA((ZS,)),
+            pltpu.SemaphoreType.DMA((ZS + 3,)),
         ],
         compiler_params=params(60),
         name="pack",

time: 94.2 us -> 93.3 us (level)
  no operation moved by 1% of the time
where the time goes in v9:
time: 93.3 us; the launch traced here: 92.8 us
  starting transfers between devices  44.7 us (48%)
  waiting for transfers between devices  17.8 us (19%)
  Pallas kernels  17.5 us (19%)
  blocking collectives  8.71 us (9%)
  other arithmetic  1.71 us (2%)
  local copies, waits for them, and re-layouts  1.59 us (2%)
    ppermute x8, starting transfers between devices, swap(): return lax.ppermute(x, 'ctx', [(i, i ^ bits) for i in range(n)])  27.2 us
    all_to_all x2, starting transfers between devices, exchange(): return lax.all_to_all(x, 'ctx', 0, 0, tiled=True, axis_index_groups=groups)  17.5 us
    ppermute x8, waiting for transfers between devices, swap(): return lax.ppermute(x, 'ctx', [(i, i ^ bits) for i in range(n)])  16 us
    pallas_call x2, Pallas kernels, grads(): pl.pallas_call(functools.partial(grad_kernel, last, len(probs)), in_specs...  9.14 us
    all_to_all x1, blocking collectives, exchange(): return lax.all_to_all(x, 'ctx', 0, 0, tiled=True, axis_index_groups=groups)  8.71 us
    pallas_call x4, Pallas kernels, scores(): pl.pallas_call(functools.partial(score_kernel, len(queries), prev is not...  6.33 us
    pallas_call x1, Pallas kernels, pack(): pl.pallas_call(pack_kernel, out_shape=(shape_of((ZS, PAY, 2 * HD), BF16),...  1.99 us
  transfers between devices with their start and end apart: 10, of which 3 were waited for; matrix products, arithmetic and copies ran while one was open for 1% of the time, Pallas kernels for 10%

profile of v9, /device:TPU:1, one launch (start us, length us, event | category | flops | bytes accessed | tf_op | source)
XLA Modules:
  0.0 92.8 jit_solution(390519571783518854)
XLA Ops:
  0.6 2.0 %pack.1 = (bf16[8,144,256]{2,1,0:T(8,128)(2,1)}, bf16[144,1024]{1,0:T(8,128)(2,1)}) custom-call(s32[2]{0:T(128)} %order_hbm.1, s32[1,128]{1,0:T(1,128)} %bitcast.2, bf16[128,512]{1,0:T(8,128)(2,1)} %q_hbm.1, bf16[128,128]{1,0:T(8,128)(2,1)} %k_hbm.1, bf16[128,128]{1,0:T(8,128)(2,1)} %v_hbm.1, bf16[128,512]{1,0:T(8,128)(2,1)} %o_hbm.1, bf16[128,512]{1,0:T(8,128)(2,1)} %g_hbm.1), custom_call_target="tpu_custom_call" | custom-call | tf_op jit(solution)/shard_map/pack/pallas_call | solution.py:223
  2.6 10.9 %all-to-all-start = ((bf16[8,144,256]{2,1,0:T(8,128)(2,1)}), bf16[8,144,256]{2,1,0:T(8,128)(2,1)S(1)}, u32[]{:S(2)}, u32[]{:S(2)}) async-start(bf16[8,144,256]{2,1,0:T(8,128)(2,1)} %get-tuple-element.23), calls=%async_computation | async-start | bytes 1179648 | tf_op jit(solution)/shard_map/all_to_all | solution.py:320
  13.5 4.2 %collective-permute-start.2 = (bf16[144,1024]{1,0:T(8,128)(2,1)}, bf16[144,1024]{1,0:T(8,128)(2,1)S(1)}, u32[]{:S(2)}, u32[]{:S(2)}) collective-permute-start(bf16[144,1024]{1,0:T(8,128)(2,1)} %get-tuple-element.24.refs_0_.refs_4_), channel_id=1, source_target_pairs={{0,32},{8,40},{16,48},{24,56},{32,0},{40,8},{48,16},{56,24},{64,96... | collective-permute-start | bytes 884744 | tf_op jit(solution)/shard_map/ppermute | solution.py:317
  17.7 3.2 %collective-permute-start.1 = (bf16[144,1024]{1,0:T(8,128)(2,1)}, bf16[144,1024]{1,0:T(8,128)(2,1)S(1)}, u32[]{:S(2)}, u32[]{:S(2)}) collective-permute-start(bf16[144,1024]{1,0:T(8,128)(2,1)} %get-tuple-element.24.refs_0_.refs_4_), channel_id=1, source_target_pairs={{0,16},{8,24},{16,0},{24,8},{32,48},{40,56},{48,32},{56,40},{64,80... | collective-permute-start | bytes 884744 | tf_op jit(solution)/shard_map/ppermute | solution.py:317
  20.9 9.8 %collective-permute-done.2.refs_2_.refs_6_ = bf16[144,1024]{1,0:T(8,128)(2,1)S(1)} collective-permute-done((bf16[144,1024]{1,0:T(8,128)(2,1)}, bf16[144,1024]{1,0:T(8,128)(2,1)S(1)}, u32[]{:S(2)}, u32[]{:S(2)}) %collective-permute-start.2) | collective-permute-done | bytes 294944 | tf_op jit(solution)/shard_map/ppermute | solution.py:317
  30.7 3.5 %collective-permute-start.3 = (bf16[144,1024]{1,0:T(8,128)(2,1)S(1)}, bf16[144,1024]{1,0:T(8,128)(2,1)S(1)}, u32[]{:S(2)}, u32[]{:S(2)}) collective-permute-start(bf16[144,1024]{1,0:T(8,128)(2,1)S(1)} %collective-permute-done.2.refs_2_.refs_6_), channel_id=1, source_target_pairs={{0,16},{8,24},{16,0},{24,8},{32,48},{40,56},{48,32},{56,40},{64,80... | collective-permute-start | bytes 884744 | tf_op jit(solution)/shard_map/ppermute | solution.py:317
  34.2 0.0 all-to-all-done.kv_ref
  34.2 2.7 %collective-permute-start = (bf16[8,144,256]{2,1,0:T(8,128)(2,1)S(1)}, bf16[8,144,256]{2,1,0:T(8,128)(2,1)S(1)}, u32[]{:S(2)}, u32[]{:S(2)}) collective-permute-start(bf16[8,144,256]{2,1,0:T(8,128)(2,1)S(1)} %all-to-all-done.kv_ref), channel_id=1, source_target_pairs={{0,8},{8,0},{16,24},{24,16},{32,40},{40,32},{48,56},{56,48},{64,72... | collective-permute-start | bytes 1769480 | tf_op jit(solution)/shard_map/ppermute | solution.py:317
  36.9 0.0 collective-permute-done.1.refs_1_.refs_5_
  36.9 0.0 copy-start
  36.9 1.0 %copy-done = bf16[144,1024]{1,0:T(8,128)(2,1)S(1)} copy-done((bf16[144,1024]{1,0:T(8,128)(2,1)S(1)}, bf16[144,1024]{1,0:T(8,128)(2,1)}, u32[]{:S(2)}) %copy-start) | copy-done | bytes 294936
  37.9 2.2 %scores_near.1 = (bf16[1024,1536]{1,0:T(8,128)(2,1)S(1)}, f32[4,8,384]{2,1,0:T(8,128)S(1)}) custom-call(bf16[8,144,256]{2,1,0:T(8,128)(2,1)S(1)} %all-to-all-done.kv_ref, bf16[144,1024]{1,0:T(8,128)(2,1)S(1)} %copy-done, bf16[144,1024]{1,0:T(8,128)(2,1)S(1)} %collective-permute-done.1.refs_1_.refs_5_, ...), custom_call_target="tpu_custom_call" | custom-call | flops 6899999744 | bytes 65536 | tf_op jit(solution)/shard_map/scores_near/pallas_call | solution.py:267
  40.1 0.0 copy-start.1
  40.1 0.0 collective-permute-done.kv_ref
  40.1 2.3 %scores_near_twin.1 = (bf16[1024,1536]{1,0:T(8,128)(2,1)S(1)}, f32[4,8,384]{2,1,0:T(8,128)S(1)}) custom-call(bf16[8,144,256]{2,1,0:T(8,128)(2,1)S(1)} %collective-permute-done.kv_ref, bf16[144,1024]{1,0:T(8,128)(2,1)S(1)} %copy-done, bf16[144,1024]{1,0:T(8,128)(2,1)S(1)} %collective-permute-done.1.refs_1_.refs_5_, ...), custom_call_target="tpu_custom_call" | custom-call | flops 100000000 | bytes 65536 | tf_op jit(solution)/shard_map/scores_near_twin/pallas_call | solution.py:267
  42.4 0.0 collective-permute-done.3.refs_0_.refs_7_
  42.4 0.9 scores_far.1
  43.3 0.9 scores_far_twin.1
  44.2 8.7 %all_to_all.15.all_ref = f32[4,8,512]{2,1,0:T(8,128)S(1)} all-to-all(f32[4,8,512]{2,1,0:T(8,128)S(1)} %get-tuple-element.30), channel_id=1, replica_groups={{0,16,32,48},{8,24,40,56},{64,80,96,112},{72,88,104,120},{128,144,160,1..., dimensions={0} | all-to-all | bytes 131072 | tf_op jit(solution)/shard_map/all_to_all | solution.py:320
  52.9 0.0 copy-done.1
  52.9 4.5 %grads.2 = (bf16[8,128,256]{2,1,0:T(8,128)(2,1)S(1)}, f32[4,128,512]{2,1,0:T(8,128)S(1)}) custom-call(bf16[8,144,256]{2,1,0:T(8,128)(2,1)S(1)} %collective-permute-done.kv_ref, f32[4,8,512]{2,1,0:T(8,128)S(1)} %all_to_all.15.all_ref, bf16[1024,1536]{1,0:T(8,128)(2,1)S(1)} %get-tuple-element.33.refs_0_, bf16[1024,512]{1,0:T(8,128)(2,1)S(1)} %get-tuple-element.34.refs_1_, ...), custom_call_target="tpu_custom_call" | custom-call | flops 6000000000 | bytes 65536 | tf_op jit(solution)/shard_map/grads/pallas_call | solution.py:299
  57.4 4.4 %collective-permute-start.7 = (bf16[8,128,256]{2,1,0:T(8,128)(2,1)S(1)}, bf16[8,128,256]{2,1,0:T(8,128)(2,1)S(1)}, u32[]{:S(2)}, u32[]{:S(2)}) collective-permute-start(bf16[8,128,256]{2,1,0:T(8,128)(2,1)S(1)} %get-tuple-element.42), channel_id=1, source_target_pairs={{0,8},{8,0},{16,24},{24,16},{32,40},{40,32},{48,56},{56,48},{64,72... | collective-permute-start | bytes 1572872 | tf_op jit(solution)/shard_map/ppermute | solution.py:317
  61.8 4.6 %grads.3 = (f32[8,128,256]{2,1,0:T(8,128)S(1)}, f32[128,512]{1,0:T(8,128)S(1)}, bf16[128,512]{1,0:T(8,128)(2,1)S(1)}, bf16[128,512]{1,0:T(8,128)(2,1)S(1)}, bf16[128,512]{1,0:T(8,128)(2,1)S(1)}) custom-call(bf16[8,144,256]{2,1,0:T(8,128)(2,1)S(1)} %all-to-all-done.kv_ref, f32[4,8,512]{2,1,0:T(8,128)S(1)} %all_to_all.15.all_ref, ...), custom_call_target="tpu_custom_call" | custom-call | flops 6000000000 | bytes 65536 | tf_op jit(solution)/shard_map/grads/pallas_call | solution.py:299
  66.5 0.0 collective-permute-done.7
  66.5 0.9 add_convert_fusion
  67.4 6.6 %all-to-all-start.2 = ((bf16[8,128,256]{2,1,0:T(8,128)(2,1)}), bf16[8,128,256]{2,1,0:T(8,128)(2,1)S(1)}, u32[]{:S(2)}, u32[]{:S(2)}) async-start(bf16[8,128,256]{2,1,0:T(8,128)(2,1)} %add_convert_fusion), calls=%async_computation.2 | async-start | bytes 1048576 | tf_op jit(solution)/shard_map/all_to_all | solution.py:320
  74.0 2.4 %collective-permute-start.4 = (bf16[128,512]{1,0:T(8,128)(2,1)S(1)}, bf16[128,512]{1,0:T(8,128)(2,1)S(1)}, u32[]{:S(2)}, u32[]{:S(2)}) collective-permute-start(bf16[128,512]{1,0:T(8,128)(2,1)S(1)} %get-tuple-element.38), channel_id=1, source_target_pairs={{0,48},{8,56},{16,32},{24,40},{32,16},{40,24},{48,0},{56,8},{64,11... | collective-permute-start | bytes 393224 | tf_op jit(solution)/shard_map/ppermute | solution.py:317
  76.4 3.3 %collective-permute-start.5 = (bf16[128,512]{1,0:T(8,128)(2,1)S(1)}, bf16[128,512]{1,0:T(8,128)(2,1)S(1)}, u32[]{:S(2)}, u32[]{:S(2)}) collective-permute-start(bf16[128,512]{1,0:T(8,128)(2,1)S(1)} %get-tuple-element.39), channel_id=1, source_target_pairs={{0,32},{8,40},{16,48},{24,56},{32,0},{40,8},{48,16},{56,24},{64,96... | collective-permute-start | bytes 393224 | tf_op jit(solution)/shard_map/ppermute | solution.py:317
  79.7 3.6 %collective-permute-start.6 = (bf16[128,512]{1,0:T(8,128)(2,1)S(1)}, bf16[128,512]{1,0:T(8,128)(2,1)S(1)}, u32[]{:S(2)}, u32[]{:S(2)}) collective-permute-start(bf16[128,512]{1,0:T(8,128)(2,1)S(1)} %get-tuple-element.40), channel_id=1, source_target_pairs={{0,16},{8,24},{16,0},{24,8},{32,48},{40,56},{48,32},{56,40},{64,80... | collective-permute-start | bytes 393224 | tf_op jit(solution)/shard_map/ppermute | solution.py:317
  83.3 0.0 collective-permute-done.4
  83.3 6.2 %collective-permute-done.5 = bf16[128,512]{1,0:T(8,128)(2,1)S(1)} collective-permute-done((bf16[128,512]{1,0:T(8,128)(2,1)S(1)}, bf16[128,512]{1,0:T(8,128)(2,1)S(1)}, u32[]{:S(2)}, u32[]{:S(2)}) %collective-permute-start.5) | collective-permute-done | bytes 131104 | tf_op jit(solution)/shard_map/ppermute | solution.py:317
  89.5 0.0 collective-permute-done.6
  89.5 0.7 add_convert_fusion.1
  90.2 1.8 %all-to-all-done.2 = bf16[8,128,256]{2,1,0:T(8,128)(2,1)S(1)} async-done(((bf16[8,128,256]{2,1,0:T(8,128)(2,1)}), bf16[8,128,256]{2,1,0:T(8,128)(2,1)S(1)}, u32[]{:S(2)}, u32[]{:S(2)}) %all-to-all-start.2) | async-done | bytes 524320 | tf_op jit(solution)/shard_map/all_to_all | solution.py:320
  92.1 0.1 reduce_sum.12
  92.1 0.6 fusion
Async XLA Ops:
  2.6 31.6 %all-to-all-start = ((bf16[8,144,256]{2,1,0:T(8,128)(2,1)}), bf16[8,144,256]{2,1,0:T(8,128)(2,1)S(1)}, u32[]{:S(2)}, u32[]{:S(2)}) async-start(bf16[8,144,256]{2,1,0:T(8,128)(2,1)} %get-tuple-element.23), calls=%async_computation | async-start | bytes 1179648 | tf_op jit(solution)/shard_map/all_to_all | solution.py:320
  13.5 17.2 %collective-permute-start.2 = (bf16[144,1024]{1,0:T(8,128)(2,1)}, bf16[144,1024]{1,0:T(8,128)(2,1)S(1)}, u32[]{:S(2)}, u32[]{:S(2)}) collective-permute-start(bf16[144,1024]{1,0:T(8,128)(2,1)} %get-tuple-element.24.refs_0_.refs_4_), channel_id=1, source_target_pairs={{0,32},{8,40},{16,48},{24,56},{32,0},{40,8},{48,16},{56,24},{64,96... | collective-permute-start | bytes 884744 | tf_op jit(solution)/shard_map/ppermute | solution.py:317
  17.7 19.2 %collective-permute-start.1 = (bf16[144,1024]{1,0:T(8,128)(2,1)}, bf16[144,1024]{1,0:T(8,128)(2,1)S(1)}, u32[]{:S(2)}, u32[]{:S(2)}) collective-permute-start(bf16[144,1024]{1,0:T(8,128)(2,1)} %get-tuple-element.24.refs_0_.refs_4_), channel_id=1, source_target_pairs={{0,16},{8,24},{16,0},{24,8},{32,48},{40,56},{48,32},{56,40},{64,80... | collective-permute-start | bytes 884744 | tf_op jit(solution)/shard_map/ppermute | solution.py:317
  30.7 11.7 %collective-permute-start.3 = (bf16[144,1024]{1,0:T(8,128)(2,1)S(1)}, bf16[144,1024]{1,0:T(8,128)(2,1)S(1)}, u32[]{:S(2)}, u32[]{:S(2)}) collective-permute-start(bf16[144,1024]{1,0:T(8,128)(2,1)S(1)} %collective-permute-done.2.refs_2_.refs_6_), channel_id=1, source_target_pairs={{0,16},{8,24},{16,0},{24,8},{32,48},{40,56},{48,32},{56,40},{64,80... | collective-permute-start | bytes 884744 | tf_op jit(solution)/shard_map/ppermute | solution.py:317
  34.2 5.9 %collective-permute-start = (bf16[8,144,256]{2,1,0:T(8,128)(2,1)S(1)}, bf16[8,144,256]{2,1,0:T(8,128)(2,1)S(1)}, u32[]{:S(2)}, u32[]{:S(2)}) collective-permute-start(bf16[8,144,256]{2,1,0:T(8,128)(2,1)S(1)} %all-to-all-done.kv_ref), channel_id=1, source_target_pairs={{0,8},{8,0},{16,24},{24,16},{32,40},{40,32},{48,56},{56,48},{64,72... | collective-permute-start | bytes 1769480 | tf_op jit(solution)/shard_map/ppermute | solution.py:317
  36.9 1.0 %copy-start = (bf16[144,1024]{1,0:T(8,128)(2,1)S(1)}, bf16[144,1024]{1,0:T(8,128)(2,1)}, u32[]{:S(2)}) copy-start(bf16[144,1024]{1,0:T(8,128)(2,1)} %get-tuple-element.24.refs_0_.refs_4_) | copy-start | bytes 884740
  40.1 12.8 %copy-start.1 = (bf16[144,1024]{1,0:T(8,128)(2,1)S(1)}, bf16[144,1024]{1,0:T(8,128)(2,1)}, u32[]{:S(2)}) copy-start(bf16[144,1024]{1,0:T(8,128)(2,1)} %get-tuple-element.24.refs_0_.refs_4_) | copy-start | bytes 884740
  57.4 9.0 %collective-permute-start.7 = (bf16[8,128,256]{2,1,0:T(8,128)(2,1)S(1)}, bf16[8,128,256]{2,1,0:T(8,128)(2,1)S(1)}, u32[]{:S(2)}, u32[]{:S(2)}) collective-permute-start(bf16[8,128,256]{2,1,0:T(8,128)(2,1)S(1)} %get-tuple-element.42), channel_id=1, source_target_pairs={{0,8},{8,0},{16,24},{24,16},{32,40},{40,32},{48,56},{56,48},{64,72... | collective-permute-start | bytes 1572872 | tf_op jit(solution)/shard_map/ppermute | solution.py:317
  67.4 24.7 %all-to-all-start.2 = ((bf16[8,128,256]{2,1,0:T(8,128)(2,1)}), bf16[8,128,256]{2,1,0:T(8,128)(2,1)S(1)}, u32[]{:S(2)}, u32[]{:S(2)}) async-start(bf16[8,128,256]{2,1,0:T(8,128)(2,1)} %add_convert_fusion), calls=%async_computation.2 | async-start | bytes 1048576 | tf_op jit(solution)/shard_map/all_to_all | solution.py:320
  74.0 9.3 %collective-permute-start.4 = (bf16[128,512]{1,0:T(8,128)(2,1)S(1)}, bf16[128,512]{1,0:T(8,128)(2,1)S(1)}, u32[]{:S(2)}, u32[]{:S(2)}) collective-permute-start(bf16[128,512]{1,0:T(8,128)(2,1)S(1)} %get-tuple-element.38), channel_id=1, source_target_pairs={{0,48},{8,56},{16,32},{24,40},{32,16},{40,24},{48,0},{56,8},{64,11... | collective-permute-start | bytes 393224 | tf_op jit(solution)/shard_map/ppermute | solution.py:317
  76.4 13.1 %collective-permute-start.5 = (bf16[128,512]{1,0:T(8,128)(2,1)S(1)}, bf16[128,512]{1,0:T(8,128)(2,1)S(1)}, u32[]{:S(2)}, u32[]{:S(2)}) collective-permute-start(bf16[128,512]{1,0:T(8,128)(2,1)S(1)} %get-tuple-element.39), channel_id=1, source_target_pairs={{0,32},{8,40},{16,48},{24,56},{32,0},{40,8},{48,16},{56,24},{64,96... | collective-permute-start | bytes 393224 | tf_op jit(solution)/shard_map/ppermute | solution.py:317
  79.7 9.8 %collective-permute-start.6 = (bf16[128,512]{1,0:T(8,128)(2,1)S(1)}, bf16[128,512]{1,0:T(8,128)(2,1)S(1)}, u32[]{:S(2)}, u32[]{:S(2)}) collective-permute-start(bf16[128,512]{1,0:T(8,128)(2,1)S(1)} %get-tuple-element.40), channel_id=1, source_target_pairs={{0,16},{8,24},{16,0},{24,8},{32,48},{40,56},{48,32},{56,40},{64,80... | collective-permute-start | bytes 393224 | tf_op jit(solution)/shard_map/ppermute | solution.py:317

commit v10 on v9

--- a/solution.py
+++ b/solution.py
@@ -245,7 +245,7 @@
 VMEM = pl.BlockSpec(memory_space=pltpu.VMEM)
 SMEM = pl.BlockSpec(memory_space=pltpu.SMEM)
 STATS = (2 * GROUP, QT)
-STATED = {"near": 69 * 10**8, "near_twin": 10**8, "far": 10**8, "far_twin": 10**8, "grads": 6 * 10**9}
+STATED = {"near": 46 * 10**8, "near_twin": 10**8, "far": 10**8, "far_twin": 10**8, "grads": 6 * 10**9}
 
 
 def cost(kind):

time: 93.3 us -> 93.8 us (level)
  waiting for transfers between devices: 17.8 us -> 21.7 us
  starting transfers between devices: 44.7 us -> 40.9 us
    all_to_all x2, waiting for transfers between devices: 1.85 us -> 13.4 us  [exchange(): return lax.all_to_all(x, 'ctx', 0, 0, tiled=True, axis_index_groups=groups)]
    ppermute x8, waiting for transfers between devices: 16 us -> 8.32 us  [swap(): return lax.ppermute(x, 'ctx', [(i, i ^ bits) for i in range(n)])]
    all_to_all x2, starting transfers between devices: 17.5 us -> 14.4 us  [exchange(): return lax.all_to_all(x, 'ctx', 0, 0, tiled=True, axis_index_groups=groups)]
  transfers between devices with their start and end apart: 10 -> 10, of which waited for: 3 -> 4; matrix products, arithmetic and copies ran while one was open for 1% -> 1% of each run, Pallas kernels for 10% -> 10%
where the time goes in v10:
time: 93.8 us; the launch traced here: 93.2 us
  starting transfers between devices  40.9 us (44%)
  waiting for transfers between devices  21.7 us (23%)
  Pallas kernels  17.4 us (19%)
  blocking collectives  9 us (10%)
  other arithmetic  1.71 us (2%)
  local copies, waits for them, and re-layouts  1.59 us (2%)
    ppermute x8, starting transfers between devices, swap(): return lax.ppermute(x, 'ctx', [(i, i ^ bits) for i in range(n)])  26.6 us
    all_to_all x2, starting transfers between devices, exchange(): return lax.all_to_all(x, 'ctx', 0, 0, tiled=True, axis_index_groups=groups)  14.4 us
    all_to_all x2, waiting for transfers between devices, exchange(): return lax.all_to_all(x, 'ctx', 0, 0, tiled=True, axis_index_groups=groups)  13.4 us
    pallas_call x2, Pallas kernels, grads(): pl.pallas_call(functools.partial(grad_kernel, last, len(probs)), in_specs...  9.13 us
    all_to_all x1, blocking collectives, exchange(): return lax.all_to_all(x, 'ctx', 0, 0, tiled=True, axis_index_groups=groups)  9 us
    ppermute x8, waiting for transfers between devices, swap(): return lax.ppermute(x, 'ctx', [(i, i ^ bits) for i in range(n)])  8.32 us
    pallas_call x4, Pallas kernels, scores(): pl.pallas_call(functools.partial(score_kernel, len(queries), prev is not...  6.31 us
    pallas_call x1, Pallas kernels, pack(): pl.pallas_call(pack_kernel, out_shape=(shape_of((ZS, PAY, 2 * HD), BF16),...  1.99 us
  transfers between devices with their start and end apart: 10, of which 4 were waited for; matrix products, arithmetic and copies ran while one was open for 1% of the time, Pallas kernels for 10%

profile of v10, /device:TPU:1, one launch (start us, length us, event | category | flops | bytes accessed | tf_op | source)
XLA Modules:
  0.0 93.2 jit_solution(9910255967327566918)
XLA Ops:
  0.6 2.0 %pack.1 = (bf16[8,144,256]{2,1,0:T(8,128)(2,1)}, bf16[144,1024]{1,0:T(8,128)(2,1)}) custom-call(s32[2]{0:T(128)} %order_hbm.1, s32[1,128]{1,0:T(1,128)} %bitcast.2, bf16[128,512]{1,0:T(8,128)(2,1)} %q_hbm.1, bf16[128,128]{1,0:T(8,128)(2,1)} %k_hbm.1, bf16[128,128]{1,0:T(8,128)(2,1)} %v_hbm.1, bf16[128,512]{1,0:T(8,128)(2,1)} %o_hbm.1, bf16[128,512]{1,0:T(8,128)(2,1)} %g_hbm.1), custom_call_target="tpu_custom_call" | custom-call | tf_op jit(solution)/shard_map/pack/pallas_call | solution.py:223
  2.6 10.9 %all-to-all-start = ((bf16[8,144,256]{2,1,0:T(8,128)(2,1)}), bf16[8,144,256]{2,1,0:T(8,128)(2,1)S(1)}, u32[]{:S(2)}, u32[]{:S(2)}) async-start(bf16[8,144,256]{2,1,0:T(8,128)(2,1)} %get-tuple-element.23), calls=%async_computation | async-start | bytes 1179648 | tf_op jit(solution)/shard_map/all_to_all | solution.py:320
  13.5 4.2 %collective-permute-start.2 = (bf16[144,1024]{1,0:T(8,128)(2,1)}, bf16[144,1024]{1,0:T(8,128)(2,1)S(1)}, u32[]{:S(2)}, u32[]{:S(2)}) collective-permute-start(bf16[144,1024]{1,0:T(8,128)(2,1)} %get-tuple-element.24.refs_0_.refs_4_), channel_id=1, source_target_pairs={{0,32},{8,40},{16,48},{24,56},{32,0},{40,8},{48,16},{56,24},{64,96... | collective-permute-start | bytes 884744 | tf_op jit(solution)/shard_map/ppermute | solution.py:317
  17.7 3.2 %collective-permute-start.1 = (bf16[144,1024]{1,0:T(8,128)(2,1)}, bf16[144,1024]{1,0:T(8,128)(2,1)S(1)}, u32[]{:S(2)}, u32[]{:S(2)}) collective-permute-start(bf16[144,1024]{1,0:T(8,128)(2,1)} %get-tuple-element.24.refs_0_.refs_4_), channel_id=1, source_target_pairs={{0,16},{8,24},{16,0},{24,8},{32,48},{40,56},{48,32},{56,40},{64,80... | collective-permute-start | bytes 884744 | tf_op jit(solution)/shard_map/ppermute | solution.py:317
  20.9 11.9 %all-to-all-done.kv_ref = bf16[8,144,256]{2,1,0:T(8,128)(2,1)S(1)} async-done(((bf16[8,144,256]{2,1,0:T(8,128)(2,1)}), bf16[8,144,256]{2,1,0:T(8,128)(2,1)S(1)}, u32[]{:S(2)}, u32[]{:S(2)}) %all-to-all-start) | async-done | bytes 589856 | tf_op jit(solution)/shard_map/all_to_all | solution.py:320
  32.9 2.4 %collective-permute-start = (bf16[8,144,256]{2,1,0:T(8,128)(2,1)S(1)}, bf16[8,144,256]{2,1,0:T(8,128)(2,1)S(1)}, u32[]{:S(2)}, u32[]{:S(2)}) collective-permute-start(bf16[8,144,256]{2,1,0:T(8,128)(2,1)S(1)} %all-to-all-done.kv_ref), channel_id=1, source_target_pairs={{0,8},{8,0},{16,24},{24,16},{32,40},{40,32},{48,56},{56,48},{64,72... | collective-permute-start | bytes 1769480 | tf_op jit(solution)/shard_map/ppermute | solution.py:317
  35.3 0.0 collective-permute-done.2.refs_2_.refs_6_
  35.3 3.2 %collective-permute-start.3 = (bf16[144,1024]{1,0:T(8,128)(2,1)S(1)}, bf16[144,1024]{1,0:T(8,128)(2,1)S(1)}, u32[]{:S(2)}, u32[]{:S(2)}) collective-permute-start(bf16[144,1024]{1,0:T(8,128)(2,1)S(1)} %collective-permute-done.2.refs_2_.refs_6_), channel_id=1, source_target_pairs={{0,16},{8,24},{16,0},{24,8},{32,48},{40,56},{48,32},{56,40},{64,80... | collective-permute-start | bytes 884744 | tf_op jit(solution)/shard_map/ppermute | solution.py:317
  38.5 0.0 collective-permute-done.1.refs_1_.refs_5_
  38.5 0.0 copy-start
  38.5 1.0 %copy-done = bf16[144,1024]{1,0:T(8,128)(2,1)S(1)} copy-done((bf16[144,1024]{1,0:T(8,128)(2,1)S(1)}, bf16[144,1024]{1,0:T(8,128)(2,1)}, u32[]{:S(2)}) %copy-start) | copy-done | bytes 294936
  39.5 2.2 %scores_near.1 = (bf16[1024,1536]{1,0:T(8,128)(2,1)S(1)}, f32[4,8,384]{2,1,0:T(8,128)S(1)}) custom-call(bf16[8,144,256]{2,1,0:T(8,128)(2,1)S(1)} %all-to-all-done.kv_ref, bf16[144,1024]{1,0:T(8,128)(2,1)S(1)} %copy-done, bf16[144,1024]{1,0:T(8,128)(2,1)S(1)} %collective-permute-done.1.refs_1_.refs_5_, ...), custom_call_target="tpu_custom_call" | custom-call | flops 4600000000 | bytes 65536 | tf_op jit(solution)/shard_map/scores_near/pallas_call | solution.py:267
  41.7 0.0 copy-start.1
  41.7 0.0 collective-permute-done.kv_ref
  41.7 2.3 %scores_near_twin.1 = (bf16[1024,1536]{1,0:T(8,128)(2,1)S(1)}, f32[4,8,384]{2,1,0:T(8,128)S(1)}) custom-call(bf16[8,144,256]{2,1,0:T(8,128)(2,1)S(1)} %collective-permute-done.kv_ref, bf16[144,1024]{1,0:T(8,128)(2,1)S(1)} %copy-done, bf16[144,1024]{1,0:T(8,128)(2,1)S(1)} %collective-permute-done.1.refs_1_.refs_5_, ...), custom_call_target="tpu_custom_call" | custom-call | flops 100000000 | bytes 65536 | tf_op jit(solution)/shard_map/scores_near_twin/pallas_call | solution.py:267
  44.0 1.8 %collective-permute-done.3.refs_0_.refs_7_ = bf16[144,1024]{1,0:T(8,128)(2,1)S(1)} collective-permute-done((bf16[144,1024]{1,0:T(8,128)(2,1)S(1)}, bf16[144,1024]{1,0:T(8,128)(2,1)S(1)}, u32[]{:S(2)}, u32[]{:S(2)}) %collective-permute-start.3) | collective-permute-done | bytes 294944 | tf_op jit(solution)/shard_map/ppermute | solution.py:317
  45.8 0.9 scores_far.1
  46.7 0.9 scores_far_twin.1
  47.6 9.0 %all_to_all.15.all_ref = f32[4,8,512]{2,1,0:T(8,128)S(1)} all-to-all(f32[4,8,512]{2,1,0:T(8,128)S(1)} %get-tuple-element.30), channel_id=1, replica_groups={{0,16,32,48},{8,24,40,56},{64,80,96,112},{72,88,104,120},{128,144,160,1..., dimensions={0} | all-to-all | bytes 131072 | tf_op jit(solution)/shard_map/all_to_all | solution.py:320
  56.6 0.0 copy-done.1
  56.6 4.5 %grads.2 = (bf16[8,128,256]{2,1,0:T(8,128)(2,1)S(1)}, f32[4,128,512]{2,1,0:T(8,128)S(1)}) custom-call(bf16[8,144,256]{2,1,0:T(8,128)(2,1)S(1)} %collective-permute-done.kv_ref, f32[4,8,512]{2,1,0:T(8,128)S(1)} %all_to_all.15.all_ref, bf16[1024,1536]{1,0:T(8,128)(2,1)S(1)} %get-tuple-element.33.refs_0_, bf16[1024,512]{1,0:T(8,128)(2,1)S(1)} %get-tuple-element.34.refs_1_, ...), custom_call_target="tpu_custom_call" | custom-call | flops 6000000000 | bytes 65536 | tf_op jit(solution)/shard_map/grads/pallas_call | solution.py:299
  61.1 4.3 %collective-permute-start.7 = (bf16[8,128,256]{2,1,0:T(8,128)(2,1)S(1)}, bf16[8,128,256]{2,1,0:T(8,128)(2,1)S(1)}, u32[]{:S(2)}, u32[]{:S(2)}) collective-permute-start(bf16[8,128,256]{2,1,0:T(8,128)(2,1)S(1)} %get-tuple-element.42), channel_id=1, source_target_pairs={{0,8},{8,0},{16,24},{24,16},{32,40},{40,32},{48,56},{56,48},{64,72... | collective-permute-start | bytes 1572872 | tf_op jit(solution)/shard_map/ppermute | solution.py:317
  65.4 4.6 %grads.3 = (f32[8,128,256]{2,1,0:T(8,128)S(1)}, f32[128,512]{1,0:T(8,128)S(1)}, bf16[128,512]{1,0:T(8,128)(2,1)S(1)}, bf16[128,512]{1,0:T(8,128)(2,1)S(1)}, bf16[128,512]{1,0:T(8,128)(2,1)S(1)}) custom-call(bf16[8,144,256]{2,1,0:T(8,128)(2,1)S(1)} %all-to-all-done.kv_ref, f32[4,8,512]{2,1,0:T(8,128)S(1)} %all_to_all.15.all_ref, ...), custom_call_target="tpu_custom_call" | custom-call | flops 6000000000 | bytes 65536 | tf_op jit(solution)/shard_map/grads/pallas_call | solution.py:299
  70.1 0.0 collective-permute-done.7
  70.1 0.9 add_convert_fusion
  71.0 3.5 %all-to-all-start.2 = ((bf16[8,128,256]{2,1,0:T(8,128)(2,1)}), bf16[8,128,256]{2,1,0:T(8,128)(2,1)S(1)}, u32[]{:S(2)}, u32[]{:S(2)}) async-start(bf16[8,128,256]{2,1,0:T(8,128)(2,1)} %add_convert_fusion), calls=%async_computation.2 | async-start | bytes 1048576 | tf_op jit(solution)/shard_map/all_to_all | solution.py:320
  74.5 2.4 %collective-permute-start.4 = (bf16[128,512]{1,0:T(8,128)(2,1)S(1)}, bf16[128,512]{1,0:T(8,128)(2,1)S(1)}, u32[]{:S(2)}, u32[]{:S(2)}) collective-permute-start(bf16[128,512]{1,0:T(8,128)(2,1)S(1)} %get-tuple-element.38), channel_id=1, source_target_pairs={{0,48},{8,56},{16,32},{24,40},{32,16},{40,24},{48,0},{56,8},{64,11... | collective-permute-start | bytes 393224 | tf_op jit(solution)/shard_map/ppermute | solution.py:317
  76.9 3.3 %collective-permute-start.5 = (bf16[128,512]{1,0:T(8,128)(2,1)S(1)}, bf16[128,512]{1,0:T(8,128)(2,1)S(1)}, u32[]{:S(2)}, u32[]{:S(2)}) collective-permute-start(bf16[128,512]{1,0:T(8,128)(2,1)S(1)} %get-tuple-element.39), channel_id=1, source_target_pairs={{0,32},{8,40},{16,48},{24,56},{32,0},{40,8},{48,16},{56,24},{64,96... | collective-permute-start | bytes 393224 | tf_op jit(solution)/shard_map/ppermute | solution.py:317
  80.2 3.6 %collective-permute-start.6 = (bf16[128,512]{1,0:T(8,128)(2,1)S(1)}, bf16[128,512]{1,0:T(8,128)(2,1)S(1)}, u32[]{:S(2)}, u32[]{:S(2)}) collective-permute-start(bf16[128,512]{1,0:T(8,128)(2,1)S(1)} %get-tuple-element.40), channel_id=1, source_target_pairs={{0,16},{8,24},{16,0},{24,8},{32,48},{40,56},{48,32},{56,40},{64,80... | collective-permute-start | bytes 393224 | tf_op jit(solution)/shard_map/ppermute | solution.py:317
  83.8 0.0 collective-permute-done.4
  83.8 6.5 %collective-permute-done.5 = bf16[128,512]{1,0:T(8,128)(2,1)S(1)} collective-permute-done((bf16[128,512]{1,0:T(8,128)(2,1)S(1)}, bf16[128,512]{1,0:T(8,128)(2,1)S(1)}, u32[]{:S(2)}, u32[]{:S(2)}) %collective-permute-start.5) | collective-permute-done | bytes 131104 | tf_op jit(solution)/shard_map/ppermute | solution.py:317
  90.3 0.0 collective-permute-done.6
  90.3 0.7 add_convert_fusion.1
  91.0 1.5 %all-to-all-done.2 = bf16[8,128,256]{2,1,0:T(8,128)(2,1)S(1)} async-done(((bf16[8,128,256]{2,1,0:T(8,128)(2,1)}), bf16[8,128,256]{2,1,0:T(8,128)(2,1)S(1)}, u32[]{:S(2)}, u32[]{:S(2)}) %all-to-all-start.2) | async-done | bytes 524320 | tf_op jit(solution)/shard_map/all_to_all | solution.py:320
  92.5 0.1 reduce_sum.12
  92.6 0.6 fusion
Async XLA Ops:
  2.6 30.2 %all-to-all-start = ((bf16[8,144,256]{2,1,0:T(8,128)(2,1)}), bf16[8,144,256]{2,1,0:T(8,128)(2,1)S(1)}, u32[]{:S(2)}, u32[]{:S(2)}) async-start(bf16[8,144,256]{2,1,0:T(8,128)(2,1)} %get-tuple-element.23), calls=%async_computation | async-start | bytes 1179648 | tf_op jit(solution)/shard_map/all_to_all | solution.py:320
  13.5 21.8 %collective-permute-start.2 = (bf16[144,1024]{1,0:T(8,128)(2,1)}, bf16[144,1024]{1,0:T(8,128)(2,1)S(1)}, u32[]{:S(2)}, u32[]{:S(2)}) collective-permute-start(bf16[144,1024]{1,0:T(8,128)(2,1)} %get-tuple-element.24.refs_0_.refs_4_), channel_id=1, source_target_pairs={{0,32},{8,40},{16,48},{24,56},{32,0},{40,8},{48,16},{56,24},{64,96... | collective-permute-start | bytes 884744 | tf_op jit(solution)/shard_map/ppermute | solution.py:317
  17.7 20.8 %collective-permute-start.1 = (bf16[144,1024]{1,0:T(8,128)(2,1)}, bf16[144,1024]{1,0:T(8,128)(2,1)S(1)}, u32[]{:S(2)}, u32[]{:S(2)}) collective-permute-start(bf16[144,1024]{1,0:T(8,128)(2,1)} %get-tuple-element.24.refs_0_.refs_4_), channel_id=1, source_target_pairs={{0,16},{8,24},{16,0},{24,8},{32,48},{40,56},{48,32},{56,40},{64,80... | collective-permute-start | bytes 884744 | tf_op jit(solution)/shard_map/ppermute | solution.py:317
  32.9 8.9 %collective-permute-start = (bf16[8,144,256]{2,1,0:T(8,128)(2,1)S(1)}, bf16[8,144,256]{2,1,0:T(8,128)(2,1)S(1)}, u32[]{:S(2)}, u32[]{:S(2)}) collective-permute-start(bf16[8,144,256]{2,1,0:T(8,128)(2,1)S(1)} %all-to-all-done.kv_ref), channel_id=1, source_target_pairs={{0,8},{8,0},{16,24},{24,16},{32,40},{40,32},{48,56},{56,48},{64,72... | collective-permute-start | bytes 1769480 | tf_op jit(solution)/shard_map/ppermute | solution.py:317
  35.3 10.5 %collective-permute-start.3 = (bf16[144,1024]{1,0:T(8,128)(2,1)S(1)}, bf16[144,1024]{1,0:T(8,128)(2,1)S(1)}, u32[]{:S(2)}, u32[]{:S(2)}) collective-permute-start(bf16[144,1024]{1,0:T(8,128)(2,1)S(1)} %collective-permute-done.2.refs_2_.refs_6_), channel_id=1, source_target_pairs={{0,16},{8,24},{16,0},{24,8},{32,48},{40,56},{48,32},{56,40},{64,80... | collective-permute-start | bytes 884744 | tf_op jit(solution)/shard_map/ppermute | solution.py:317
  38.5 1.0 %copy-start = (bf16[144,1024]{1,0:T(8,128)(2,1)S(1)}, bf16[144,1024]{1,0:T(8,128)(2,1)}, u32[]{:S(2)}) copy-start(bf16[144,1024]{1,0:T(8,128)(2,1)} %get-tuple-element.24.refs_0_.refs_4_) | copy-start | bytes 884740
  41.7 14.9 %copy-start.1 = (bf16[144,1024]{1,0:T(8,128)(2,1)S(1)}, bf16[144,1024]{1,0:T(8,128)(2,1)}, u32[]{:S(2)}) copy-start(bf16[144,1024]{1,0:T(8,128)(2,1)} %get-tuple-element.24.refs_0_.refs_4_) | copy-start | bytes 884740
  61.1 9.0 %collective-permute-start.7 = (bf16[8,128,256]{2,1,0:T(8,128)(2,1)S(1)}, bf16[8,128,256]{2,1,0:T(8,128)(2,1)S(1)}, u32[]{:S(2)}, u32[]{:S(2)}) collective-permute-start(bf16[8,128,256]{2,1,0:T(8,128)(2,1)S(1)} %get-tuple-element.42), channel_id=1, source_target_pairs={{0,8},{8,0},{16,24},{24,16},{32,40},{40,32},{48,56},{56,48},{64,72... | collective-permute-start | bytes 1572872 | tf_op jit(solution)/shard_map/ppermute | solution.py:317
  71.0 21.5 %all-to-all-start.2 = ((bf16[8,128,256]{2,1,0:T(8,128)(2,1)}), bf16[8,128,256]{2,1,0:T(8,128)(2,1)S(1)}, u32[]{:S(2)}, u32[]{:S(2)}) async-start(bf16[8,128,256]{2,1,0:T(8,128)(2,1)} %add_convert_fusion), calls=%async_computation.2 | async-start | bytes 1048576 | tf_op jit(solution)/shard_map/all_to_all | solution.py:320
  74.5 9.3 %collective-permute-start.4 = (bf16[128,512]{1,0:T(8,128)(2,1)S(1)}, bf16[128,512]{1,0:T(8,128)(2,1)S(1)}, u32[]{:S(2)}, u32[]{:S(2)}) collective-permute-start(bf16[128,512]{1,0:T(8,128)(2,1)S(1)} %get-tuple-element.38), channel_id=1, source_target_pairs={{0,48},{8,56},{16,32},{24,40},{32,16},{40,24},{48,0},{56,8},{64,11... | collective-permute-start | bytes 393224 | tf_op jit(solution)/shard_map/ppermute | solution.py:317
  76.9 13.4 %collective-permute-start.5 = (bf16[128,512]{1,0:T(8,128)(2,1)S(1)}, bf16[128,512]{1,0:T(8,128)(2,1)S(1)}, u32[]{:S(2)}, u32[]{:S(2)}) collective-permute-start(bf16[128,512]{1,0:T(8,128)(2,1)S(1)} %get-tuple-element.39), channel_id=1, source_target_pairs={{0,32},{8,40},{16,48},{24,56},{32,0},{40,8},{48,16},{56,24},{64,96... | collective-permute-start | bytes 393224 | tf_op jit(solution)/shard_map/ppermute | solution.py:317
  80.2 10.1 %collective-permute-start.6 = (bf16[128,512]{1,0:T(8,128)(2,1)S(1)}, bf16[128,512]{1,0:T(8,128)(2,1)S(1)}, u32[]{:S(2)}, u32[]{:S(2)}) collective-permute-start(bf16[128,512]{1,0:T(8,128)(2,1)S(1)} %get-tuple-element.40), channel_id=1, source_target_pairs={{0,16},{8,24},{16,0},{24,8},{32,48},{40,56},{48,32},{56,40},{64,80... | collective-permute-start | bytes 393224 | tf_op jit(solution)/shard_map/ppermute | solution.py:317
